TPU v7x, 512 devices: a whole 4x4x16 slice. The times are simulated.
512 devices in a mesh: dp: 64 (over z, x), tensor: 8 (over y, core).
Axes of the slice: x: 4, y: 4, z: 16, core: 2. Of those that a mesh axis runs over, the one named last changes fastest.
Arguments:
- attn_out: bfloat16 [64, 384, 4096], P('dp', None, 'tensor'), may hold values from -6 to 6
- resid: bfloat16 [64, 384, 4096], P('dp', None, 'tensor'), may hold values from -17 to 17
- cotangent: bfloat16 [64, 384, 4096], P('dp', None, 'tensor'), may hold values from -6 to 6
- o_weight: bfloat16 [4096, 4096], P('tensor', 'dp'), may hold values from -0.09375 to 0.09375
- norm_gain: float32 [4096], P('tensor'), may hold values from 0.1 to 1.9
- proj_in: bfloat16 [4096, 64], P('tensor'), may hold values from -0.09375 to 0.09375
- proj_out: bfloat16 [4096, 64], P('tensor'), may hold values from -0.09375 to 0.09375
- queries: float32 [64, 4096], P('dp'), may hold values from -6 to 6
Outputs:
- train_grads: float32 [64, 64, 64], P('dp')
- scores: float32 [64, 64], P('dp')
All inputs are finite; a program needn't handle non-finite values.
Results may differ from a plain program's by a relative error of at most 0.0035.
Values may be sent and summed in bfloat16 or wider, within the bound.
No kernel may reach another device: no remote copies, remote signals or barrier semaphores. Data moves between devices by JAX's collectives and lax.ppermute only.
A program may use at most 64 MiB of HBM per device.

v0:
```python
import math

import jax
import jax.numpy as jnp
from jax import lax
from jax.sharding import PartitionSpec as P


def norm_backward(stream, weighted, sum_squares, dot_term, width):
    inv_rms = lax.rsqrt(sum_squares / width + 1e-05)[:, None]
    return (inv_rms * weighted - stream * (inv_rms**3 / width) * dot_term[:, None]).astype(
        jnp.bfloat16
    )


def weight_gather(o_weight, column_fn):
    return column_fn(lax.all_gather(o_weight, "dp", axis=1, tiled=True), jnp.int32(0))


def shards(attn_out, resid, cotangent, o_weight, norm_gain, proj_in, proj_out, queries):
    inputs = attn_out[0]
    resid_part = resid[0]
    cot_part = cotangent[0]
    length = inputs.shape[0]
    blocks = lax.axis_size("tensor")
    width = o_weight.shape[0] * blocks
    rank = proj_in.shape[1]

    def forward(piece, start):
        return jnp.dot(inputs, piece, preferred_element_type=jnp.float32)

    partial_out = weight_gather(o_weight, forward)
    in_part = jnp.dot(inputs, proj_in, preferred_element_type=jnp.float32)
    layer_out = lax.psum_scatter(
        partial_out.astype(jnp.bfloat16), "tensor", scatter_dimension=1, tiled=True
    ).astype(jnp.float32)
    stream = resid_part.astype(jnp.float32) + layer_out
    weighted = norm_gain * cot_part.astype(jnp.float32)
    sum_squares, dot_term = lax.psum(
        (jnp.sum(stream * stream, axis=1), jnp.sum(weighted * stream, axis=1)), "tensor"
    )
    out_grad = norm_backward(stream, weighted, sum_squares, dot_term, width)
    out_part = jnp.dot(out_grad, proj_out, preferred_element_type=jnp.float32)
    in_full, out_full = lax.psum((in_part, out_part), "tensor")
    gram = jnp.einsum("lr,ls->rs", in_full, out_full, precision=lax.Precision.HIGHEST)
    train_grads = gram / math.sqrt(length)
    flat = train_grads.reshape(rank * rank)
    scores = (
        jnp.dot(
            lax.all_gather(queries, "dp", axis=0, tiled=True), flat, precision=lax.Precision.HIGHEST
        )
        / rank
    )[None]
    return (train_grads[None], scores)


def solution(mesh):
    in_specs = (
        P("dp", None, "tensor"),
        P("dp", None, "tensor"),
        P("dp", None, "tensor"),
        P("tensor", "dp"),
        P("tensor"),
        P("tensor", None),
        P("tensor", None),
        P("dp", None),
    )
    out_specs = (P("dp", None, None), P("dp", None))
    return jax.shard_map(shards, mesh=mesh, in_specs=in_specs, out_specs=out_specs, check_vma=False)
```

profile of v0, /device:TPU:1, one launch (start us, length us, event | category | flops | bytes accessed | tf_op | source)
XLA Modules:
  0.0 439.6 jit_solution(10964580078585106171)
XLA Ops:
  7.2 0.0 copy-start
  7.2 0.0 all-gather.4.cloned.1.call-start
  7.2 0.7 all-gather.4.cloned.1.call-update
  7.9 0.0 copy-start.4
  7.9 0.0 copy-start.1
  7.9 0.0 copy-start.2
  7.9 0.0 copy-start.5
  8.0 0.0 reduce-scatter.2.cloned.1.call-start
  8.0 146.7 %all-gather.4.cloned.1.call-done = bf16[512,4096]{0,1:T(8,128)(2,1)} async-done(((bf16[512,64]{0,1:T(8,128)(2,1)}), bf16[512,4096]{0,1:T(8,128)(2,1)}) %all-gather.4.cloned.1.call-update) | async-done | bytes 4194320 | tf_op jit(solution)/shard_map/all_gather | solution.py:17
  154.7 0.0 copy-done
  154.7 5.7 %convolution_convert_fusion = bf16[384,4096]{1,0:T(8,128)(2,1)} fusion(bf16[512,4096]{0,1:T(8,128)(2,1)} %all-gather.4.cloned.1.call-done, bf16[1,384,512]{2,1,0:T(8,128)(2,1)S(1)} %copy-done), kind=kOutput, calls=%fused_computation | convolution fusion | flops 1612185600 | bytes 7733248 | tf_op jit(solution)/shard_map/dot_general | solution.py:30
  160.4 0.0 copy-start.6
  160.4 0.0 reduce-scatter.2.cloned.1.call-update
  160.4 0.0 all-reduce.4.cloned.1.call-start
  160.5 0.0 copy-done.4
  160.5 0.9 fusion.10
  161.4 43.4 %reduce-scatter.2.cloned.1.call-done = bf16[384,512]{1,0:T(8,128)(2,1)} async-done(((bf16[384,4096]{1,0:T(8,128)(2,1)}), bf16[384,512]{1,0:T(8,128)(2,1)}) %reduce-scatter.2.cloned.1.call-update) | async-done | bytes 393232 | tf_op jit(solution)/shard_map/reduce_scatter | solution.py:34
  204.8 0.0 copy-done.1
  204.8 0.0 copy-done.2
  204.8 0.0 copy-done.5
  204.9 1.3 multiply_reduce_fusion
  206.2 14.4 %all-reduce = (f32[384]{0:T(512)S(1)}, f32[384]{0:T(512)S(1)}) all-reduce(f32[384]{0:T(512)S(1)} %get-tuple-element.3, f32[384]{0:T(512)S(1)} %get-tuple-element.2), channel_id=1, replica_groups=mesh['dp'=64,'tensor'=8] {'tensor'}, use_global_device_ids=true, to_apply=%region_5.0 | all-reduce | flops 768 | bytes 6144 | tf_op jit(solution)/shard_map/psum | solution.py:39
  220.5 0.0 copy-done.6
  220.5 2.1 fusion.12
  222.6 0.0 all-reduce.4.cloned.1.call-update
  222.6 0.0 all-gather.6.cloned.1.call-start
  222.7 0.5 all-gather.6.cloned.1.call-update
  223.2 73.4 %all-reduce.4.cloned.1.call-done = (f32[384,64]{1,0:T(8,128)}, f32[384,64]{1,0:T(8,128)}) async-done(((f32[384,64]{1,0:T(8,128)}, f32[384,64]{1,0:T(8,128)}), (f32[384,64]{1,0:T(8,128)}, f32[384,64]{1,0:T(8,128)})) %all-reduce.4.cloned.1.call-update) | async-done | bytes 196624 | tf_op jit(solution)/shard_map/psum | solution.py:44
  296.6 1.5 convolution_multiply_fusion
  298.1 0.0 copy-start.3
  298.1 0.1 reshape.23
  298.2 131.8 %all-gather.6.cloned.1.call-done = f32[64,1,4096]{2,1,0:T(1,128)} async-done(((f32[1,1,4096]{2,1,0:T(1,128)}), f32[64,1,4096]{2,1,0:T(1,128)}) %all-gather.6.cloned.1.call-update) | async-done | bytes 1048592 | tf_op jit(solution)/shard_map/all_gather | solution.py:50
  430.0 3.1 fusion.1
  433.1 0.0 copy-done.3
  (1 shorter events, 0.0 us)
Async XLA Ops:
  7.2 147.6 %copy-start = (bf16[1,384,512]{2,1,0:T(8,128)(2,1)S(1)}, bf16[1,384,512]{2,1,0:T(8,128)(2,1)}, u32[]{:S(2)}) copy-start(bf16[1,384,512]{2,1,0:T(8,128)(2,1)} %param.8) | copy-start | bytes 1179652
  7.2 147.5 %all-gather.4.cloned.1.call-start = ((), (), s32[]{:S(2)}) async-start(), calls=%async_computation.1 | async-start | bytes 4259840 | tf_op jit(solution)/shard_map/all_gather | solution.py:17
  7.9 152.6 %copy-start.4 = (bf16[512,64]{0,1:T(8,128)(2,1)S(1)}, bf16[512,64]{0,1:T(8,128)(2,1)}, u32[]{:S(2)}) copy-start(bf16[512,64]{0,1:T(8,128)(2,1)} %param.13) | copy-start | bytes 196612
  7.9 196.9 %copy-start.1 = (bf16[1,384,512]{2,1,0:T(8,128)(2,1)S(1)}, bf16[1,384,512]{2,1,0:T(8,128)(2,1)}, u32[]{:S(2)}) copy-start(bf16[1,384,512]{2,1,0:T(8,128)(2,1)} %param.10) | copy-start | bytes 1179652
  7.9 196.9 %copy-start.2 = (bf16[1,384,512]{2,1,0:T(8,128)(2,1)S(1)}, bf16[1,384,512]{2,1,0:T(8,128)(2,1)}, u32[]{:S(2)}) copy-start(bf16[1,384,512]{2,1,0:T(8,128)(2,1)} %param.9) | copy-start | bytes 1179652
  7.9 196.9 %copy-start.5 = (f32[512]{0:T(512)S(1)}, f32[512]{0:T(512)}, u32[]{:S(2)}) copy-start(f32[512]{0:T(512)} %param.12) | copy-start | bytes 6148
  8.0 196.9 %reduce-scatter.2.cloned.1.call-start = ((), (), s32[]{:S(2)}) async-start(), calls=%async_computation.2 | async-start | bytes 3538944 | tf_op jit(solution)/shard_map/reduce_scatter | solution.py:34
  160.4 60.1 %copy-start.6 = (bf16[512,64]{0,1:T(8,128)(2,1)S(1)}, bf16[512,64]{0,1:T(8,128)(2,1)}, u32[]{:S(2)}) copy-start(bf16[512,64]{0,1:T(8,128)(2,1)} %param.14) | copy-start | bytes 196612
  160.4 136.1 %all-reduce.4.cloned.1.call-start = ((), (), s32[]{:S(2)}) async-start(), calls=%async_computation.4 | async-start | bytes 786432 | tf_op jit(solution)/shard_map/psum | solution.py:44
  222.6 207.4 %all-gather.6.cloned.1.call-start = ((), (), s32[]{:S(2)}) async-start(), calls=%async_computation.3 | async-start | bytes 1064960 | tf_op jit(solution)/shard_map/all_gather | solution.py:50
  298.1 135.0 %copy-start.3 = (f32[64,64]{1,0:T(8,128)}, f32[64,64]{1,0:T(8,128)S(1)}, u32[]{:S(2)}) copy-start(f32[64,64]{1,0:T(8,128)S(1)} %convolution_multiply_fusion) | copy-start | bytes 49156
Sparse Core Ops, SparseCore 0:
  11.0 143.7 all-gather.3
  160.6 44.2 reduce-scatter.1
  222.7 73.7 all-reduce.3
  299.8 130.1 all-gather.5
where the time goes:
time: 448 us; the launch traced here: 440 us
  waiting for transfers between devices  397 us (89%)
  blocking collectives  14.4 us (3%)
  between operations  13.8 us (3%)
  matrix products  13.2 us (3%)
    all_gather x1, waiting for transfers between devices, weight_gather(): lax.all_gather(o_weight, 'dp', axis=1, tiled=True)  147 us
    all_gather x1, waiting for transfers between devices, shards(): lax.all_gather(queries, 'dp', axis=0, tiled=True)  132 us
    psum x1, waiting for transfers between devices, shards(): in_full, out_full = lax.psum((in_part, out_part), 'tensor')  73.4 us
    reduce_scatter x1, waiting for transfers between devices, shards(): lax.psum_scatter(partial_out.astype(jnp.bfloat16), 'tensor', scatter_dime...  43.4 us
    psum x1, blocking collectives, shards(): lax.psum((jnp.sum(stream * stream, axis=1), jnp.sum(weighted * stream, ax...  14.4 us
  transfers between devices with their start and end apart: 4, of which 4 were waited for; matrix products, arithmetic and copies ran while one was open for 1% of the time, Pallas kernels for 0%

commit v1 on v0

v1 whole, which is shorter than its diff:
```python
import functools
import math

import jax
import jax.numpy as jnp
import numpy as np
from jax import lax
from jax.experimental import pallas as pl
from jax.experimental.pallas import tpu as pltpu
from jax.sharding import Mesh, PartitionSpec as P

Z = ("zh", "zl")
PLANE = ("x", "y")
TENSOR = ("y", "core")
EPS = 1e-05
NT = (((1,), (1,)), ((), ()))
TN = (((0,), (0,)), ((), ()))
HIGHEST = lax.Precision.HIGHEST
PARAMS = pltpu.CompilerParams(vmem_limit_bytes=48 * 1024 * 1024)
VMEM = pl.BlockSpec(memory_space=pltpu.VMEM)
SMEM = pl.BlockSpec(memory_space=pltpu.SMEM)
ANY = pl.BlockSpec(memory_space=pl.ANY)


def cost(flops, moved):
    return pl.CostEstimate(flops=flops, bytes_accessed=moved, transcendentals=0)


def split3(value):
    high = value.astype(jnp.bfloat16)
    rest = value - high.astype(jnp.float32)
    mid = rest.astype(jnp.bfloat16)
    low = (rest - mid.astype(jnp.float32)).astype(jnp.bfloat16)
    return high, mid, low


def pack_kernel(place, weight, query, out):
    core = place[3]
    tile = weight[...].astype(jnp.float32).T
    out[0:64, :] = tile.astype(jnp.bfloat16)
    rows = [query[:, pl.ds(pl.multiple_of(core * 2048 + j * 512, 512), 512)] for j in range(4)]
    half = jnp.concatenate(rows, axis=0)
    high, low, _ = split3(half)
    out[64:72, :] = jnp.concatenate([high, low], axis=0)


def load(place, tokens, weights, all_tokens, all_weights, sems):
    zl = place[1]
    copies = []
    for at, ref in enumerate(tokens):
        copies.append(pltpu.make_async_copy(ref, all_tokens.at[pl.ds(at * 384, 384)], sems.at[at]))
    for at, ref in enumerate(weights):
        copies.append(pltpu.make_async_copy(ref, all_weights.at[lax.rem(zl + at, 4)], sems.at[4 + at]))
    for copy in copies:
        copy.start()
    for copy in copies:
        copy.wait()


def product(all_tokens, all_weights, half, pair):
    parts = []
    for zh in (2 * pair, 2 * pair + 1):
        for k in range(2):
            parts.append(all_weights[2 * half + k, zh, 0:64, :])
    rows = jnp.concatenate(parts, axis=0)
    return lax.dot_general(all_tokens[...], rows, NT, preferred_element_type=jnp.float32)


def other_kernel(place, t0, t1, t2, t3, w0, w1, w2, w3, out, query, all_tokens, all_weights, sems):
    load(place, (t0, t1, t2, t3), (w0, w1, w2, w3), all_tokens, all_weights, sems)
    x, half = place[0], 1 - place[3]
    for pair in range(2):
        total = product(all_tokens, all_weights, half, pair).astype(jnp.bfloat16)
        for at in range(4):
            for k in range(2):
                out[at, 2 * pair + k] = total[at * 384 : (at + 1) * 384, k * 128 : (k + 1) * 128]
    for zh in range(4):
        for zl in range(4):
            terms = all_weights[zl, zh, 64:72, :].astype(jnp.float32)
            query[pl.ds((zh * 4 + zl) * 4, 4), :] = terms[0:4] + terms[4:8]


def own_kernel(place, t0, t1, t2, t3, w0, w1, w2, w3, other, out, all_tokens, all_weights, sems):
    load(place, (t0, t1, t2, t3), (w0, w1, w2, w3), all_tokens, all_weights, sems)
    x, half = place[0], place[3]
    for pair in range(2):
        total = product(all_tokens, all_weights, half, pair)
        for at in range(4):
            to = lax.rem(x + at, 4)
            for k in range(2):
                y = 2 * pair + k
                block = total[at * 384 : (at + 1) * 384, k * 128 : (k + 1) * 128]
                out[to * 4 + y] = (block + other[at, y].astype(jnp.float32)).astype(jnp.bfloat16)


def sums_kernel(parts, tokens, resid, cot, gain, proj_in, proj_out, out):
    blocks = []
    for x in range(4):
        total = parts[4 * x].astype(jnp.float32)
        for y in range(1, 4):
            total = total + parts[4 * x + y].astype(jnp.float32)
        blocks.append(total)
    layer_out = jnp.concatenate(
        [block[:, 0:64] for block in blocks] + [block[:, 64:128] for block in blocks], axis=1
    )
    stream = resid[...].astype(jnp.float32) + layer_out
    weighted = gain[...] * cot[...].astype(jnp.float32)
    squares = jnp.sum(stream * stream, axis=1, keepdims=True)
    dots = jnp.sum(weighted * stream, axis=1, keepdims=True)
    rows = jnp.concatenate(split3(weighted) + split3(stream), axis=0)
    terms = jnp.dot(rows, proj_out[...], preferred_element_type=jnp.float32)
    n = resid.shape[0]
    weighted_out = terms[0:n] + terms[n : 2 * n] + terms[2 * n : 3 * n]
    stream_out = terms[3 * n : 4 * n] + terms[4 * n : 5 * n] + terms[5 * n : 6 * n]
    in_part = jnp.dot(tokens[...], proj_in[...], preferred_element_type=jnp.float32)
    out[:, 0:128] = jnp.concatenate([weighted_out, stream_out], axis=1)
    lane = lax.broadcasted_iota(jnp.int32, (n, 64), 1)
    stats = jnp.where(lane == 0, squares, jnp.where(lane == 1, dots, 0.0))
    out[:, 128:256] = jnp.concatenate([in_part, stats], axis=1)


def gram_kernel(width, parts, out):
    total = parts[0]
    for at in range(1, 8):
        total = total + parts[at]
    squares, dots = total[:, 192:193], total[:, 193:194]
    inv_rms = lax.rsqrt(squares / width + EPS)
    out_proj = inv_rms * total[:, 0:64] - total[:, 64:128] * (inv_rms**3 / width * dots)
    row = lax.broadcasted_iota(jnp.int32, (64, 64), 0)
    column = lax.broadcasted_iota(jnp.int32, (64, 64), 1)
    source = jnp.where(column < 32, 2 * column, 2 * column - 63)
    order = (row == source).astype(jnp.float32)
    in_proj = jnp.dot(total[:, 128:192], order, precision=HIGHEST)
    gram = lax.dot_general(in_proj, out_proj, TN, precision=HIGHEST, preferred_element_type=jnp.float32)
    packed = jnp.concatenate([gram[0:32], gram[32:64]], axis=1)
    for at in range(8):
        out[at] = packed


def score_kernel(length, parts, queries, grads, scores, packed):
    total = parts[0]
    for at in range(1, 8):
        total = total + parts[at]
    total = total / math.sqrt(length)
    packed[...] = total
    grads[pl.ds(0, 32, stride=2), :] = total[:, 0:64]
    grads[pl.ds(1, 32, stride=2), :] = total[:, 64:128]
    sums = [None] * 4
    for core in range(2):
        for m in range(4):
            four = packed[pl.ds(core * 16 + m, 4, stride=4), :]
            factor = jnp.concatenate([four] * 16, axis=0)
            for x in range(4):
                term = queries[2 * x + core, :, m * 128 : (m + 1) * 128] * factor
                sums[x] = term if sums[x] is None else sums[x] + term
    every = jnp.concatenate(sums, axis=0)
    ones = jnp.ones((8, 128), jnp.float32)
    flat = lax.dot_general(ones, every, NT, precision=HIGHEST, preferred_element_type=jnp.float32)
    row = lax.broadcasted_iota(jnp.int32, (256, 64), 0)
    column = lax.broadcasted_iota(jnp.int32, (256, 64), 1)
    chosen = ((row % 64) // 4 * 4 + row // 64 == column).astype(jnp.float32)
    result = jnp.dot(flat, chosen, precision=HIGHEST, preferred_element_type=jnp.float32)
    scores[...] = result[0:1] / 64.0


def shift(size, by):
    return [((at + by) % size, at) for at in range(size)]


def shards(attn_out, resid, cotangent, o_weight, norm_gain, proj_in, proj_out, queries):
    tokens = attn_out[0]
    length, features = tokens.shape
    width = features * 8
    bf16, f32 = jnp.bfloat16, jnp.float32
    place = jnp.stack([lax.axis_index(name) for name in ("x", "zl", "y", "core")]).astype(jnp.int32)

    with jax.named_scope("pack"):
        piece = pl.pallas_call(
            pack_kernel,
            out_shape=jax.ShapeDtypeStruct((72, 512), bf16),
            in_specs=[SMEM, VMEM, VMEM],
            out_specs=VMEM,
            compiler_params=PARAMS,
            cost_estimate=cost(0, 1 << 18),
        )(place, o_weight, queries)
    with jax.named_scope("gather_tokens"):
        all_tokens = [tokens] + [lax.ppermute(tokens, "x", shift(4, by)) for by in (1, 2, 3)]
    with jax.named_scope("gather_weight"):
        mine = lax.all_gather(piece, "zh", axis=0)
        all_weights = [mine] + [lax.ppermute(mine, Z, shift(16, by)) for by in (1, 2, -1)]

    scratch = [
        pltpu.VMEM((4 * length, 512), bf16),
        pltpu.VMEM((4, 4, 72, 512), bf16),
        pltpu.SemaphoreType.DMA((8,)),
    ]
    flops = 2 * 4 * length * 512 * 512
    with jax.named_scope("other_half"):
        other, query = pl.pallas_call(
            other_kernel,
            out_shape=(
                jax.ShapeDtypeStruct((4, 4, length, 128), bf16),
                jax.ShapeDtypeStruct((64, 512), f32),
            ),
            in_specs=[SMEM] + [ANY] * 8,
            out_specs=(VMEM, VMEM),
            scratch_shapes=scratch,
            compiler_params=PARAMS,
            cost_estimate=cost(flops, 4 << 20),
        )(place, *all_tokens, *all_weights)
        other = lax.ppermute(other, "core", shift(2, 1))
    with jax.named_scope("gather_queries"):
        all_queries = lax.all_gather(query, ("x", "core"), axis=0)
    with jax.named_scope("own_half"):
        partial = pl.pallas_call(
            own_kernel,
            out_shape=jax.ShapeDtypeStruct((16, length, 128), bf16),
            in_specs=[SMEM] + [ANY] * 8 + [VMEM],
            out_specs=VMEM,
            scratch_shapes=scratch,
            compiler_params=PARAMS,
            cost_estimate=cost(flops, 5 << 20),
        )(place, *all_tokens, *all_weights, other)
    with jax.named_scope("exchange_parts"):
        parts = lax.all_to_all(partial, PLANE, 0, 0, tiled=True)
    with jax.named_scope("token_sums"):
        sums = pl.pallas_call(
            sums_kernel,
            out_shape=jax.ShapeDtypeStruct((length, 256), f32),
            in_specs=[VMEM] * 7,
            out_specs=VMEM,
            compiler_params=PARAMS,
            cost_estimate=cost(14 * length * 512 * 64, 4 << 20),
        )(parts, tokens, resid[0], cotangent[0], norm_gain[None], proj_in, proj_out)
        sums = lax.all_to_all(sums.reshape(8, length // 8, 256), TENSOR, 0, 0, tiled=True)
    with jax.named_scope("gram"):
        gram = pl.pallas_call(
            functools.partial(gram_kernel, width),
            out_shape=jax.ShapeDtypeStruct((8, 32, 128), f32),
            in_specs=[VMEM],
            out_specs=VMEM,
            compiler_params=PARAMS,
            cost_estimate=cost(1 << 22, 1 << 19),
        )(sums)
        gram = lax.all_to_all(gram, TENSOR, 0, 0, tiled=True)
    with jax.named_scope("scores"):
        grads, scores = pl.pallas_call(
            functools.partial(score_kernel, length),
            out_shape=(jax.ShapeDtypeStruct((64, 64), f32), jax.ShapeDtypeStruct((1, 64), f32)),
            in_specs=[VMEM, VMEM],
            out_specs=(VMEM, VMEM),
            scratch_shapes=[pltpu.VMEM((32, 128), f32)],
            compiler_params=PARAMS,
            cost_estimate=cost(1 << 20, 1 << 20),
        )(gram, all_queries)
    return grads[None], scores


def solution(mesh):
    devices = np.asarray(mesh.devices).reshape(4, 4, 4, 4, 2)
    fine = Mesh(devices, ("zh", "zl", "x", "y", "core"))
    dp = ("zh", "zl", "x")
    in_specs = (
        P(dp, None, TENSOR),
        P(dp, None, TENSOR),
        P(dp, None, TENSOR),
        P(TENSOR, dp),
        P(TENSOR),
        P(TENSOR, None),
        P(TENSOR, None),
        P(dp, None),
    )
    out_specs = (P(dp, None, None), P(dp, None))
    return jax.shard_map(shards, mesh=fine, in_specs=in_specs, out_specs=out_specs, check_vma=False)
```

time: 448 us -> 142 us (0.32); the launches traced: 440 us -> 142 us
  waiting for transfers between devices: 397 us -> 41.9 us
  starting transfers between devices: 0.16 us -> 31.6 us
  blocking collectives: 14.4 us -> 38.6 us
  matrix products: 13.2 us -> 0 us
  Pallas kernels: 0 us -> 11.1 us
    all_gather x2 -> x1, waiting for transfers between devices: 279 us -> 0.01 us  [shards(): all_queries = lax.all_gather(query, ('x', 'core'), axis=0)]
    psum x1 -> x0, waiting for transfers between devices: 73.4 us -> none  [shards(): in_full, out_full = lax.psum((in_part, out_part), 'tensor')]
    reduce_scatter x1 -> x0, waiting for transfers between devices: 43.4 us -> none  [shards(): lax.psum_scatter(partial_out.astype(jnp.bfloat16), 'tensor', scatter_dime...]
    all_to_all x0 -> x2, waiting for transfers between devices: none -> 26.5 us  [the longest x1 21.2 us: shards(): parts = lax.all_to_all(partial, PLANE, 0, 0, tiled=True)]
    all_gather x0 -> x1, blocking collectives: none -> 25.3 us  [shards(): mine = lax.all_gather(piece, 'zh', axis=0)]
    ppermute x0 -> x7, starting transfers between devices: none -> 22 us  [the longest x3 9.34 us: shards(): lax.ppermute(tokens, 'x', shift(4, by))]
    ppermute x0 -> x7, waiting for transfers between devices: none -> 14.7 us  [the longest x3 9.45 us: shards(): lax.ppermute(mine, Z, shift(16, by))]
    psum x1 -> x0, blocking collectives: 14.4 us -> none  [shards(): lax.psum((jnp.sum(stream * stream, axis=1), jnp.sum(weighted * stream, ax...]
  transfers between devices with their start and end apart: 4 -> 10, of which waited for: 4 -> 5; matrix products, arithmetic and copies ran while one was open for 1% -> 0% of each run, Pallas kernels for 0% -> 2%
where the time goes in v1:
time: 142 us
  waiting for transfers between devices  41.9 us (30%)
  blocking collectives  38.6 us (27%)
  starting transfers between devices  31.6 us (22%)
  between operations  14.2 us (10%)
  Pallas kernels  11.1 us (8%)
  local copies, waits for them, and re-layouts  4.17 us (3%)
    all_gather x1, blocking collectives, shards(): mine = lax.all_gather(piece, 'zh', axis=0)  25.3 us
    all_to_all x1, waiting for transfers between devices, shards(): parts = lax.all_to_all(partial, PLANE, 0, 0, tiled=True)  21.2 us
    all_to_all x1, blocking collectives, shards(): lax.all_to_all(sums.reshape(8, length // 8, 256), TENSOR, 0, 0, tiled=True)  13.2 us
    ppermute x3, waiting for transfers between devices, shards(): lax.ppermute(mine, Z, shift(16, by))  9.45 us
    ppermute x3, starting transfers between devices, shards(): lax.ppermute(tokens, 'x', shift(4, by))  9.34 us
    ppermute x3, starting transfers between devices, shards(): lax.ppermute(mine, Z, shift(16, by))  8.87 us
    all_to_all x1, starting transfers between devices, shards(): parts = lax.all_to_all(partial, PLANE, 0, 0, tiled=True)  5.49 us
    all_to_all x1, waiting for transfers between devices, shards(): gram = lax.all_to_all(gram, TENSOR, 0, 0, tiled=True)  5.29 us
  transfers between devices with their start and end apart: 10, of which 5 were waited for; matrix products, arithmetic and copies ran while one was open for 0% of the time, Pallas kernels for 2%

profile of v1, /device:TPU:1, one launch (start us, length us, event | category | flops | bytes accessed | tf_op | source)
XLA Modules:
  0.0 141.7 jit_solution(7665940529861751592)
XLA Ops:
  7.2 1.0 copy.10.weight
  8.1 0.1 pad_add_fusion.place
  8.2 0.0 copy-start.5
  8.2 0.7 copy-done.5
  8.9 0.6 pack.1
  9.6 25.3 %all-gather = bf16[288,512]{1,0:T(8,128)(2,1)S(1)} all-gather(bf16[72,512]{1,0:T(8,128)(2,1)S(1)} %pack.1), channel_id=2, replica_groups=mesh['zh'=4,'zl'=4,'x'=4,'y'=4,'core'=2] {'zh'}, dimensions={0}, use_global_device_ids=true | all-gather | bytes 368640 | tf_op jit(solution)/shard_map/gather_weight/all_gather | solution.py:189
  34.9 3.9 %collective-permute-start.3 = (bf16[4,72,512]{2,1,0:T(8,128)(2,1)S(1)}, bf16[4,72,512]{2,1,0:T(8,128)(2,1)S(1)}, u32[]{:S(2)}, u32[]{:S(2)}) collective-permute-start(bf16[4,72,512]{2,1,0:T(8,128)(2,1)S(1)} %bitcast.19), channel_id=1, source_target_pairs={{32,0},{64,32},{96,64},{128,96},{160,128},{192,160},{224,192},{256... | collective-permute-start | bytes 884744 | tf_op jit(solution)/shard_map/gather_weight/ppermute | solution.py:190
  38.8 4.4 %collective-permute-start = (bf16[384,512]{1,0:T(8,128)(2,1)}, bf16[384,512]{1,0:T(8,128)(2,1)S(1)}, u32[]{:S(2)}, u32[]{:S(2)}) collective-permute-start(bf16[384,512]{1,0:T(8,128)(2,1)} %bitcast.12), channel_id=1, source_target_pairs={{8,0},{16,8},{24,16},{0,24},{9,1},{17,9},{25,17},{1,25},{10,2},{18... | collective-permute-start | bytes 1179656 | tf_op jit(solution)/shard_map/gather_tokens/ppermute | solution.py:187
  43.2 2.4 %collective-permute-start.1 = (bf16[384,512]{1,0:T(8,128)(2,1)}, bf16[384,512]{1,0:T(8,128)(2,1)S(1)}, u32[]{:S(2)}, u32[]{:S(2)}) collective-permute-start(bf16[384,512]{1,0:T(8,128)(2,1)} %bitcast.13), channel_id=1, source_target_pairs={{16,0},{24,8},{0,16},{8,24},{17,1},{25,9},{1,17},{9,25},{18,2},{26... | collective-permute-start | bytes 1179656 | tf_op jit(solution)/shard_map/gather_tokens/ppermute | solution.py:187
  45.6 2.5 %collective-permute-start.2 = (bf16[384,512]{1,0:T(8,128)(2,1)}, bf16[384,512]{1,0:T(8,128)(2,1)S(1)}, u32[]{:S(2)}, u32[]{:S(2)}) collective-permute-start(bf16[384,512]{1,0:T(8,128)(2,1)} %bitcast.14), channel_id=1, source_target_pairs={{24,0},{0,8},{8,16},{16,24},{25,1},{1,9},{9,17},{17,25},{26,2},{2,... | collective-permute-start | bytes 1179656 | tf_op jit(solution)/shard_map/gather_tokens/ppermute | solution.py:187
  48.1 2.2 %collective-permute-start.4 = (bf16[4,72,512]{2,1,0:T(8,128)(2,1)S(1)}, bf16[4,72,512]{2,1,0:T(8,128)(2,1)S(1)}, u32[]{:S(2)}, u32[]{:S(2)}) collective-permute-start(bf16[4,72,512]{2,1,0:T(8,128)(2,1)S(1)} %bitcast.20), channel_id=1, source_target_pairs={{64,0},{96,32},{128,64},{160,96},{192,128},{224,160},{256,192},{28... | collective-permute-start | bytes 884744 | tf_op jit(solution)/shard_map/gather_weight/ppermute | solution.py:190
  50.4 0.0 collective-permute-done.3.w1
  50.4 2.8 %collective-permute-start.5 = (bf16[4,72,512]{2,1,0:T(8,128)(2,1)S(1)}, bf16[4,72,512]{2,1,0:T(8,128)(2,1)S(1)}, u32[]{:S(2)}, u32[]{:S(2)}) collective-permute-start(bf16[4,72,512]{2,1,0:T(8,128)(2,1)S(1)} %bitcast.21), channel_id=1, source_target_pairs={{480,0},{0,32},{32,64},{64,96},{96,128},{128,160},{160,192},{192,2... | collective-permute-start | bytes 884744 | tf_op jit(solution)/shard_map/gather_weight/ppermute | solution.py:190
  53.2 9.4 %collective-permute-done.4.w2 = bf16[4,72,512]{2,1,0:T(8,128)(2,1)S(1)} collective-permute-done((bf16[4,72,512]{2,1,0:T(8,128)(2,1)S(1)}, bf16[4,72,512]{2,1,0:T(8,128)(2,1)S(1)}, u32[]{:S(2)}, u32[]{:S(2)}) %collective-permute-start.4) | collective-permute-done | bytes 294944 | tf_op jit(solution)/shard_map/gather_weight/ppermute | solution.py:190
  62.6 0.0 collective-permute-done.5.w3
  62.6 0.0 collective-permute-done.t1
  62.6 0.0 collective-permute-done.1.t2
  62.6 2.3 %collective-permute-done.2.t3 = bf16[384,512]{1,0:T(8,128)(2,1)S(1)} collective-permute-done((bf16[384,512]{1,0:T(8,128)(2,1)}, bf16[384,512]{1,0:T(8,128)(2,1)S(1)}, u32[]{:S(2)}, u32[]{:S(2)}) %collective-permute-start.2) | collective-permute-done | bytes 393248 | tf_op jit(solution)/shard_map/gather_tokens/ppermute | solution.py:187
  64.9 1.0 copy-done
  65.9 3.3 %other_half.1 = (bf16[4,4,384,128]{3,2,1,0:T(8,128)(2,1)S(1)}, f32[64,512]{1,0:T(8,128)}) custom-call(s32[4]{0:T(128)S(1)} %pad_add_fusion.place, bf16[384,512]{1,0:T(8,128)(2,1)S(1)} %bitcast.15, bf16[384,512]{1,0:T(8,128)(2,1)S(1)} %collective-permute-done.t1, bf16[384,512]{1,0:T(8,128)(2,1)S(1)} %collective-permute-done.1.t2, ...), custom_call_target="tpu_custom_call" | custom-call | flops 805306368 | bytes 4194304 | tf_op jit(solution)/shard_map/other_half/pallas_call | solution.py:199
  69.2 3.8 %collective-permute-start.6 = (bf16[4,4,384,128]{3,2,1,0:T(8,128)(2,1)S(1)}, bf16[4,4,384,128]{3,2,1,0:T(8,128)(2,1)S(1)}, u32[]{:S(2)}, u32[]{:S(2)}) collective-permute-start(bf16[4,4,384,128]{3,2,1,0:T(8,128)(2,1)S(1)} %get-tuple-element.6), channel_id=1, source_target_pairs={{1,0},{0,1},{3,2},{2,3},{5,4},{4,5},{7,6},{6,7},{9,8},{8,9},{11,10... | collective-permute-start | bytes 4718600 | tf_op jit(solution)/shard_map/other_half/ppermute | solution.py:211
  72.9 3.0 %collective-permute-done.6.other = bf16[4,4,384,128]{3,2,1,0:T(8,128)(2,1)S(1)} collective-permute-done((bf16[4,4,384,128]{3,2,1,0:T(8,128)(2,1)S(1)}, bf16[4,4,384,128]{3,2,1,0:T(8,128)(2,1)S(1)}, u32[]{:S(2)}, u32[]{:S(2)}) %collective-permute-start.6) | collective-permute-done | bytes 1572896 | tf_op jit(solution)/shard_map/other_half/ppermute | solution.py:211
  75.9 3.8 %own_half.1 = bf16[16,384,128]{2,1,0:T(8,128)(2,1)} custom-call(s32[4]{0:T(128)S(1)} %pad_add_fusion.place, bf16[384,512]{1,0:T(8,128)(2,1)S(1)} %bitcast.16, bf16[384,512]{1,0:T(8,128)(2,1)S(1)} %collective-permute-done.t1, bf16[384,512]{1,0:T(8,128)(2,1)S(1)} %collective-permute-done.1.t2, bf16[384,512]{1,0:T(8,128)(2,1)S(1)} %collective-permute-done.2.t3, ...), custom_call_target="tpu_custom_call" | custom-call | flops 805306368 | bytes 5242880 | tf_op jit(solution)/shard_map/own_half/pallas_call | solution.py:215
  79.8 0.0 copy-start.7
  79.8 0.0 copy-start.8
  79.8 0.0 copy-start.1
  79.8 0.0 copy-start.3
  79.8 0.0 copy-start.4
  79.8 0.0 copy-start.6
  79.8 5.5 %all-to-all-start = ((bf16[16,384,128]{2,1,0:T(8,128)(2,1)}), bf16[16,384,128]{2,1,0:T(8,128)(2,1)S(1)}, u32[]{:S(2)}, u32[]{:S(2)}) async-start(bf16[16,384,128]{2,1,0:T(8,128)(2,1)} %own_half.1), calls=%async_computation | async-start | bytes 3145728 | tf_op jit(solution)/shard_map/exchange_parts/all_to_all | solution.py:225
  85.3 0.0 all-gather.4.cloned.1.call-start
  85.4 0.7 all-gather.4.cloned.1.call-update
  86.1 0.0 copy-done.7
  86.1 0.1 copy.11.proj_in
  86.2 0.0 copy-done.8
  86.2 0.1 copy.12.proj_out
  86.3 21.2 %all-to-all-done.parts = bf16[16,384,128]{2,1,0:T(8,128)(2,1)S(1)} async-done(((bf16[16,384,128]{2,1,0:T(8,128)(2,1)}), bf16[16,384,128]{2,1,0:T(8,128)(2,1)S(1)}, u32[]{:S(2)}, u32[]{:S(2)}) %all-to-all-start) | async-done | bytes 1572896 | tf_op jit(solution)/shard_map/exchange_parts/all_to_all | solution.py:225
  107.6 0.0 copy-done.1
  107.6 0.0 copy-done.3
  107.6 0.0 copy-done.4
  107.6 0.0 copy-done.6
  107.6 1.2 token_sums.1
  108.8 13.2 %all_to_all.15.parts = f32[8,48,256]{2,1,0:T(8,128)S(1)} all-to-all(f32[8,48,256]{2,1,0:T(8,128)S(1)} %bitcast.18), channel_id=1, replica_groups=mesh['zh'=4,'zl'=4,'x'=4,'y'=4,'core'=2] {'y','core'}, dimensions={0} | all-to-all | bytes 786432 | tf_op jit(solution)/shard_map/token_sums/all_to_all | solution.py:235
  122.0 1.1 gram.1
  123.1 4.1 %all-to-all-start.2 = ((f32[8,32,128]{2,1,0:T(8,128)}), f32[8,32,128]{2,1,0:T(8,128)S(1)}, u32[]{:S(2)}, u32[]{:S(2)}) async-start(f32[8,32,128]{2,1,0:T(8,128)} %gram.1), calls=%async_computation.2 | async-start | bytes 262144 | tf_op jit(solution)/shard_map/gram/all_to_all | solution.py:245
  127.3 5.3 %all-to-all-done.2.parts = f32[8,32,128]{2,1,0:T(8,128)S(1)} async-done(((f32[8,32,128]{2,1,0:T(8,128)}), f32[8,32,128]{2,1,0:T(8,128)S(1)}, u32[]{:S(2)}, u32[]{:S(2)}) %all-to-all-start.2) | async-done | bytes 131104 | tf_op jit(solution)/shard_map/gram/all_to_all | solution.py:245
  132.6 1.2 copy-done.2
  133.8 1.1 scores.1
  (3 shorter events, 0.0 us)
Async XLA Ops:
  8.2 0.7 copy-start.5
  34.9 15.5 %collective-permute-start.3 = (bf16[4,72,512]{2,1,0:T(8,128)(2,1)S(1)}, bf16[4,72,512]{2,1,0:T(8,128)(2,1)S(1)}, u32[]{:S(2)}, u32[]{:S(2)}) collective-permute-start(bf16[4,72,512]{2,1,0:T(8,128)(2,1)S(1)} %bitcast.19), channel_id=1, source_target_pairs={{32,0},{64,32},{96,64},{128,96},{160,128},{192,160},{224,192},{256... | collective-permute-start | bytes 884744 | tf_op jit(solution)/shard_map/gather_weight/ppermute | solution.py:190
  38.8 23.8 %collective-permute-start = (bf16[384,512]{1,0:T(8,128)(2,1)}, bf16[384,512]{1,0:T(8,128)(2,1)S(1)}, u32[]{:S(2)}, u32[]{:S(2)}) collective-permute-start(bf16[384,512]{1,0:T(8,128)(2,1)} %bitcast.12), channel_id=1, source_target_pairs={{8,0},{16,8},{24,16},{0,24},{9,1},{17,9},{25,17},{1,25},{10,2},{18... | collective-permute-start | bytes 1179656 | tf_op jit(solution)/shard_map/gather_tokens/ppermute | solution.py:187
  43.2 19.5 %collective-permute-start.1 = (bf16[384,512]{1,0:T(8,128)(2,1)}, bf16[384,512]{1,0:T(8,128)(2,1)S(1)}, u32[]{:S(2)}, u32[]{:S(2)}) collective-permute-start(bf16[384,512]{1,0:T(8,128)(2,1)} %bitcast.13), channel_id=1, source_target_pairs={{16,0},{24,8},{0,16},{8,24},{17,1},{25,9},{1,17},{9,25},{18,2},{26... | collective-permute-start | bytes 1179656 | tf_op jit(solution)/shard_map/gather_tokens/ppermute | solution.py:187
  45.6 19.3 %collective-permute-start.2 = (bf16[384,512]{1,0:T(8,128)(2,1)}, bf16[384,512]{1,0:T(8,128)(2,1)S(1)}, u32[]{:S(2)}, u32[]{:S(2)}) collective-permute-start(bf16[384,512]{1,0:T(8,128)(2,1)} %bitcast.14), channel_id=1, source_target_pairs={{24,0},{0,8},{8,16},{16,24},{25,1},{1,9},{9,17},{17,25},{26,2},{2,... | collective-permute-start | bytes 1179656 | tf_op jit(solution)/shard_map/gather_tokens/ppermute | solution.py:187
  48.1 14.5 %collective-permute-start.4 = (bf16[4,72,512]{2,1,0:T(8,128)(2,1)S(1)}, bf16[4,72,512]{2,1,0:T(8,128)(2,1)S(1)}, u32[]{:S(2)}, u32[]{:S(2)}) collective-permute-start(bf16[4,72,512]{2,1,0:T(8,128)(2,1)S(1)} %bitcast.20), channel_id=1, source_target_pairs={{64,0},{96,32},{128,64},{160,96},{192,128},{224,160},{256,192},{28... | collective-permute-start | bytes 884744 | tf_op jit(solution)/shard_map/gather_weight/ppermute | solution.py:190
  50.4 12.2 %collective-permute-start.5 = (bf16[4,72,512]{2,1,0:T(8,128)(2,1)S(1)}, bf16[4,72,512]{2,1,0:T(8,128)(2,1)S(1)}, u32[]{:S(2)}, u32[]{:S(2)}) collective-permute-start(bf16[4,72,512]{2,1,0:T(8,128)(2,1)S(1)} %bitcast.21), channel_id=1, source_target_pairs={{480,0},{0,32},{32,64},{64,96},{96,128},{128,160},{160,192},{192,2... | collective-permute-start | bytes 884744 | tf_op jit(solution)/shard_map/gather_weight/ppermute | solution.py:190
  64.9 1.0 copy-start
  69.2 6.8 %collective-permute-start.6 = (bf16[4,4,384,128]{3,2,1,0:T(8,128)(2,1)S(1)}, bf16[4,4,384,128]{3,2,1,0:T(8,128)(2,1)S(1)}, u32[]{:S(2)}, u32[]{:S(2)}) collective-permute-start(bf16[4,4,384,128]{3,2,1,0:T(8,128)(2,1)S(1)} %get-tuple-element.6), channel_id=1, source_target_pairs={{1,0},{0,1},{3,2},{2,3},{5,4},{4,5},{7,6},{6,7},{9,8},{8,9},{11,10... | collective-permute-start | bytes 4718600 | tf_op jit(solution)/shard_map/other_half/ppermute | solution.py:211
  79.8 6.3 %copy-start.7 = (bf16[512,64]{0,1:T(8,128)(2,1)S(1)}, bf16[512,64]{0,1:T(8,128)(2,1)}, u32[]{:S(2)}) copy-start(bf16[512,64]{0,1:T(8,128)(2,1)} %param.13) | copy-start | bytes 196612
  79.8 6.4 %copy-start.8 = (bf16[512,64]{0,1:T(8,128)(2,1)S(1)}, bf16[512,64]{0,1:T(8,128)(2,1)}, u32[]{:S(2)}) copy-start(bf16[512,64]{0,1:T(8,128)(2,1)} %param.14) | copy-start | bytes 196612
  79.8 27.8 %copy-start.1 = (bf16[1,384,512]{2,1,0:T(8,128)(2,1)S(1)}, bf16[1,384,512]{2,1,0:T(8,128)(2,1)}, u32[]{:S(2)}) copy-start(bf16[1,384,512]{2,1,0:T(8,128)(2,1)} %param.8) | copy-start | bytes 1179652
  79.8 27.8 %copy-start.3 = (bf16[1,384,512]{2,1,0:T(8,128)(2,1)S(1)}, bf16[1,384,512]{2,1,0:T(8,128)(2,1)}, u32[]{:S(2)}) copy-start(bf16[1,384,512]{2,1,0:T(8,128)(2,1)} %param.9) | copy-start | bytes 1179652
  79.8 27.8 %copy-start.4 = (bf16[1,384,512]{2,1,0:T(8,128)(2,1)S(1)}, bf16[1,384,512]{2,1,0:T(8,128)(2,1)}, u32[]{:S(2)}) copy-start(bf16[1,384,512]{2,1,0:T(8,128)(2,1)} %param.10) | copy-start | bytes 1179652
  79.8 27.8 %copy-start.6 = (f32[512]{0:T(512)S(1)}, f32[512]{0:T(512)}, u32[]{:S(2)}) copy-start(f32[512]{0:T(512)} %param.12) | copy-start | bytes 6148
  79.8 27.7 %all-to-all-start = ((bf16[16,384,128]{2,1,0:T(8,128)(2,1)}), bf16[16,384,128]{2,1,0:T(8,128)(2,1)S(1)}, u32[]{:S(2)}, u32[]{:S(2)}) async-start(bf16[16,384,128]{2,1,0:T(8,128)(2,1)} %own_half.1), calls=%async_computation | async-start | bytes 3145728 | tf_op jit(solution)/shard_map/exchange_parts/all_to_all | solution.py:225
  85.3 41.9 %all-gather.4.cloned.1.call-start = ((), (), s32[]{:S(2)}) async-start(), calls=%async_computation.3 | async-start | bytes 1179648 | tf_op jit(solution)/shard_map/gather_queries/all_gather | solution.py:213
  123.1 9.4 %all-to-all-start.2 = ((f32[8,32,128]{2,1,0:T(8,128)}), f32[8,32,128]{2,1,0:T(8,128)S(1)}, u32[]{:S(2)}, u32[]{:S(2)}) async-start(f32[8,32,128]{2,1,0:T(8,128)} %gram.1), calls=%async_computation.2 | async-start | bytes 262144 | tf_op jit(solution)/shard_map/gram/all_to_all | solution.py:245
  132.6 1.2 copy-start.2
Sparse Core Ops, SparseCore 0:
  88.3 28.3 all-gather.3

commit v2 on v1

v2 whole, which is shorter than its diff:
```python
import functools
import math

import jax
import jax.numpy as jnp
import numpy as np
from jax import lax
from jax.experimental import pallas as pl
from jax.experimental.pallas import tpu as pltpu
from jax.sharding import Mesh, PartitionSpec as P

Z = ("zh", "zl")
PLANE = ("x", "y")
TENSOR = ("y", "core")
EPS = 1e-05
NT = (((1,), (1,)), ((), ()))
TN = (((0,), (0,)), ((), ()))
HIGHEST = lax.Precision.HIGHEST
PARAMS = pltpu.CompilerParams(vmem_limit_bytes=24 * 1024 * 1024)
VMEM = pl.BlockSpec(memory_space=pltpu.VMEM)
SMEM = pl.BlockSpec(memory_space=pltpu.SMEM)
ANY = pl.BlockSpec(memory_space=pl.ANY)


def cost(flops, moved):
    return pl.CostEstimate(flops=flops, bytes_accessed=moved, transcendentals=0)


def split3(value):
    high = value.astype(jnp.bfloat16)
    rest = value - high.astype(jnp.float32)
    mid = rest.astype(jnp.bfloat16)
    low = (rest - mid.astype(jnp.float32)).astype(jnp.bfloat16)
    return high, mid, low


def pack_kernel(place, weight, query, out):
    for at in range(4):
        out[64 * at : 64 * at + 64, :] = weight[:, 128 * at : 128 * at + 128]
    first = place[2] * 1024
    rows = [query[:, pl.ds(pl.multiple_of(first + j * 128, 128), 128)] for j in range(8)]
    rows.append(jnp.zeros((8, 128), jnp.float32))
    out[256:272, :] = jnp.concatenate(rows, axis=0).astype(jnp.bfloat16)


def repeat_kernel(tokens, out, sems):
    copies = [pltpu.make_async_copy(tokens, out.at[at], sems.at[at]) for at in range(4)]
    for copy in copies:
        copy.start()
    for copy in copies:
        copy.wait()


def product(tokens, first, second, pair):
    strips = []
    for zh in (2 * pair, 2 * pair + 1):
        for ref in (first, second):
            blocks = [ref[zh, 64 * at : 64 * at + 64, :] for at in range(4)]
            strips.append(jnp.concatenate(blocks, axis=1))
    rows = jnp.concatenate(strips, axis=0)
    return lax.dot_general(tokens[...], rows, NT, preferred_element_type=jnp.float32)


def half_kernel(mine, place, tokens, w0, w1, w2, w3, out):
    weights = (w0, w1, w2, w3)
    half = place[3] if mine else 1 - place[3]
    slot = lax.rem(2 * half - place[1] + 4, 4)
    for at in range(4):

        @pl.when(slot == at)
        def _():
            for pair in range(2):
                total = product(tokens, weights[at], weights[(at + 1) % 4], pair)
                out[:, 256 * pair : 256 * pair + 256] = total.astype(jnp.bfloat16)


def add_kernel(first, second, w0, w1, w2, w3, out):
    slots = []
    for ref in (w0, w1, w2, w3):
        rows = [ref[zh, 256:272, :].astype(jnp.float32)[0:8] for zh in range(4)]
        slots.append(jnp.concatenate(rows, axis=0))
    queries = jnp.concatenate(slots, axis=1).astype(jnp.bfloat16)
    for at in range(16):
        rows = slice(96 * at, 96 * at + 96)
        total = first[rows, :].astype(jnp.float32) + second[rows, :].astype(jnp.float32)
        out[at, 0:96, :] = total.astype(jnp.bfloat16)
        out[at, 96:128, :] = queries


def share_kernel(tokens, resid, cot, gain, proj_in, proj_out, out):
    in_part = lax.dot_general(tokens[...], proj_in[...], NT, preferred_element_type=jnp.float32)
    high, low, _ = split3(in_part)
    terms = jnp.concatenate([high.astype(jnp.float32), low.astype(jnp.float32)], axis=1)
    gains = [term.astype(jnp.float32) for term in split3(gain[...])]
    gains = jnp.concatenate(gains + [jnp.zeros((5, 512), jnp.float32)], axis=0)
    for at in range(4):
        rows = slice(96 * at, 96 * at + 96)
        out[at, 0:96, :] = resid[rows, :]
        out[at, 96:192, :] = cot[rows, :]
        out[at, 192:256, :] = proj_out[...]
        first = 96 * at
        four = [terms[first + 24 * k : first + 24 * k + 24] for k in range(4)]
        tail = jnp.concatenate([jnp.concatenate(four, axis=1), gains], axis=0)
        out[at, 256:288, :] = tail.astype(jnp.bfloat16)


def sums_kernel(parts, shared, out):
    blocks = []
    for x in range(4):
        total = parts[4 * x, 0:96, :].astype(jnp.float32)
        for y in range(1, 4):
            total = total + parts[4 * x + y, 0:96, :].astype(jnp.float32)
        blocks.append(total)
    weighted_out = stream_out = in_proj = jnp.zeros((96, 64), jnp.float32)
    squares = dots = jnp.zeros((96, 1), jnp.float32)
    for y in range(4):
        strips = [block[:, 128 * y + 64 * k : 128 * y + 64 * k + 64] for k in range(2) for block in blocks]
        stream = shared[y, 0:96, :].astype(jnp.float32) + jnp.concatenate(strips, axis=1)
        tail = shared[y, 256:288, :].astype(jnp.float32)
        gain = tail[24:25] + tail[25:26] + tail[26:27]
        weighted = gain * shared[y, 96:192, :].astype(jnp.float32)
        squares = squares + jnp.sum(stream * stream, axis=1, keepdims=True)
        dots = dots + jnp.sum(weighted * stream, axis=1, keepdims=True)
        rows = jnp.concatenate(split3(weighted) + split3(stream), axis=0)
        terms = lax.dot_general(rows, shared[y, 192:256, :], NT, preferred_element_type=jnp.float32)
        weighted_out = weighted_out + (terms[0:96] + terms[96:192] + terms[192:288])
        stream_out = stream_out + (terms[288:384] + terms[384:480] + terms[480:576])
        four = [tail[0:24, 128 * k : 128 * k + 128] for k in range(4)]
        four = jnp.concatenate(four, axis=0)
        in_proj = in_proj + (four[:, 0:64] + four[:, 64:128])
    lane = lax.broadcasted_iota(jnp.int32, (96, 64), 1)
    stats = jnp.where(lane == 0, squares, jnp.where(lane == 1, dots, 0.0))
    out[:, 0:128] = jnp.concatenate([weighted_out, stream_out], axis=1)
    out[:, 128:256] = jnp.concatenate([in_proj, stats], axis=1)


def gram_kernel(width, mine, theirs, out):
    total = mine[...] + theirs[...]
    squares, dots = total[:, 192:193], total[:, 193:194]
    inv_rms = lax.rsqrt(squares / width + EPS)
    out_proj = inv_rms * total[:, 0:64] - total[:, 64:128] * (inv_rms**3 / width * dots)
    row = lax.broadcasted_iota(jnp.int32, (64, 64), 0)
    column = lax.broadcasted_iota(jnp.int32, (64, 64), 1)
    source = jnp.where(column < 32, 2 * column, 2 * column - 63)
    order = (row == source).astype(jnp.float32)
    in_proj = jnp.dot(total[:, 128:192], order, precision=HIGHEST)
    gram = lax.dot_general(in_proj, out_proj, TN, precision=HIGHEST, preferred_element_type=jnp.float32)
    packed = jnp.concatenate([gram[0:32], gram[32:64]], axis=1)
    for at in range(4):
        out[at] = packed


def score_kernel(length, place, grams, parts, grads, scores, packed):
    total = grams[0] + grams[1] + grams[2] + grams[3]
    total = total / math.sqrt(length)
    packed[...] = total
    grads[pl.ds(0, 32, stride=2), :] = total[:, 0:64]
    grads[pl.ds(1, 32, stride=2), :] = total[:, 64:128]
    zl = place[1]
    sources = []
    for x in range(4):
        every = None
        for y in range(4):
            eight = jnp.concatenate([packed[8 * y : 8 * y + 8, :]] * 4, axis=0)
            eight = jnp.concatenate([eight] * 4, axis=1)
            term = parts[4 * x + y, 96:128, :].astype(jnp.float32) * eight
            every = term if every is None else every + term
        sources = sources + [every[:, 128 * at : 128 * at + 128] for at in range(4)]
    every = jnp.concatenate(sources, axis=0)
    ones = jnp.ones((8, 128), jnp.float32)
    flat = lax.dot_general(ones, every, NT, precision=HIGHEST, preferred_element_type=jnp.float32)
    row = lax.broadcasted_iota(jnp.int32, (512, 64), 0) // 8
    column = lax.broadcasted_iota(jnp.int32, (512, 64), 1)
    chosen = ((row % 4) * 16 + (row // 4 + zl) % 4 * 4 + row // 16 == column).astype(jnp.float32)
    result = jnp.dot(flat, chosen, precision=HIGHEST, preferred_element_type=jnp.float32)
    scores[...] = result[0:1] / 64.0


def swing(size):
    return [((at + (2 if at % 2 == 0 else -2)) % size, at) for at in range(size)]


def shift(size, by):
    return [((at + by) % size, at) for at in range(size)]


def shards(attn_out, resid, cotangent, o_weight, norm_gain, proj_in, proj_out, queries):
    tokens = attn_out[0]
    length, features = tokens.shape
    width = features * 8
    bf16, f32 = jnp.bfloat16, jnp.float32
    place = jnp.stack([lax.axis_index(name) for name in ("x", "zl", "y", "core")]).astype(jnp.int32)

    with jax.named_scope("pack"):
        piece = pl.pallas_call(
            pack_kernel,
            out_shape=jax.ShapeDtypeStruct((272, 128), bf16),
            in_specs=[SMEM, VMEM, VMEM],
            out_specs=VMEM,
            compiler_params=PARAMS,
            cost_estimate=cost(0, 1 << 18),
        )(place, o_weight.T, queries)
    with jax.named_scope("gather_tokens"):
        copies = pl.pallas_call(
            repeat_kernel,
            out_shape=jax.ShapeDtypeStruct((4,) + tokens.shape, bf16),
            in_specs=[ANY],
            out_specs=ANY,
            scratch_shapes=[pltpu.SemaphoreType.DMA((4,))],
            compiler_params=PARAMS,
            cost_estimate=cost(0, 2 << 20),
        )(tokens)
        every = lax.all_to_all(copies, "x", 0, 0, tiled=True).reshape(4 * length, features)
    with jax.named_scope("gather_weight"):
        mine = lax.all_gather(piece, "zh", axis=0)
        mine, every = lax.optimization_barrier((mine, every))
        ways = (shift(16, 1), swing(16), shift(16, -1))
        all_weights = [mine] + [lax.ppermute(mine, Z, way) for way in ways]
    with jax.named_scope("share_tokens"):
        shared = pl.pallas_call(
            share_kernel,
            out_shape=jax.ShapeDtypeStruct((4, 288, 512), bf16),
            in_specs=[VMEM] * 6,
            out_specs=VMEM,
            compiler_params=PARAMS,
            cost_estimate=cost(2 * length * 512 * 64, 3 << 20),
        )(tokens, resid[0], cotangent[0], norm_gain[None], proj_in.T, proj_out.T)
        shared, every = lax.optimization_barrier((shared, every))
        shared = lax.all_to_all(shared, "y", 0, 0, tiled=True)
        shared, every = lax.optimization_barrier((shared, every))


    def partial_sums(own):
        return pl.pallas_call(
            functools.partial(half_kernel, own),
            out_shape=jax.ShapeDtypeStruct((4 * length, 512), bf16),
            in_specs=[SMEM] + [VMEM] * 5,
            out_specs=VMEM,
            compiler_params=PARAMS,
            cost_estimate=cost(0, 1 << 10),
        )(place, every, *all_weights)

    with jax.named_scope("other_half"):
        other = lax.ppermute(partial_sums(False), "core", shift(2, 1))
    with jax.named_scope("own_half"):
        partial = pl.pallas_call(
            add_kernel,
            out_shape=jax.ShapeDtypeStruct((16, length // 4 + 32, 512), bf16),
            in_specs=[VMEM] * 6,
            out_specs=VMEM,
            compiler_params=PARAMS,
            cost_estimate=cost(0, 1 << 10),
        )(partial_sums(True), other, *all_weights)
    with jax.named_scope("exchange_parts"):
        parts = lax.all_to_all(partial, PLANE, 0, 0, tiled=True)
    with jax.named_scope("token_sums"):
        sums = pl.pallas_call(
            sums_kernel,
            out_shape=jax.ShapeDtypeStruct((length // 4, 256), f32),
            in_specs=[VMEM, VMEM],
            out_specs=VMEM,
            compiler_params=PARAMS,
            cost_estimate=cost(14 * length * 512 * 64, 4 << 20),
        )(parts, shared)
        theirs = lax.ppermute(sums, "core", shift(2, 1))
    with jax.named_scope("gram"):
        gram = pl.pallas_call(
            functools.partial(gram_kernel, width),
            out_shape=jax.ShapeDtypeStruct((4, 32, 128), f32),
            in_specs=[VMEM, VMEM],
            out_specs=VMEM,
            compiler_params=PARAMS,
            cost_estimate=cost(1 << 22, 1 << 19),
        )(sums, theirs)
        gram = lax.all_to_all(gram, "y", 0, 0, tiled=True)
    with jax.named_scope("scores"):
        grads, scores = pl.pallas_call(
            functools.partial(score_kernel, length),
            out_shape=(jax.ShapeDtypeStruct((64, 64), f32), jax.ShapeDtypeStruct((1, 64), f32)),
            in_specs=[SMEM, VMEM, VMEM],
            out_specs=(VMEM, VMEM),
            scratch_shapes=[pltpu.VMEM((32, 128), f32)],
            compiler_params=PARAMS,
            cost_estimate=cost(1 << 22, 3 << 20),
        )(place, gram, parts)
    return grads[None], scores


def solution(mesh):
    devices = np.asarray(mesh.devices).reshape(4, 4, 4, 4, 2)
    fine = Mesh(devices, ("zh", "zl", "x", "y", "core"))
    dp = ("zh", "zl", "x")
    in_specs = (
        P(dp, None, TENSOR),
        P(dp, None, TENSOR),
        P(dp, None, TENSOR),
        P(TENSOR, dp),
        P(TENSOR),
        P(TENSOR, None),
        P(TENSOR, None),
        P(dp, None),
    )
    out_specs = (P(dp, None, None), P(dp, None))
    return jax.shard_map(shards, mesh=fine, in_specs=in_specs, out_specs=out_specs, check_vma=False)
```

time: 142 us -> 118 us (0.83)
  waiting for transfers between devices: 41.9 us -> 11 us
  blocking collectives: 38.6 us -> 65.2 us
  between operations: 14.2 us -> 0.86 us
  starting transfers between devices: 31.6 us -> 27.4 us
  local copies, waits for them, and re-layouts: 4.17 us -> 2.06 us
    all_to_all x1 -> x2, blocking collectives: 13.2 us -> 40.7 us  [the longest x1 33.8 us: shards(): parts = lax.all_to_all(partial, PLANE, 0, 0, tiled=True)]
    all_to_all x2, waiting for transfers between devices: 26.5 us -> 3.27 us  [the longest x1 3.26 us: shards(): shared = lax.all_to_all(shared, 'y', 0, 0, tiled=True)]
    ppermute x7 -> x5, waiting for transfers between devices: 14.7 us -> 7.71 us  [the longest x3 5.87 us: shards(): all_weights = [mine] + [lax.ppermute(mine, Z, way) for way in ways]]
    ppermute x7 -> x5, starting transfers between devices: 22 us -> 18.3 us  [the longest x3 9.65 us: shards(): all_weights = [mine] + [lax.ppermute(mine, Z, way) for way in ways]]
    unnamed x21 -> x20, local copies, waits for them, and re-layouts: 4.17 us -> 2.06 us
    pallas_call x4 -> x7, Pallas kernels: 8.87 us -> 8.76 us  [the longest x2 4.17 us: partial_sums(): pl.pallas_call(functools.partial(half_kernel, own), out_shape=jax.ShapeDt...]
  transfers between devices with their start and end apart: 10 -> 7, of which waited for: 5 -> 4; matrix products, arithmetic and copies ran while one was open for 0% -> 0% of each run, Pallas kernels for 2% -> 3%
where the time goes in v2:
time: 118 us
  blocking collectives  65.2 us (55%)
  starting transfers between devices  27.4 us (23%)
  Pallas kernels  11 us (9%)
  waiting for transfers between devices  11 us (9%)
  local copies, waits for them, and re-layouts  2.06 us (2%)
    all_to_all x1, blocking collectives, shards(): parts = lax.all_to_all(partial, PLANE, 0, 0, tiled=True)  33.8 us
    all_gather x1, blocking collectives, shards(): mine = lax.all_gather(piece, 'zh', axis=0)  24.5 us
    ppermute x3, starting transfers between devices, shards(): all_weights = [mine] + [lax.ppermute(mine, Z, way) for way in ways]  9.65 us
    all_to_all x1, blocking collectives, shards(): gram = lax.all_to_all(gram, 'y', 0, 0, tiled=True)  6.89 us
    ppermute x3, waiting for transfers between devices, shards(): all_weights = [mine] + [lax.ppermute(mine, Z, way) for way in ways]  5.87 us
    all_to_all x1, starting transfers between devices, shards(): lax.all_to_all(copies, 'x', 0, 0, tiled=True).reshape(4 * length, features)  4.99 us
    ppermute x1, starting transfers between devices, shards(): other = lax.ppermute(partial_sums(False), 'core', shift(2, 1))  4.68 us
    pallas_call x2, Pallas kernels, partial_sums(): pl.pallas_call(functools.partial(half_kernel, own), out_shape=jax.ShapeDt...  4.17 us
  transfers between devices with their start and end apart: 7, of which 4 were waited for; matrix products, arithmetic and copies ran while one was open for 0% of the time, Pallas kernels for 3%

profile of v2, /device:TPU:1, one launch (start us, length us, event | category | flops | bytes accessed | tf_op | source)
XLA Modules:
  0.0 117.5 jit_solution(15196271424848559291)
XLA Ops:
  0.6 0.0 copy-start.1
  0.6 1.0 copy-done.1
  1.6 1.2 %gather_tokens.1 = bf16[4,384,512]{2,1,0:T(8,128)(2,1)} custom-call(bf16[384,512]{1,0:T(8,128)(2,1)S(1)} %bitcast.22), custom_call_target="tpu_custom_call" | custom-call | bytes 2097152 | tf_op jit(solution)/shard_map/gather_tokens/pallas_call | solution.py:204
  2.8 0.0 copy-start.7
  2.9 0.0 copy-start.8
  2.9 0.0 copy-start.2
  2.9 0.0 copy-start.3
  2.9 0.0 copy-start.4
  2.9 0.0 copy-start.5
  2.9 0.0 copy-start.6
  2.9 0.0 copy-start.9
  2.9 5.0 %all-to-all-start = ((bf16[4,384,512]{2,1,0:T(8,128)(2,1)}), bf16[4,384,512]{2,1,0:T(8,128)(2,1)S(1)}, u32[]{:S(2)}, u32[]{:S(2)}) async-start(bf16[4,384,512]{2,1,0:T(8,128)(2,1)} %gather_tokens.1), calls=%async_computation | async-start | bytes 3145728 | tf_op jit(solution)/shard_map/gather_tokens/all_to_all | solution.py:213
  7.9 0.1 pad_add_fusion.place
  8.0 0.0 copy-done.7
  8.0 0.0 copy-done.8
  8.0 0.6 pack.1
  8.6 0.0 copy-done.2
  8.6 0.0 copy-done.3
  8.6 0.0 copy-done.4
  8.6 0.0 copy-done.5
  8.6 0.0 copy-done.6
  8.6 0.0 copy-done.9
  8.6 0.3 share_tokens.1
  9.0 0.0 copy-start
  9.0 1.0 copy-done
  10.0 24.5 %all-gather = bf16[1088,128]{1,0:T(8,128)(2,1)S(1)} all-gather(bf16[272,128]{1,0:T(8,128)(2,1)S(1)} %pack.1), channel_id=2, replica_groups=mesh['zh'=4,'zl'=4,'x'=4,'y'=4,'core'=2] {'zh'}, dimensions={0}, use_global_device_ids=true | all-gather | bytes 348160 | tf_op jit(solution)/shard_map/gather_weight/all_gather | solution.py:215
  34.5 0.0 all-to-all-done
  34.5 4.1 %all-to-all-start.1 = ((bf16[4,288,512]{2,1,0:T(8,128)(2,1)}), bf16[4,288,512]{2,1,0:T(8,128)(2,1)S(1)}, u32[]{:S(2)}, u32[]{:S(2)}) async-start(bf16[4,288,512]{2,1,0:T(8,128)(2,1)} %copy-done), calls=%async_computation.1 | async-start | bytes 2359296 | tf_op jit(solution)/shard_map/share_tokens/all_to_all | solution.py:229
  38.6 2.7 %collective-permute-start.2 = (bf16[4,272,128]{2,1,0:T(8,128)(2,1)S(1)}, bf16[4,272,128]{2,1,0:T(8,128)(2,1)S(1)}, u32[]{:S(2)}, u32[]{:S(2)}) collective-permute-start(bf16[4,272,128]{2,1,0:T(8,128)(2,1)S(1)} %bitcast.16), channel_id=1, source_target_pairs={{480,0},{0,32},{32,64},{64,96},{96,128},{128,160},{160,192},{192,2... | collective-permute-start | bytes 835592 | tf_op jit(solution)/shard_map/gather_weight/ppermute | solution.py:218
  41.3 4.8 %collective-permute-start.1 = (bf16[4,272,128]{2,1,0:T(8,128)(2,1)S(1)}, bf16[4,272,128]{2,1,0:T(8,128)(2,1)}, u32[]{:S(2)}, u32[]{:S(2)}) collective-permute-start(bf16[4,272,128]{2,1,0:T(8,128)(2,1)S(1)} %bitcast.17), channel_id=1, source_target_pairs={{64,0},{480,32},{128,64},{32,96},{192,128},{96,160},{256,192},{160... | collective-permute-start | bytes 835592 | tf_op jit(solution)/shard_map/gather_weight/ppermute | solution.py:218
  46.1 2.1 %collective-permute-start = (bf16[4,272,128]{2,1,0:T(8,128)(2,1)S(1)}, bf16[4,272,128]{2,1,0:T(8,128)(2,1)}, u32[]{:S(2)}, u32[]{:S(2)}) collective-permute-start(bf16[4,272,128]{2,1,0:T(8,128)(2,1)S(1)} %bitcast.18), channel_id=1, source_target_pairs={{32,0},{64,32},{96,64},{128,96},{160,128},{192,160},{224,192},{256... | collective-permute-start | bytes 835592 | tf_op jit(solution)/shard_map/gather_weight/ppermute | solution.py:218
  48.3 3.3 %all-to-all-done.1.shared = bf16[4,288,512]{2,1,0:T(8,128)(2,1)S(1)} async-done(((bf16[4,288,512]{2,1,0:T(8,128)(2,1)}), bf16[4,288,512]{2,1,0:T(8,128)(2,1)S(1)}, u32[]{:S(2)}, u32[]{:S(2)}) %all-to-all-start.1) | async-done | bytes 1179680 | tf_op jit(solution)/shard_map/share_tokens/all_to_all | solution.py:229
  51.5 0.0 collective-permute-done.2.w3
  51.5 0.0 collective-permute-done.1.w2
  51.6 5.9 %collective-permute-done.w1 = bf16[4,272,128]{2,1,0:T(8,128)(2,1)} collective-permute-done((bf16[4,272,128]{2,1,0:T(8,128)(2,1)S(1)}, bf16[4,272,128]{2,1,0:T(8,128)(2,1)}, u32[]{:S(2)}, u32[]{:S(2)}) %collective-permute-start) | collective-permute-done | bytes 278560 | tf_op jit(solution)/shard_map/gather_weight/ppermute | solution.py:218
  57.4 2.1 %other_half.1 = bf16[1536,512]{1,0:T(8,128)(2,1)S(1)} custom-call(s32[4]{0:T(128)S(1)} %pad_add_fusion.place, bf16[1536,512]{1,0:T(8,128)(2,1)S(1)} %bitcast.14, bf16[4,272,128]{2,1,0:T(8,128)(2,1)S(1)} %bitcast.19, bf16[4,272,128]{2,1,0:T(8,128)(2,1)} %collective-permute-done.w1, bf16[4,272,128]{2,1,0:T(8,128)(2,1)} %collective-permute-done.1.w2, ...), custom_call_target="tpu_custom_call" | custom-call | bytes 1024 | tf_op jit(solution)/shard_map/other_half/pallas_call | solution.py:234
  59.5 4.7 %collective-permute-start.3 = (bf16[1536,512]{1,0:T(8,128)(2,1)S(1)}, bf16[1536,512]{1,0:T(8,128)(2,1)S(1)}, u32[]{:S(2)}, u32[]{:S(2)}) collective-permute-start(bf16[1536,512]{1,0:T(8,128)(2,1)S(1)} %other_half.1), channel_id=1, source_target_pairs={{1,0},{0,1},{3,2},{2,3},{5,4},{4,5},{7,6},{6,7},{9,8},{8,9},{11,10... | collective-permute-start | bytes 4718600 | tf_op jit(solution)/shard_map/other_half/ppermute | solution.py:244
  64.2 2.1 %own_half.2.first = bf16[1536,512]{1,0:T(8,128)(2,1)S(1)} custom-call(s32[4]{0:T(128)S(1)} %pad_add_fusion.place, bf16[1536,512]{1,0:T(8,128)(2,1)S(1)} %bitcast.15, bf16[4,272,128]{2,1,0:T(8,128)(2,1)S(1)} %bitcast.20, bf16[4,272,128]{2,1,0:T(8,128)(2,1)} %collective-permute-done.w1, bf16[4,272,128]{2,1,0:T(8,128)(2,1)} %collective-permute-done.1.w2, ...), custom_call_target="tpu_custom_call" | custom-call | bytes 1024 | tf_op jit(solution)/shard_map/own_half/pallas_call | solution.py:234
  66.3 0.9 collective-permute-done.3.second
  67.2 1.4 %own_half.3 = bf16[16,128,512]{2,1,0:T(8,128)(2,1)S(1)} custom-call(bf16[1536,512]{1,0:T(8,128)(2,1)S(1)} %own_half.2.first, bf16[1536,512]{1,0:T(8,128)(2,1)S(1)} %collective-permute-done.3.second, bf16[4,272,128]{2,1,0:T(8,128)(2,1)S(1)} %bitcast.21, bf16[4,272,128]{2,1,0:T(8,128)(2,1)} %collective-permute-done.w1, ...), custom_call_target="tpu_custom_call" | custom-call | bytes 1024 | tf_op jit(solution)/shard_map/own_half/pallas_call | solution.py:246
  68.7 33.8 %all_to_all.20.parts = bf16[16,128,512]{2,1,0:T(8,128)(2,1)S(1)} all-to-all(bf16[16,128,512]{2,1,0:T(8,128)(2,1)S(1)} %own_half.3), channel_id=1, replica_groups=mesh['zh'=4,'zl'=4,'x'=4,'y'=4,'core'=2] {'x','y'}, dimensions={0} | all-to-all | bytes 4194304 | tf_op jit(solution)/shard_map/exchange_parts/all_to_all | solution.py:255
  102.4 1.1 token_sums.1.mine
  103.5 4.0 %collective-permute-start.4 = (f32[96,256]{1,0:T(8,128)S(1)}, f32[96,256]{1,0:T(8,128)S(1)}, u32[]{:S(2)}, u32[]{:S(2)}) collective-permute-start(f32[96,256]{1,0:T(8,128)S(1)} %token_sums.1.mine), channel_id=1, source_target_pairs={{1,0},{0,1},{3,2},{2,3},{5,4},{4,5},{7,6},{6,7},{9,8},{8,9},{11,10... | collective-permute-start | bytes 294920 | tf_op jit(solution)/shard_map/token_sums/ppermute | solution.py:265
  107.5 0.9 collective-permute-done.4.theirs
  108.4 0.5 gram.1
  108.9 6.9 %all_to_all.21.grams = f32[4,32,128]{2,1,0:T(8,128)S(1)} all-to-all(f32[4,32,128]{2,1,0:T(8,128)S(1)} %gram.1), channel_id=1, replica_groups=mesh['zh'=4,'zl'=4,'x'=4,'y'=4,'core'=2] {'y'}, dimensions={0} | all-to-all | bytes 131072 | tf_op jit(solution)/shard_map/gram/all_to_all | solution.py:275
  115.8 1.7 %scores.1 = (f32[64,64]{1,0:T(8,128)}, f32[1,64]{1,0:T(1,128)}) custom-call(s32[4]{0:T(128)S(1)} %pad_add_fusion.place, f32[4,32,128]{2,1,0:T(8,128)S(1)} %all_to_all.21.grams, bf16[16,128,512]{2,1,0:T(8,128)(2,1)S(1)} %all_to_all.20.parts), custom_call_target="tpu_custom_call" | custom-call | flops 4194304 | bytes 3145728 | tf_op jit(solution)/shard_map/scores/pallas_call | solution.py:277
Async XLA Ops:
  0.6 1.0 copy-start.1
  2.8 5.2 %copy-start.7 = (bf16[512,64]{0,1:T(8,128)(2,1)S(1)}, bf16[512,64]{0,1:T(8,128)(2,1)}, u32[]{:S(2)}) copy-start(bf16[512,64]{0,1:T(8,128)(2,1)} %param.11) | copy-start | bytes 196612
  2.9 5.2 %copy-start.8 = (f32[1,4096]{1,0:T(1,128)S(1)}, f32[1,4096]{1,0:T(1,128)}, u32[]{:S(2)}) copy-start(f32[1,4096]{1,0:T(1,128)} %query.1) | copy-start | bytes 49156
  2.9 5.7 %copy-start.2 = (bf16[1,384,512]{2,1,0:T(8,128)(2,1)S(1)}, bf16[1,384,512]{2,1,0:T(8,128)(2,1)}, u32[]{:S(2)}) copy-start(bf16[1,384,512]{2,1,0:T(8,128)(2,1)} %param.8) | copy-start | bytes 1179652
  2.9 5.7 %copy-start.3 = (bf16[1,384,512]{2,1,0:T(8,128)(2,1)S(1)}, bf16[1,384,512]{2,1,0:T(8,128)(2,1)}, u32[]{:S(2)}) copy-start(bf16[1,384,512]{2,1,0:T(8,128)(2,1)} %param.9) | copy-start | bytes 1179652
  2.9 5.7 %copy-start.4 = (bf16[1,384,512]{2,1,0:T(8,128)(2,1)S(1)}, bf16[1,384,512]{2,1,0:T(8,128)(2,1)}, u32[]{:S(2)}) copy-start(bf16[1,384,512]{2,1,0:T(8,128)(2,1)} %param.10) | copy-start | bytes 1179652
  2.9 5.7 %copy-start.5 = (bf16[512,64]{0,1:T(8,128)(2,1)S(1)}, bf16[512,64]{0,1:T(8,128)(2,1)}, u32[]{:S(2)}) copy-start(bf16[512,64]{0,1:T(8,128)(2,1)} %param.13) | copy-start | bytes 196612
  2.9 5.7 %copy-start.6 = (bf16[512,64]{0,1:T(8,128)(2,1)S(1)}, bf16[512,64]{0,1:T(8,128)(2,1)}, u32[]{:S(2)}) copy-start(bf16[512,64]{0,1:T(8,128)(2,1)} %param.14) | copy-start | bytes 196612
  2.9 5.7 %copy-start.9 = (f32[512]{0:T(512)S(1)}, f32[512]{0:T(512)}, u32[]{:S(2)}) copy-start(f32[512]{0:T(512)} %param.12) | copy-start | bytes 6148
  2.9 31.6 %all-to-all-start = ((bf16[4,384,512]{2,1,0:T(8,128)(2,1)}), bf16[4,384,512]{2,1,0:T(8,128)(2,1)S(1)}, u32[]{:S(2)}, u32[]{:S(2)}) async-start(bf16[4,384,512]{2,1,0:T(8,128)(2,1)} %gather_tokens.1), calls=%async_computation | async-start | bytes 3145728 | tf_op jit(solution)/shard_map/gather_tokens/all_to_all | solution.py:213
  9.0 1.0 copy-start
  34.5 17.0 %all-to-all-start.1 = ((bf16[4,288,512]{2,1,0:T(8,128)(2,1)}), bf16[4,288,512]{2,1,0:T(8,128)(2,1)S(1)}, u32[]{:S(2)}, u32[]{:S(2)}) async-start(bf16[4,288,512]{2,1,0:T(8,128)(2,1)} %copy-done), calls=%async_computation.1 | async-start | bytes 2359296 | tf_op jit(solution)/shard_map/share_tokens/all_to_all | solution.py:229
  38.6 12.9 %collective-permute-start.2 = (bf16[4,272,128]{2,1,0:T(8,128)(2,1)S(1)}, bf16[4,272,128]{2,1,0:T(8,128)(2,1)S(1)}, u32[]{:S(2)}, u32[]{:S(2)}) collective-permute-start(bf16[4,272,128]{2,1,0:T(8,128)(2,1)S(1)} %bitcast.16), channel_id=1, source_target_pairs={{480,0},{0,32},{32,64},{64,96},{96,128},{128,160},{160,192},{192,2... | collective-permute-start | bytes 835592 | tf_op jit(solution)/shard_map/gather_weight/ppermute | solution.py:218
  41.3 10.2 %collective-permute-start.1 = (bf16[4,272,128]{2,1,0:T(8,128)(2,1)S(1)}, bf16[4,272,128]{2,1,0:T(8,128)(2,1)}, u32[]{:S(2)}, u32[]{:S(2)}) collective-permute-start(bf16[4,272,128]{2,1,0:T(8,128)(2,1)S(1)} %bitcast.17), channel_id=1, source_target_pairs={{64,0},{480,32},{128,64},{32,96},{192,128},{96,160},{256,192},{160... | collective-permute-start | bytes 835592 | tf_op jit(solution)/shard_map/gather_weight/ppermute | solution.py:218
  46.1 11.3 %collective-permute-start = (bf16[4,272,128]{2,1,0:T(8,128)(2,1)S(1)}, bf16[4,272,128]{2,1,0:T(8,128)(2,1)}, u32[]{:S(2)}, u32[]{:S(2)}) collective-permute-start(bf16[4,272,128]{2,1,0:T(8,128)(2,1)S(1)} %bitcast.18), channel_id=1, source_target_pairs={{32,0},{64,32},{96,64},{128,96},{160,128},{192,160},{224,192},{256... | collective-permute-start | bytes 835592 | tf_op jit(solution)/shard_map/gather_weight/ppermute | solution.py:218
  59.5 7.7 %collective-permute-start.3 = (bf16[1536,512]{1,0:T(8,128)(2,1)S(1)}, bf16[1536,512]{1,0:T(8,128)(2,1)S(1)}, u32[]{:S(2)}, u32[]{:S(2)}) collective-permute-start(bf16[1536,512]{1,0:T(8,128)(2,1)S(1)} %other_half.1), channel_id=1, source_target_pairs={{1,0},{0,1},{3,2},{2,3},{5,4},{4,5},{7,6},{6,7},{9,8},{8,9},{11,10... | collective-permute-start | bytes 4718600 | tf_op jit(solution)/shard_map/other_half/ppermute | solution.py:244
  103.5 4.9 %collective-permute-start.4 = (f32[96,256]{1,0:T(8,128)S(1)}, f32[96,256]{1,0:T(8,128)S(1)}, u32[]{:S(2)}, u32[]{:S(2)}) collective-permute-start(f32[96,256]{1,0:T(8,128)S(1)} %token_sums.1.mine), channel_id=1, source_target_pairs={{1,0},{0,1},{3,2},{2,3},{5,4},{4,5},{7,6},{6,7},{9,8},{8,9},{11,10... | collective-permute-start | bytes 294920 | tf_op jit(solution)/shard_map/token_sums/ppermute | solution.py:265

commit v3 on v2

v3 whole, which is shorter than its diff:
```python
import functools
import math

import jax
import jax.numpy as jnp
import numpy as np
from jax import lax
from jax.experimental import pallas as pl
from jax.experimental.pallas import tpu as pltpu
from jax.sharding import Mesh, PartitionSpec as P

Z = ("zh", "zl")
PLANE = ("x", "y")
TENSOR = ("y", "core")
EPS = 1e-05
NT = (((1,), (1,)), ((), ()))
TN = (((0,), (0,)), ((), ()))
HIGHEST = lax.Precision.HIGHEST
PARAMS = pltpu.CompilerParams(vmem_limit_bytes=16 * 1024 * 1024)
WIDE = pltpu.CompilerParams(vmem_limit_bytes=56 * 1024 * 1024)
VMEM = pl.BlockSpec(memory_space=pltpu.VMEM)
ANY = pl.BlockSpec(memory_space=pl.ANY)


def cost(flops, moved):
    return pl.CostEstimate(flops=flops, bytes_accessed=moved, transcendentals=0)


def split3(value):
    high = value.astype(jnp.bfloat16)
    rest = value - high.astype(jnp.float32)
    mid = rest.astype(jnp.bfloat16)
    low = (rest - mid.astype(jnp.float32)).astype(jnp.bfloat16)
    return high, mid, low


def prepare_kernel(
    tokens, resid, cot, gain, weight, query, proj_in, proj_out, copies, piece, shared,
    tokens_here, gain_here, weight_here, query_here, in_here, piece_here, shared_here, sems,
):
    pairs = [
        (weight, weight_here),
        (query, query_here),
        (tokens, tokens_here),
        (gain, gain_here),
        (proj_in, in_here),
    ]
    for at in range(4):
        rows = pl.ds(96 * at, 96)
        pairs.append((resid.at[rows], shared_here.at[at, pl.ds(0, 96)]))
        pairs.append((cot.at[rows], shared_here.at[at, pl.ds(96, 96)]))
        pairs.append((proj_out, shared_here.at[at, pl.ds(192, 64)]))
    loads = [pltpu.make_async_copy(*pair, sems.at[at]) for at, pair in enumerate(pairs)]
    for copy in loads:
        copy.start()
    stores = [pltpu.make_async_copy(tokens_here, copies.at[at], sems.at[17 + at]) for at in range(4)]
    stores.append(pltpu.make_async_copy(piece_here, piece, sems.at[21]))
    for at in range(4):
        stores.append(pltpu.make_async_copy(shared_here.at[at], shared.at[at], sems.at[22 + at]))
    loads[2].wait()
    for copy in stores[0:4]:
        copy.start()
    loads[0].wait()
    loads[1].wait()
    for at in range(4):
        piece_here[64 * at : 64 * at + 64, :] = weight_here[:, 128 * at : 128 * at + 128]
    first = (lax.axis_index("y") * 2 + lax.axis_index("core")) * 512
    rows = [query_here[:, pl.ds(pl.multiple_of(first + j * 128, 128), 128)] for j in range(4)]
    high, low, _ = split3(jnp.concatenate(rows, axis=0))
    rows = [high.astype(jnp.float32), low.astype(jnp.float32), jnp.zeros((8, 128), jnp.float32)]
    piece_here[256:272, :] = jnp.concatenate(rows, axis=0).astype(jnp.bfloat16)
    stores[4].start()
    loads[3].wait()
    loads[4].wait()
    in_part = lax.dot_general(tokens_here[...], in_here[...], NT, preferred_element_type=jnp.float32)
    high, low, _ = split3(in_part)
    terms = jnp.concatenate([high.astype(jnp.float32), low.astype(jnp.float32)], axis=1)
    gains = [term.astype(jnp.float32) for term in split3(gain_here[...])]
    gains = jnp.concatenate(gains + [jnp.zeros((5, 512), jnp.float32)], axis=0)
    for at in range(4):
        first = 96 * at
        four = [terms[first + 24 * k : first + 24 * k + 24] for k in range(4)]
        tail = jnp.concatenate([jnp.concatenate(four, axis=1), gains], axis=0)
        shared_here[at, 256:288, :] = tail.astype(jnp.bfloat16)
        for k in range(3):
            loads[5 + 3 * at + k].wait()
        stores[5 + at].start()
    for copy in stores:
        copy.wait()


def product(tokens, first, second, pair):
    strips = []
    for zh in (2 * pair, 2 * pair + 1):
        for ref in (first, second):
            blocks = [ref[zh, 64 * at : 64 * at + 64, :] for at in range(4)]
            strips.append(jnp.concatenate(blocks, axis=1))
    rows = jnp.concatenate(strips, axis=0)
    return lax.dot_general(tokens[...], rows, NT, preferred_element_type=jnp.float32)


def half_kernel(mine, tokens, w0, w1, w2, w3, out, *queries):
    weights = (w0, w1, w2, w3)
    half = lax.axis_index("core") if mine else 1 - lax.axis_index("core")
    slot = lax.rem(2 * half - lax.axis_index("zl") + 4, 4)
    for at in range(4):

        @pl.when(slot == at)
        def _():
            for pair in range(2):
                total = product(tokens, weights[at], weights[(at + 1) % 4], pair)
                out[:, 256 * pair : 256 * pair + 256] = total.astype(jnp.bfloat16)

    for ref in queries:
        slots = []
        for weight in weights:
            rows = [weight[zh, 256:272, :].astype(jnp.float32)[0:8] for zh in range(4)]
            slots.append(jnp.concatenate(rows, axis=0))
        ref[...] = jnp.concatenate(slots, axis=1).astype(jnp.bfloat16)


def add_kernel(first, second, queries, out):
    for at in range(16):
        rows = slice(96 * at, 96 * at + 96)
        total = first[rows, :].astype(jnp.float32) + second[rows, :].astype(jnp.float32)
        out[at, 0:96, :] = total.astype(jnp.bfloat16)
        out[at, 96:128, :] = queries[...]


def sums_kernel(parts, shared, out):
    blocks = []
    for x in range(4):
        total = parts[4 * x, 0:96, :].astype(jnp.float32)
        for y in range(1, 4):
            total = total + parts[4 * x + y, 0:96, :].astype(jnp.float32)
        blocks.append(total)
    weighted_out = stream_out = in_proj = jnp.zeros((96, 64), jnp.float32)
    squares = dots = jnp.zeros((96, 1), jnp.float32)
    for y in range(4):
        strips = [block[:, 128 * y + 64 * k : 128 * y + 64 * k + 64] for k in range(2) for block in blocks]
        stream = shared[y, 0:96, :].astype(jnp.float32) + jnp.concatenate(strips, axis=1)
        tail = shared[y, 256:288, :].astype(jnp.float32)
        gain = tail[24:25] + tail[25:26] + tail[26:27]
        weighted = gain * shared[y, 96:192, :].astype(jnp.float32)
        squares = squares + jnp.sum(stream * stream, axis=1, keepdims=True)
        dots = dots + jnp.sum(weighted * stream, axis=1, keepdims=True)
        rows = jnp.concatenate(split3(weighted) + split3(stream), axis=0)
        terms = lax.dot_general(rows, shared[y, 192:256, :], NT, preferred_element_type=jnp.float32)
        weighted_out = weighted_out + (terms[0:96] + terms[96:192] + terms[192:288])
        stream_out = stream_out + (terms[288:384] + terms[384:480] + terms[480:576])
        four = [tail[0:24, 128 * k : 128 * k + 128] for k in range(4)]
        four = jnp.concatenate(four, axis=0)
        in_proj = in_proj + (four[:, 0:64] + four[:, 64:128])
    lane = lax.broadcasted_iota(jnp.int32, (96, 64), 1)
    stats = jnp.where(lane == 0, squares, jnp.where(lane == 1, dots, 0.0))
    total = jnp.concatenate([weighted_out, stream_out, in_proj, stats], axis=1)
    out[0:48, :] = jnp.concatenate([total[0:48], total[48:96]], axis=1)
    for at in range(16):
        terms = parts[at, 96:128, :].astype(jnp.float32)
        rows = [terms[8 * zh : 8 * zh + 4] + terms[8 * zh + 4 : 8 * zh + 8] for zh in range(4)]
        out[48 + 16 * at : 64 + 16 * at, :] = jnp.concatenate(rows, axis=0)


def gram_kernel(width, mine, theirs, out):
    total = mine[0:48, :] + theirs[0:48, :]
    total = jnp.concatenate([total[:, 0:256], total[:, 256:512]], axis=0)
    squares, dots = total[:, 192:193], total[:, 193:194]
    inv_rms = lax.rsqrt(squares / width + EPS)
    out_proj = inv_rms * total[:, 0:64] - total[:, 64:128] * (inv_rms**3 / width * dots)
    row = lax.broadcasted_iota(jnp.int32, (64, 64), 0)
    column = lax.broadcasted_iota(jnp.int32, (64, 64), 1)
    source = jnp.where(column < 32, 2 * column, 2 * column - 63)
    order = (row == source).astype(jnp.float32)
    in_proj = jnp.dot(total[:, 128:192], order, precision=HIGHEST)
    gram = lax.dot_general(in_proj, out_proj, TN, precision=HIGHEST, preferred_element_type=jnp.float32)
    packed = jnp.concatenate([gram[0:32], gram[32:64]], axis=1)
    for at in range(4):
        out[at] = packed


def score_kernel(length, grams, mine, theirs, grads, scores, packed):
    total = grams[0] + grams[1] + grams[2] + grams[3]
    total = total / math.sqrt(length)
    packed[...] = total
    grads[pl.ds(0, 32, stride=2), :] = total[:, 0:64]
    grads[pl.ds(1, 32, stride=2), :] = total[:, 64:128]
    zl, core = lax.axis_index("zl"), lax.axis_index("core")
    sources = []
    for x in range(4):
        every = None
        for y in range(4):
            rows = slice(48 + 16 * (4 * x + y), 64 + 16 * (4 * x + y))
            halves = [packed[8 * y + 4 * at : 8 * y + 4 * at + 4, :] for at in range(2)]
            for queries, first in ((mine, 0), (theirs, 1)):
                four = jnp.where(core == first, halves[0], halves[1])
                four = jnp.concatenate([four] * 4, axis=0)
                four = jnp.concatenate([four] * 4, axis=1)
                term = queries[rows, :] * four
                every = term if every is None else every + term
        sources = sources + [every[:, 128 * at : 128 * at + 128] for at in range(4)]
    every = jnp.concatenate(sources, axis=0)
    ones = jnp.ones((8, 128), jnp.float32)
    flat = lax.dot_general(ones, every, NT, precision=HIGHEST, preferred_element_type=jnp.float32)
    row = lax.broadcasted_iota(jnp.int32, (256, 64), 0) // 4
    column = lax.broadcasted_iota(jnp.int32, (256, 64), 1)
    chosen = ((row % 4) * 16 + (row // 4 + zl) % 4 * 4 + row // 16 == column).astype(jnp.float32)
    result = jnp.dot(flat, chosen, precision=HIGHEST, preferred_element_type=jnp.float32)
    scores[...] = result[0:1] / 64.0


def swing(size):
    return [((at + (2 if at % 2 == 0 else -2)) % size, at) for at in range(size)]


def shift(size, by):
    return [((at + by) % size, at) for at in range(size)]


def shards(attn_out, resid, cotangent, o_weight, norm_gain, proj_in, proj_out, queries):
    tokens = attn_out[0]
    length, features = tokens.shape
    width = features * 8
    bf16, f32 = jnp.bfloat16, jnp.float32

    with jax.named_scope("prepare"):
        copies, piece, shared = pl.pallas_call(
            prepare_kernel,
            out_shape=(
                jax.ShapeDtypeStruct((4, length, features), bf16),
                jax.ShapeDtypeStruct((272, 128), bf16),
                jax.ShapeDtypeStruct((4, 288, 512), bf16),
            ),
            in_specs=[ANY] * 8,
            out_specs=(ANY, ANY, ANY),
            scratch_shapes=[
                pltpu.VMEM((length, features), bf16),
                pltpu.VMEM((1, 512), f32),
                pltpu.VMEM((64, 512), bf16),
                pltpu.VMEM((1, 4096), f32),
                pltpu.VMEM((64, 512), bf16),
                pltpu.VMEM((272, 128), bf16),
                pltpu.VMEM((4, 288, 512), bf16),
                pltpu.SemaphoreType.DMA((26,)),
            ],
            compiler_params=WIDE,
            cost_estimate=cost(2 * length * 512 * 64, 5 << 20),
        )(
            tokens, resid[0], cotangent[0], norm_gain[None], o_weight.T, queries,
            proj_in.T, proj_out.T,
        )
    with jax.named_scope("gather_tokens"):
        every = lax.all_to_all(copies, "x", 0, 0, tiled=True).reshape(4 * length, features)
    with jax.named_scope("gather_weight"):
        mine = lax.all_gather(piece, "zh", axis=0)
        mine, every = lax.optimization_barrier((mine, every))
        ways = (shift(16, 1), swing(16), shift(16, -1))
        all_weights = [mine] + [lax.ppermute(mine, Z, way) for way in ways]
    with jax.named_scope("share_tokens"):
        shared, every = lax.optimization_barrier((shared, every))
        shared = lax.all_to_all(shared, "y", 0, 0, tiled=True)
        shared, every = lax.optimization_barrier((shared, every))


    def partial_sums(own):
        sums = jax.ShapeDtypeStruct((4 * length, 512), bf16)
        query = jax.ShapeDtypeStruct((32, 512), bf16)
        return pl.pallas_call(
            functools.partial(half_kernel, own),
            out_shape=sums if own else (sums, query),
            in_specs=[VMEM] * 5,
            out_specs=VMEM if own else (VMEM, VMEM),
            compiler_params=PARAMS,
            cost_estimate=cost(0, 1 << 10),
        )(every, *all_weights)

    with jax.named_scope("other_half"):
        other, query = partial_sums(False)
        other = lax.ppermute(other, "core", shift(2, 1))
    with jax.named_scope("own_half"):
        partial = pl.pallas_call(
            add_kernel,
            out_shape=jax.ShapeDtypeStruct((16, length // 4 + 32, 512), bf16),
            in_specs=[VMEM] * 3,
            out_specs=VMEM,
            compiler_params=PARAMS,
            cost_estimate=cost(0, 1 << 10),
        )(partial_sums(True), other, query)
    with jax.named_scope("exchange_parts"):
        parts = lax.all_to_all(partial, PLANE, 0, 0, tiled=True)
    with jax.named_scope("token_sums"):
        sums = pl.pallas_call(
            sums_kernel,
            out_shape=jax.ShapeDtypeStruct((304, 512), f32),
            in_specs=[VMEM, VMEM],
            out_specs=VMEM,
            compiler_params=PARAMS,
            cost_estimate=cost(14 * length * 512 * 64, 4 << 20),
        )(parts, shared)
        theirs = lax.ppermute(sums, "core", shift(2, 1))
    with jax.named_scope("gram"):
        gram = pl.pallas_call(
            functools.partial(gram_kernel, width),
            out_shape=jax.ShapeDtypeStruct((4, 32, 128), f32),
            in_specs=[VMEM, VMEM],
            out_specs=VMEM,
            compiler_params=PARAMS,
            cost_estimate=cost(1 << 22, 1 << 19),
        )(sums, theirs)
        gram = lax.all_to_all(gram, "y", 0, 0, tiled=True)
    with jax.named_scope("scores"):
        grads, scores = pl.pallas_call(
            functools.partial(score_kernel, length),
            out_shape=(jax.ShapeDtypeStruct((64, 64), f32), jax.ShapeDtypeStruct((1, 64), f32)),
            in_specs=[VMEM] * 3,
            out_specs=(VMEM, VMEM),
            scratch_shapes=[pltpu.VMEM((32, 128), f32)],
            compiler_params=PARAMS,
            cost_estimate=cost(1 << 22, 3 << 20),
        )(gram, sums, theirs)
    return grads[None], scores


def solution(mesh):
    devices = np.asarray(mesh.devices).reshape(4, 4, 4, 4, 2)
    fine = Mesh(devices, ("zh", "zl", "x", "y", "core"))
    dp = ("zh", "zl", "x")
    in_specs = (
        P(dp, None, TENSOR),
        P(dp, None, TENSOR),
        P(dp, None, TENSOR),
        P(TENSOR, dp),
        P(TENSOR),
        P(TENSOR, None),
        P(TENSOR, None),
        P(dp, None),
    )
    out_specs = (P(dp, None, None), P(dp, None))
    return jax.shard_map(shards, mesh=fine, in_specs=in_specs, out_specs=out_specs, check_vma=False)
```

time: 118 us -> 116 us (0.983)
  local copies, waits for them, and re-layouts: 2.06 us -> 0.01 us
  waiting for transfers between devices: 11 us -> 12.2 us
    ppermute x3, waiting for transfers between devices: 5.87 us -> 8.05 us  [shards(): all_weights = [mine] + [lax.ppermute(mine, Z, way) for way in ways]]
    unnamed x20 -> x2, local copies, waits for them, and re-layouts: 2.06 us -> 0.01 us
    ppermute x3, starting transfers between devices: 9.65 us -> 11.4 us  [shards(): all_weights = [mine] + [lax.ppermute(mine, Z, way) for way in ways]]
    all_to_all x1, waiting for transfers between devices: 3.26 us -> 1.49 us  [shards(): shared = lax.all_to_all(shared, 'y', 0, 0, tiled=True)]
    pallas_call x6 -> x4, Pallas kernels: 7.33 us -> 8.15 us  [the longest x2 4.12 us: partial_sums(): pl.pallas_call(functools.partial(half_kernel, own), out_shape=sums if own...]
  transfers between devices with their start and end apart: 7 -> 7, of which waited for: 4 -> 4; matrix products, arithmetic and copies ran while one was open for 0% -> 0% of each run, Pallas kernels for 3% -> 2%
where the time goes in v3:
time: 116 us; the launch traced here: 115 us
  blocking collectives  64.1 us (55%)
  starting transfers between devices  28.3 us (24%)
  waiting for transfers between devices  12.2 us (11%)
  Pallas kernels  10.1 us (9%)
    all_to_all x1, blocking collectives, shards(): parts = lax.all_to_all(partial, PLANE, 0, 0, tiled=True)  32.7 us
    all_gather x1, blocking collectives, shards(): mine = lax.all_gather(piece, 'zh', axis=0)  24.5 us
    ppermute x3, starting transfers between devices, shards(): all_weights = [mine] + [lax.ppermute(mine, Z, way) for way in ways]  11.4 us
    ppermute x3, waiting for transfers between devices, shards(): all_weights = [mine] + [lax.ppermute(mine, Z, way) for way in ways]  8.05 us
    all_to_all x1, blocking collectives, shards(): gram = lax.all_to_all(gram, 'y', 0, 0, tiled=True)  6.89 us
    all_to_all x1, starting transfers between devices, shards(): lax.all_to_all(copies, 'x', 0, 0, tiled=True).reshape(4 * length, features)  4.99 us
    all_to_all x1, starting transfers between devices, shards(): shared = lax.all_to_all(shared, 'y', 0, 0, tiled=True)  4.19 us
    pallas_call x2, Pallas kernels, partial_sums(): pl.pallas_call(functools.partial(half_kernel, own), out_shape=sums if own...  4.12 us
  transfers between devices with their start and end apart: 7, of which 4 were waited for; matrix products, arithmetic and copies ran while one was open for 0% of the time, Pallas kernels for 2%

profile of v3, /device:TPU:1, one launch (start us, length us, event | category | flops | bytes accessed | tf_op | source)
XLA Modules:
  0.0 115.4 jit_solution(3627869115170271873)
XLA Ops:
  0.6 2.8 %prepare.1 = (bf16[4,384,512]{2,1,0:T(8,128)(2,1)}, bf16[272,128]{1,0:T(8,128)(2,1)}, bf16[4,288,512]{2,1,0:T(8,128)(2,1)}) custom-call(bf16[384,512]{1,0:T(8,128)(2,1)} %bitcast.17, bf16[384,512]{1,0:T(8,128)(2,1)} %bitcast.18, bf16[384,512]{1,0:T(8,128)(2,1)} %bitcast.19, f32[1,512]{1,0:T(1,128)} %bitcast.23, bf16[64,512]{1,0:T(8,128)(2,1)} %bitcast.20, ...), custom_call_target="tpu_custom_call" | custom-call | flops 25165824 | bytes 5242880 | tf_op jit(solution)/shard_map/prepare/pallas_call | solution.py:226
  3.5 0.0 copy-start
  3.5 5.0 %all-to-all-start = ((bf16[4,384,512]{2,1,0:T(8,128)(2,1)}), bf16[4,384,512]{2,1,0:T(8,128)(2,1)S(1)}, u32[]{:S(2)}, u32[]{:S(2)}) async-start(bf16[4,384,512]{2,1,0:T(8,128)(2,1)} %get-tuple-element.17), calls=%async_computation | async-start | bytes 3145728 | tf_op jit(solution)/shard_map/gather_tokens/all_to_all | solution.py:252
  8.5 0.0 copy-done
  8.5 24.5 %all-gather = bf16[1088,128]{1,0:T(8,128)(2,1)S(1)} all-gather(bf16[272,128]{1,0:T(8,128)(2,1)S(1)} %copy-done), channel_id=2, replica_groups=mesh['zh'=4,'zl'=4,'x'=4,'y'=4,'core'=2] {'zh'}, dimensions={0}, use_global_device_ids=true | all-gather | bytes 348160 | tf_op jit(solution)/shard_map/gather_weight/all_gather | solution.py:254
  33.0 0.0 all-to-all-done
  33.0 4.2 %all-to-all-start.1 = ((bf16[4,288,512]{2,1,0:T(8,128)(2,1)}), bf16[4,288,512]{2,1,0:T(8,128)(2,1)S(1)}, u32[]{:S(2)}, u32[]{:S(2)}) async-start(bf16[4,288,512]{2,1,0:T(8,128)(2,1)} %get-tuple-element.19), calls=%async_computation.1 | async-start | bytes 2359296 | tf_op jit(solution)/shard_map/share_tokens/all_to_all | solution.py:260
  37.2 2.6 %collective-permute-start.2 = (bf16[4,272,128]{2,1,0:T(8,128)(2,1)S(1)}, bf16[4,272,128]{2,1,0:T(8,128)(2,1)S(1)}, u32[]{:S(2)}, u32[]{:S(2)}) collective-permute-start(bf16[4,272,128]{2,1,0:T(8,128)(2,1)S(1)} %bitcast.12), channel_id=1, source_target_pairs={{480,0},{0,32},{32,64},{64,96},{96,128},{128,160},{160,192},{192,2... | collective-permute-start | bytes 835592 | tf_op jit(solution)/shard_map/gather_weight/ppermute | solution.py:257
  39.8 6.9 %collective-permute-start.1 = (bf16[4,272,128]{2,1,0:T(8,128)(2,1)S(1)}, bf16[4,272,128]{2,1,0:T(8,128)(2,1)}, u32[]{:S(2)}, u32[]{:S(2)}) collective-permute-start(bf16[4,272,128]{2,1,0:T(8,128)(2,1)S(1)} %bitcast.13), channel_id=1, source_target_pairs={{64,0},{480,32},{128,64},{32,96},{192,128},{96,160},{256,192},{160... | collective-permute-start | bytes 835592 | tf_op jit(solution)/shard_map/gather_weight/ppermute | solution.py:257
  46.7 1.9 %collective-permute-start = (bf16[4,272,128]{2,1,0:T(8,128)(2,1)S(1)}, bf16[4,272,128]{2,1,0:T(8,128)(2,1)}, u32[]{:S(2)}, u32[]{:S(2)}) collective-permute-start(bf16[4,272,128]{2,1,0:T(8,128)(2,1)S(1)} %bitcast.14), channel_id=1, source_target_pairs={{32,0},{64,32},{96,64},{128,96},{160,128},{192,160},{224,192},{256... | collective-permute-start | bytes 835592 | tf_op jit(solution)/shard_map/gather_weight/ppermute | solution.py:257
  48.6 1.5 %all-to-all-done.1.shared = bf16[4,288,512]{2,1,0:T(8,128)(2,1)S(1)} async-done(((bf16[4,288,512]{2,1,0:T(8,128)(2,1)}), bf16[4,288,512]{2,1,0:T(8,128)(2,1)S(1)}, u32[]{:S(2)}, u32[]{:S(2)}) %all-to-all-start.1) | async-done | bytes 1179680 | tf_op jit(solution)/shard_map/share_tokens/all_to_all | solution.py:260
  50.1 0.0 collective-permute-done.2.w3
  50.1 0.0 collective-permute-done.1.w2
  50.2 8.0 %collective-permute-done.w1 = bf16[4,272,128]{2,1,0:T(8,128)(2,1)} collective-permute-done((bf16[4,272,128]{2,1,0:T(8,128)(2,1)S(1)}, bf16[4,272,128]{2,1,0:T(8,128)(2,1)}, u32[]{:S(2)}, u32[]{:S(2)}) %collective-permute-start) | collective-permute-done | bytes 278560 | tf_op jit(solution)/shard_map/gather_weight/ppermute | solution.py:257
  58.2 2.1 %other_half.1 = (bf16[1536,512]{1,0:T(8,128)(2,1)S(1)}, bf16[32,512]{1,0:T(8,128)(2,1)S(1)}) custom-call(bf16[1536,512]{1,0:T(8,128)(2,1)S(1)} %bitcast.10, bf16[4,272,128]{2,1,0:T(8,128)(2,1)S(1)} %bitcast.15, bf16[4,272,128]{2,1,0:T(8,128)(2,1)} %collective-permute-done.w1, bf16[4,272,128]{2,1,0:T(8,128)(2,1)} %collective-permute-done.1.w2, ...), custom_call_target="tpu_custom_call" | custom-call | bytes 1024 | tf_op jit(solution)/shard_map/other_half/pallas_call | solution.py:267
  60.2 3.7 %collective-permute-start.3 = (bf16[1536,512]{1,0:T(8,128)(2,1)S(1)}, bf16[1536,512]{1,0:T(8,128)(2,1)S(1)}, u32[]{:S(2)}, u32[]{:S(2)}) collective-permute-start(bf16[1536,512]{1,0:T(8,128)(2,1)S(1)} %get-tuple-element.23), channel_id=1, source_target_pairs={{1,0},{0,1},{3,2},{2,3},{5,4},{4,5},{7,6},{6,7},{9,8},{8,9},{11,10... | collective-permute-start | bytes 4718600 | tf_op jit(solution)/shard_map/other_half/ppermute | solution.py:278
  63.9 2.1 %own_half.2.first = bf16[1536,512]{1,0:T(8,128)(2,1)S(1)} custom-call(bf16[1536,512]{1,0:T(8,128)(2,1)S(1)} %bitcast.11, bf16[4,272,128]{2,1,0:T(8,128)(2,1)S(1)} %bitcast.16, bf16[4,272,128]{2,1,0:T(8,128)(2,1)} %collective-permute-done.w1, bf16[4,272,128]{2,1,0:T(8,128)(2,1)} %collective-permute-done.1.w2, bf16[4,272,128]{2,1,0:T(8,128)(2,1)S(1)} %collective-permute-done.2.w3), custom_call_target="tpu_custom_call" | custom-call | bytes 1024 | tf_op jit(solution)/shard_map/own_half/pallas_call | solution.py:267
  66.0 1.0 collective-permute-done.3.second
  67.0 0.4 own_half.3
  67.3 32.7 %all_to_all.20.parts = bf16[16,128,512]{2,1,0:T(8,128)(2,1)S(1)} all-to-all(bf16[16,128,512]{2,1,0:T(8,128)(2,1)S(1)} %own_half.3), channel_id=1, replica_groups=mesh['zh'=4,'zl'=4,'x'=4,'y'=4,'core'=2] {'x','y'}, dimensions={0} | all-to-all | bytes 4194304 | tf_op jit(solution)/shard_map/exchange_parts/all_to_all | solution.py:289
  100.1 1.2 %token_sums.1.mine = f32[304,512]{1,0:T(8,128)S(1)} custom-call(bf16[16,128,512]{2,1,0:T(8,128)(2,1)S(1)} %all_to_all.20.parts, bf16[4,288,512]{2,1,0:T(8,128)(2,1)S(1)} %all-to-all-done.1.shared), custom_call_target="tpu_custom_call" | custom-call | flops 176160768 | bytes 4194304 | tf_op jit(solution)/shard_map/token_sums/pallas_call | solution.py:291
  101.2 4.0 %collective-permute-start.4 = (f32[304,512]{1,0:T(8,128)S(1)}, f32[304,512]{1,0:T(8,128)S(1)}, u32[]{:S(2)}, u32[]{:S(2)}) collective-permute-start(f32[304,512]{1,0:T(8,128)S(1)} %token_sums.1.mine), channel_id=1, source_target_pairs={{1,0},{0,1},{3,2},{2,3},{5,4},{4,5},{7,6},{6,7},{9,8},{8,9},{11,10... | collective-permute-start | bytes 1867784 | tf_op jit(solution)/shard_map/token_sums/ppermute | solution.py:299
  105.3 1.7 %collective-permute-done.4.theirs = f32[304,512]{1,0:T(8,128)S(1)} collective-permute-done((f32[304,512]{1,0:T(8,128)S(1)}, f32[304,512]{1,0:T(8,128)S(1)}, u32[]{:S(2)}, u32[]{:S(2)}) %collective-permute-start.4) | collective-permute-done | bytes 622624 | tf_op jit(solution)/shard_map/token_sums/ppermute | solution.py:299
  106.9 0.5 gram.1
  107.4 6.9 %all_to_all.21.grams = f32[4,32,128]{2,1,0:T(8,128)S(1)} all-to-all(f32[4,32,128]{2,1,0:T(8,128)S(1)} %gram.1), channel_id=1, replica_groups=mesh['zh'=4,'zl'=4,'x'=4,'y'=4,'core'=2] {'y'}, dimensions={0} | all-to-all | bytes 131072 | tf_op jit(solution)/shard_map/gram/all_to_all | solution.py:309
  114.3 1.1 scores.1
Async XLA Ops:
  3.5 5.0 %copy-start = (bf16[272,128]{1,0:T(8,128)(2,1)S(1)}, bf16[272,128]{1,0:T(8,128)(2,1)}, u32[]{:S(2)}) copy-start(bf16[272,128]{1,0:T(8,128)(2,1)} %get-tuple-element.16) | copy-start | bytes 208900
  3.5 29.5 %all-to-all-start = ((bf16[4,384,512]{2,1,0:T(8,128)(2,1)}), bf16[4,384,512]{2,1,0:T(8,128)(2,1)S(1)}, u32[]{:S(2)}, u32[]{:S(2)}) async-start(bf16[4,384,512]{2,1,0:T(8,128)(2,1)} %get-tuple-element.17), calls=%async_computation | async-start | bytes 3145728 | tf_op jit(solution)/shard_map/gather_tokens/all_to_all | solution.py:252
  33.0 17.1 %all-to-all-start.1 = ((bf16[4,288,512]{2,1,0:T(8,128)(2,1)}), bf16[4,288,512]{2,1,0:T(8,128)(2,1)S(1)}, u32[]{:S(2)}, u32[]{:S(2)}) async-start(bf16[4,288,512]{2,1,0:T(8,128)(2,1)} %get-tuple-element.19), calls=%async_computation.1 | async-start | bytes 2359296 | tf_op jit(solution)/shard_map/share_tokens/all_to_all | solution.py:260
  37.2 12.9 %collective-permute-start.2 = (bf16[4,272,128]{2,1,0:T(8,128)(2,1)S(1)}, bf16[4,272,128]{2,1,0:T(8,128)(2,1)S(1)}, u32[]{:S(2)}, u32[]{:S(2)}) collective-permute-start(bf16[4,272,128]{2,1,0:T(8,128)(2,1)S(1)} %bitcast.12), channel_id=1, source_target_pairs={{480,0},{0,32},{32,64},{64,96},{96,128},{128,160},{160,192},{192,2... | collective-permute-start | bytes 835592 | tf_op jit(solution)/shard_map/gather_weight/ppermute | solution.py:257
  39.8 10.3 %collective-permute-start.1 = (bf16[4,272,128]{2,1,0:T(8,128)(2,1)S(1)}, bf16[4,272,128]{2,1,0:T(8,128)(2,1)}, u32[]{:S(2)}, u32[]{:S(2)}) collective-permute-start(bf16[4,272,128]{2,1,0:T(8,128)(2,1)S(1)} %bitcast.13), channel_id=1, source_target_pairs={{64,0},{480,32},{128,64},{32,96},{192,128},{96,160},{256,192},{160... | collective-permute-start | bytes 835592 | tf_op jit(solution)/shard_map/gather_weight/ppermute | solution.py:257
  46.7 11.5 %collective-permute-start = (bf16[4,272,128]{2,1,0:T(8,128)(2,1)S(1)}, bf16[4,272,128]{2,1,0:T(8,128)(2,1)}, u32[]{:S(2)}, u32[]{:S(2)}) collective-permute-start(bf16[4,272,128]{2,1,0:T(8,128)(2,1)S(1)} %bitcast.14), channel_id=1, source_target_pairs={{32,0},{64,32},{96,64},{128,96},{160,128},{192,160},{224,192},{256... | collective-permute-start | bytes 835592 | tf_op jit(solution)/shard_map/gather_weight/ppermute | solution.py:257
  60.2 6.7 %collective-permute-start.3 = (bf16[1536,512]{1,0:T(8,128)(2,1)S(1)}, bf16[1536,512]{1,0:T(8,128)(2,1)S(1)}, u32[]{:S(2)}, u32[]{:S(2)}) collective-permute-start(bf16[1536,512]{1,0:T(8,128)(2,1)S(1)} %get-tuple-element.23), channel_id=1, source_target_pairs={{1,0},{0,1},{3,2},{2,3},{5,4},{4,5},{7,6},{6,7},{9,8},{8,9},{11,10... | collective-permute-start | bytes 4718600 | tf_op jit(solution)/shard_map/other_half/ppermute | solution.py:278
  101.2 5.7 %collective-permute-start.4 = (f32[304,512]{1,0:T(8,128)S(1)}, f32[304,512]{1,0:T(8,128)S(1)}, u32[]{:S(2)}, u32[]{:S(2)}) collective-permute-start(f32[304,512]{1,0:T(8,128)S(1)} %token_sums.1.mine), channel_id=1, source_target_pairs={{1,0},{0,1},{3,2},{2,3},{5,4},{4,5},{7,6},{6,7},{9,8},{8,9},{11,10... | collective-permute-start | bytes 1867784 | tf_op jit(solution)/shard_map/token_sums/ppermute | solution.py:299

commit v4 on v3

--- a/solution.py
+++ b/solution.py
@@ -99,7 +99,7 @@
     return lax.dot_general(tokens[...], rows, NT, preferred_element_type=jnp.float32)
 
 
-def half_kernel(mine, tokens, w0, w1, w2, w3, out, *queries):
+def half_kernel(mine, tokens, w0, w1, w3, w2, out, *queries):
     weights = (w0, w1, w2, w3)
     half = lax.axis_index("core") if mine else 1 - lax.axis_index("core")
     slot = lax.rem(2 * half - lax.axis_index("zl") + 4, 4)
@@ -154,15 +154,11 @@
     lane = lax.broadcasted_iota(jnp.int32, (96, 64), 1)
     stats = jnp.where(lane == 0, squares, jnp.where(lane == 1, dots, 0.0))
     total = jnp.concatenate([weighted_out, stream_out, in_proj, stats], axis=1)
-    out[0:48, :] = jnp.concatenate([total[0:48], total[48:96]], axis=1)
-    for at in range(16):
-        terms = parts[at, 96:128, :].astype(jnp.float32)
-        rows = [terms[8 * zh : 8 * zh + 4] + terms[8 * zh + 4 : 8 * zh + 8] for zh in range(4)]
-        out[48 + 16 * at : 64 + 16 * at, :] = jnp.concatenate(rows, axis=0)
-
-
-def gram_kernel(width, mine, theirs, out):
-    total = mine[0:48, :] + theirs[0:48, :]
+    out[...] = jnp.concatenate([total[0:48], total[48:96]], axis=1)
+
+
+def gram_kernel(length, width, both, parts, out, packed):
+    total = both[0] + both[1]
     total = jnp.concatenate([total[:, 0:256], total[:, 256:512]], axis=0)
     squares, dots = total[:, 192:193], total[:, 193:194]
     inv_rms = lax.rsqrt(squares / width + EPS)
@@ -173,39 +169,42 @@
     order = (row == source).astype(jnp.float32)
     in_proj = jnp.dot(total[:, 128:192], order, precision=HIGHEST)
     gram = lax.dot_general(in_proj, out_proj, TN, precision=HIGHEST, preferred_element_type=jnp.float32)
-    packed = jnp.concatenate([gram[0:32], gram[32:64]], axis=1)
-    for at in range(4):
-        out[at] = packed
-
-
-def score_kernel(length, grams, mine, theirs, grads, scores, packed):
-    total = grams[0] + grams[1] + grams[2] + grams[3]
-    total = total / math.sqrt(length)
-    packed[...] = total
-    grads[pl.ds(0, 32, stride=2), :] = total[:, 0:64]
-    grads[pl.ds(1, 32, stride=2), :] = total[:, 64:128]
+    gram = gram / math.sqrt(length)
+    packed[...] = jnp.concatenate([gram[0:32], gram[32:64]], axis=1)
     zl, core = lax.axis_index("zl"), lax.axis_index("core")
+    factors = []
+    for y in range(4):
+        halves = [packed[8 * y + 4 * at : 8 * y + 4 * at + 4, :] for at in range(2)]
+        four = jnp.where(core == 0, halves[0], halves[1])
+        four = jnp.concatenate([four] * 8, axis=0)
+        factors.append(jnp.concatenate([four] * 4, axis=1))
     sources = []
     for x in range(4):
         every = None
         for y in range(4):
-            rows = slice(48 + 16 * (4 * x + y), 64 + 16 * (4 * x + y))
-            halves = [packed[8 * y + 4 * at : 8 * y + 4 * at + 4, :] for at in range(2)]
-            for queries, first in ((mine, 0), (theirs, 1)):
-                four = jnp.where(core == first, halves[0], halves[1])
-                four = jnp.concatenate([four] * 4, axis=0)
-                four = jnp.concatenate([four] * 4, axis=1)
-                term = queries[rows, :] * four
-                every = term if every is None else every + term
+            term = parts[4 * x + y, 96:128, :].astype(jnp.float32) * factors[y]
+            every = term if every is None else every + term
         sources = sources + [every[:, 128 * at : 128 * at + 128] for at in range(4)]
     every = jnp.concatenate(sources, axis=0)
     ones = jnp.ones((8, 128), jnp.float32)
     flat = lax.dot_general(ones, every, NT, precision=HIGHEST, preferred_element_type=jnp.float32)
-    row = lax.broadcasted_iota(jnp.int32, (256, 64), 0) // 4
-    column = lax.broadcasted_iota(jnp.int32, (256, 64), 1)
+    row = lax.broadcasted_iota(jnp.int32, (512, 128), 0) // 8
+    column = lax.broadcasted_iota(jnp.int32, (512, 128), 1)
     chosen = ((row % 4) * 16 + (row // 4 + zl) % 4 * 4 + row // 16 == column).astype(jnp.float32)
     result = jnp.dot(flat, chosen, precision=HIGHEST, preferred_element_type=jnp.float32)
-    scores[...] = result[0:1] / 64.0
+    for at in range(8):
+        out[at, 0:32, :] = packed[...]
+        out[at, 32:40, :] = result
+
+
+def final_kernel(sums, grads, scores):
+    total = sums[0, 0:32, :] + sums[2, 0:32, :] + sums[4, 0:32, :] + sums[6, 0:32, :]
+    grads[pl.ds(0, 32, stride=2), :] = total[:, 0:64]
+    grads[pl.ds(1, 32, stride=2), :] = total[:, 64:128]
+    result = sums[0, 32:40, :]
+    for at in range(1, 8):
+        result = result + sums[at, 32:40, :]
+    scores[...] = result[0:1, 0:64] / 64.0
 
 
 def swing(size):
@@ -253,8 +252,8 @@
     with jax.named_scope("gather_weight"):
         mine = lax.all_gather(piece, "zh", axis=0)
         mine, every = lax.optimization_barrier((mine, every))
-        ways = (shift(16, 1), swing(16), shift(16, -1))
-        all_weights = [mine] + [lax.ppermute(mine, Z, way) for way in ways]
+        ways = (shift(16, 1), shift(16, -1), swing(16))
+        after, before, across = [lax.ppermute(mine, Z, way) for way in ways]
     with jax.named_scope("share_tokens"):
         shared, every = lax.optimization_barrier((shared, every))
         shared = lax.all_to_all(shared, "y", 0, 0, tiled=True)
@@ -271,7 +270,7 @@
             out_specs=VMEM if own else (VMEM, VMEM),
             compiler_params=PARAMS,
             cost_estimate=cost(0, 1 << 10),
-        )(every, *all_weights)
+        )(every, mine, after, before, across)
 
     with jax.named_scope("other_half"):
         other, query = partial_sums(False)
@@ -290,33 +289,33 @@
     with jax.named_scope("token_sums"):
         sums = pl.pallas_call(
             sums_kernel,
-            out_shape=jax.ShapeDtypeStruct((304, 512), f32),
+            out_shape=jax.ShapeDtypeStruct((48, 512), f32),
             in_specs=[VMEM, VMEM],
             out_specs=VMEM,
             compiler_params=PARAMS,
             cost_estimate=cost(14 * length * 512 * 64, 4 << 20),
         )(parts, shared)
-        theirs = lax.ppermute(sums, "core", shift(2, 1))
+        sums = lax.all_gather(sums, "core", axis=0)
     with jax.named_scope("gram"):
-        gram = pl.pallas_call(
-            functools.partial(gram_kernel, width),
-            out_shape=jax.ShapeDtypeStruct((4, 32, 128), f32),
-            in_specs=[VMEM, VMEM],
+        sums = pl.pallas_call(
+            functools.partial(gram_kernel, length, width),
+            out_shape=jax.ShapeDtypeStruct((8, 40, 128), f32),
+            in_specs=[VMEM] * 2,
             out_specs=VMEM,
-            compiler_params=PARAMS,
-            cost_estimate=cost(1 << 22, 1 << 19),
-        )(sums, theirs)
-        gram = lax.all_to_all(gram, "y", 0, 0, tiled=True)
+            scratch_shapes=[pltpu.VMEM((32, 128), f32)],
+            compiler_params=PARAMS,
+            cost_estimate=cost(1 << 22, 1 << 20),
+        )(sums, parts)
+        sums = lax.all_to_all(sums, TENSOR, 0, 0, tiled=True)
     with jax.named_scope("scores"):
         grads, scores = pl.pallas_call(
-            functools.partial(score_kernel, length),
+            final_kernel,
             out_shape=(jax.ShapeDtypeStruct((64, 64), f32), jax.ShapeDtypeStruct((1, 64), f32)),
-            in_specs=[VMEM] * 3,
+            in_specs=[VMEM],
             out_specs=(VMEM, VMEM),
-            scratch_shapes=[pltpu.VMEM((32, 128), f32)],
-            compiler_params=PARAMS,
-            cost_estimate=cost(1 << 22, 3 << 20),
-        )(gram, sums, theirs)
+            compiler_params=PARAMS,
+            cost_estimate=cost(0, 1 << 18),
+        )(sums)
     return grads[None], scores
 
 

time: 116 us -> 114 us (0.983)
  waiting for transfers between devices: 12.2 us -> 6.04 us
  blocking collectives: 64.1 us -> 70.2 us
  starting transfers between devices: 28.3 us -> 26.4 us
    ppermute x4 -> x3, waiting for transfers between devices: 9.7 us -> 5.08 us  [shards(): after, before, across = [lax.ppermute(mine, Z, way) for way in ways]]
    all_gather x0 -> x1, blocking collectives: none -> 3.68 us  [shards(): sums = lax.all_gather(sums, 'core', axis=0)]
    ppermute x4 -> x3, starting transfers between devices: 15.4 us -> 13.3 us  [shards(): after, before, across = [lax.ppermute(mine, Z, way) for way in ways]]
    all_to_all x1, waiting for transfers between devices: 1.49 us -> 0.01 us  [shards(): shared = lax.all_to_all(shared, 'y', 0, 0, tiled=True)]
    all_to_all x1, blocking collectives: 6.89 us -> 8.33 us  [shards(): sums = lax.all_to_all(sums, TENSOR, 0, 0, tiled=True)]
  transfers between devices with their start and end apart: 7 -> 6, of which waited for: 4 -> 2; matrix products, arithmetic and copies ran while one was open for 0% -> 0% of each run, Pallas kernels for 2% -> 2%
where the time goes in v4:
time: 114 us
  blocking collectives  70.2 us (62%)
  starting transfers between devices  26.4 us (23%)
  Pallas kernels  10.3 us (9%)
  waiting for transfers between devices  6.04 us (5%)
    all_to_all x1, blocking collectives, shards(): parts = lax.all_to_all(partial, PLANE, 0, 0, tiled=True)  33.7 us
    all_gather x1, blocking collectives, shards(): mine = lax.all_gather(piece, 'zh', axis=0)  24.5 us
    ppermute x3, starting transfers between devices, shards(): after, before, across = [lax.ppermute(mine, Z, way) for way in ways]  13.3 us
    all_to_all x1, blocking collectives, shards(): sums = lax.all_to_all(sums, TENSOR, 0, 0, tiled=True)  8.33 us
    ppermute x3, waiting for transfers between devices, shards(): after, before, across = [lax.ppermute(mine, Z, way) for way in ways]  5.08 us
    all_to_all x1, starting transfers between devices, shards(): lax.all_to_all(copies, 'x', 0, 0, tiled=True).reshape(4 * length, features)  4.99 us
    all_to_all x1, starting transfers between devices, shards(): shared = lax.all_to_all(shared, 'y', 0, 0, tiled=True)  4.19 us
    pallas_call x2, Pallas kernels, partial_sums(): pl.pallas_call(functools.partial(half_kernel, own), out_shape=sums if own...  4.11 us
  transfers between devices with their start and end apart: 6, of which 2 were waited for; matrix products, arithmetic and copies ran while one was open for 0% of the time, Pallas kernels for 2%

profile of v4, /device:TPU:1, one launch (start us, length us, event | category | flops | bytes accessed | tf_op | source)
XLA Modules:
  0.0 113.6 jit_solution(11273984217675060213)
XLA Ops:
  0.6 2.9 %prepare.1 = (bf16[4,384,512]{2,1,0:T(8,128)(2,1)}, bf16[272,128]{1,0:T(8,128)(2,1)}, bf16[4,288,512]{2,1,0:T(8,128)(2,1)}) custom-call(bf16[384,512]{1,0:T(8,128)(2,1)} %bitcast.19, bf16[384,512]{1,0:T(8,128)(2,1)} %bitcast.20, bf16[384,512]{1,0:T(8,128)(2,1)} %bitcast.21, f32[1,512]{1,0:T(1,128)} %bitcast.25, bf16[64,512]{1,0:T(8,128)(2,1)} %bitcast.22, ...), custom_call_target="tpu_custom_call" | custom-call | flops 25165824 | bytes 5242880 | tf_op jit(solution)/shard_map/prepare/pallas_call | solution.py:225
  3.5 0.0 copy-start
  3.5 5.0 %all-to-all-start = ((bf16[4,384,512]{2,1,0:T(8,128)(2,1)}), bf16[4,384,512]{2,1,0:T(8,128)(2,1)S(1)}, u32[]{:S(2)}, u32[]{:S(2)}) async-start(bf16[4,384,512]{2,1,0:T(8,128)(2,1)} %get-tuple-element.17), calls=%async_computation | async-start | bytes 3145728 | tf_op jit(solution)/shard_map/gather_tokens/all_to_all | solution.py:251
  8.5 0.0 copy-done
  8.5 24.5 %all-gather = bf16[1088,128]{1,0:T(8,128)(2,1)S(1)} all-gather(bf16[272,128]{1,0:T(8,128)(2,1)S(1)} %copy-done), channel_id=2, replica_groups=mesh['zh'=4,'zl'=4,'x'=4,'y'=4,'core'=2] {'zh'}, dimensions={0}, use_global_device_ids=true | all-gather | bytes 348160 | tf_op jit(solution)/shard_map/gather_weight/all_gather | solution.py:253
  33.0 0.0 all-to-all-done
  33.0 4.2 %all-to-all-start.1 = ((bf16[4,288,512]{2,1,0:T(8,128)(2,1)}), bf16[4,288,512]{2,1,0:T(8,128)(2,1)S(1)}, u32[]{:S(2)}, u32[]{:S(2)}) async-start(bf16[4,288,512]{2,1,0:T(8,128)(2,1)} %get-tuple-element.19), calls=%async_computation.1 | async-start | bytes 2359296 | tf_op jit(solution)/shard_map/share_tokens/all_to_all | solution.py:259
  37.2 6.8 %collective-permute-start.2 = (bf16[4,272,128]{2,1,0:T(8,128)(2,1)S(1)}, bf16[4,272,128]{2,1,0:T(8,128)(2,1)S(1)}, u32[]{:S(2)}, u32[]{:S(2)}) collective-permute-start(bf16[4,272,128]{2,1,0:T(8,128)(2,1)S(1)} %bitcast.13), channel_id=1, source_target_pairs={{64,0},{480,32},{128,64},{32,96},{192,128},{96,160},{256,192},{160... | collective-permute-start | bytes 835592 | tf_op jit(solution)/shard_map/gather_weight/ppermute | solution.py:256
  44.0 1.9 %collective-permute-start.1 = (bf16[4,272,128]{2,1,0:T(8,128)(2,1)S(1)}, bf16[4,272,128]{2,1,0:T(8,128)(2,1)}, u32[]{:S(2)}, u32[]{:S(2)}) collective-permute-start(bf16[4,272,128]{2,1,0:T(8,128)(2,1)S(1)} %bitcast.14), channel_id=1, source_target_pairs={{480,0},{0,32},{32,64},{64,96},{96,128},{128,160},{160,192},{192,2... | collective-permute-start | bytes 835592 | tf_op jit(solution)/shard_map/gather_weight/ppermute | solution.py:256
  46.0 4.6 %collective-permute-start = (bf16[4,272,128]{2,1,0:T(8,128)(2,1)S(1)}, bf16[4,272,128]{2,1,0:T(8,128)(2,1)}, u32[]{:S(2)}, u32[]{:S(2)}) collective-permute-start(bf16[4,272,128]{2,1,0:T(8,128)(2,1)S(1)} %bitcast.15), channel_id=1, source_target_pairs={{32,0},{64,32},{96,64},{128,96},{160,128},{192,160},{224,192},{256... | collective-permute-start | bytes 835592 | tf_op jit(solution)/shard_map/gather_weight/ppermute | solution.py:256
  50.6 0.0 all-to-all-done.1.shared
  50.6 0.0 collective-permute-done.2.w2
  50.6 5.1 %collective-permute-done.1.w3 = bf16[4,272,128]{2,1,0:T(8,128)(2,1)} collective-permute-done((bf16[4,272,128]{2,1,0:T(8,128)(2,1)S(1)}, bf16[4,272,128]{2,1,0:T(8,128)(2,1)}, u32[]{:S(2)}, u32[]{:S(2)}) %collective-permute-start.1) | collective-permute-done | bytes 278560 | tf_op jit(solution)/shard_map/gather_weight/ppermute | solution.py:256
  55.6 0.0 collective-permute-done.w1
  55.6 2.1 %other_half.1 = (bf16[1536,512]{1,0:T(8,128)(2,1)S(1)}, bf16[32,512]{1,0:T(8,128)(2,1)S(1)}) custom-call(bf16[1536,512]{1,0:T(8,128)(2,1)S(1)} %bitcast.11, bf16[4,272,128]{2,1,0:T(8,128)(2,1)S(1)} %bitcast.16, bf16[4,272,128]{2,1,0:T(8,128)(2,1)} %collective-permute-done.w1, bf16[4,272,128]{2,1,0:T(8,128)(2,1)} %collective-permute-done.1.w3, ...), custom_call_target="tpu_custom_call" | custom-call | bytes 1024 | tf_op jit(solution)/shard_map/other_half/pallas_call | solution.py:266
  57.7 3.8 %collective-permute-start.3 = (bf16[1536,512]{1,0:T(8,128)(2,1)S(1)}, bf16[1536,512]{1,0:T(8,128)(2,1)S(1)}, u32[]{:S(2)}, u32[]{:S(2)}) collective-permute-start(bf16[1536,512]{1,0:T(8,128)(2,1)S(1)} %get-tuple-element.23), channel_id=1, source_target_pairs={{1,0},{0,1},{3,2},{2,3},{5,4},{4,5},{7,6},{6,7},{9,8},{8,9},{11,10... | collective-permute-start | bytes 4718600 | tf_op jit(solution)/shard_map/other_half/ppermute | solution.py:277
  61.6 2.1 %own_half.2.first = bf16[1536,512]{1,0:T(8,128)(2,1)S(1)} custom-call(bf16[1536,512]{1,0:T(8,128)(2,1)S(1)} %bitcast.12, bf16[4,272,128]{2,1,0:T(8,128)(2,1)S(1)} %bitcast.17, bf16[4,272,128]{2,1,0:T(8,128)(2,1)} %collective-permute-done.w1, bf16[4,272,128]{2,1,0:T(8,128)(2,1)} %collective-permute-done.1.w3, bf16[4,272,128]{2,1,0:T(8,128)(2,1)S(1)} %collective-permute-done.2.w2), custom_call_target="tpu_custom_call" | custom-call | bytes 1024 | tf_op jit(solution)/shard_map/own_half/pallas_call | solution.py:266
  63.6 1.0 collective-permute-done.3.second
  64.6 0.4 own_half.3
  64.9 33.7 %all_to_all.20.parts = bf16[16,128,512]{2,1,0:T(8,128)(2,1)S(1)} all-to-all(bf16[16,128,512]{2,1,0:T(8,128)(2,1)S(1)} %own_half.3), channel_id=1, replica_groups=mesh['zh'=4,'zl'=4,'x'=4,'y'=4,'core'=2] {'x','y'}, dimensions={0} | all-to-all | bytes 4194304 | tf_op jit(solution)/shard_map/exchange_parts/all_to_all | solution.py:288
  98.6 1.1 token_sums.1
  99.7 3.7 %all-gather.1 = f32[96,512]{1,0:T(8,128)S(1)} all-gather(f32[48,512]{1,0:T(8,128)S(1)} %token_sums.1), channel_id=3, replica_groups=mesh['zh'=4,'zl'=4,'x'=4,'y'=4,'core'=2] {'core'}, dimensions={0}, use_global_device_ids=true | all-gather | bytes 294912 | tf_op jit(solution)/shard_map/token_sums/all_gather | solution.py:298
  103.4 1.2 %gram.1 = f32[8,40,128]{2,1,0:T(8,128)S(1)} custom-call(f32[2,48,512]{2,1,0:T(8,128)S(1)} %bitcast.18, bf16[16,128,512]{2,1,0:T(8,128)(2,1)S(1)} %all_to_all.20.parts), custom_call_target="tpu_custom_call" | custom-call | flops 4194304 | bytes 1048576 | tf_op jit(solution)/shard_map/gram/pallas_call | solution.py:300
  104.6 8.3 %all_to_all.21.sums = f32[8,40,128]{2,1,0:T(8,128)S(1)} all-to-all(f32[8,40,128]{2,1,0:T(8,128)S(1)} %gram.1), channel_id=1, replica_groups=mesh['zh'=4,'zl'=4,'x'=4,'y'=4,'core'=2] {'y','core'}, dimensions={0} | all-to-all | bytes 327680 | tf_op jit(solution)/shard_map/gram/all_to_all | solution.py:309
  112.9 0.7 scores.1
Async XLA Ops:
  3.5 5.0 %copy-start = (bf16[272,128]{1,0:T(8,128)(2,1)S(1)}, bf16[272,128]{1,0:T(8,128)(2,1)}, u32[]{:S(2)}) copy-start(bf16[272,128]{1,0:T(8,128)(2,1)} %get-tuple-element.16) | copy-start | bytes 208900
  3.5 29.5 %all-to-all-start = ((bf16[4,384,512]{2,1,0:T(8,128)(2,1)}), bf16[4,384,512]{2,1,0:T(8,128)(2,1)S(1)}, u32[]{:S(2)}, u32[]{:S(2)}) async-start(bf16[4,384,512]{2,1,0:T(8,128)(2,1)} %get-tuple-element.17), calls=%async_computation | async-start | bytes 3145728 | tf_op jit(solution)/shard_map/gather_tokens/all_to_all | solution.py:251
  33.0 17.6 %all-to-all-start.1 = ((bf16[4,288,512]{2,1,0:T(8,128)(2,1)}), bf16[4,288,512]{2,1,0:T(8,128)(2,1)S(1)}, u32[]{:S(2)}, u32[]{:S(2)}) async-start(bf16[4,288,512]{2,1,0:T(8,128)(2,1)} %get-tuple-element.19), calls=%async_computation.1 | async-start | bytes 2359296 | tf_op jit(solution)/shard_map/share_tokens/all_to_all | solution.py:259
  37.2 13.4 %collective-permute-start.2 = (bf16[4,272,128]{2,1,0:T(8,128)(2,1)S(1)}, bf16[4,272,128]{2,1,0:T(8,128)(2,1)S(1)}, u32[]{:S(2)}, u32[]{:S(2)}) collective-permute-start(bf16[4,272,128]{2,1,0:T(8,128)(2,1)S(1)} %bitcast.13), channel_id=1, source_target_pairs={{64,0},{480,32},{128,64},{32,96},{192,128},{96,160},{256,192},{160... | collective-permute-start | bytes 835592 | tf_op jit(solution)/shard_map/gather_weight/ppermute | solution.py:256
  44.0 11.6 %collective-permute-start.1 = (bf16[4,272,128]{2,1,0:T(8,128)(2,1)S(1)}, bf16[4,272,128]{2,1,0:T(8,128)(2,1)}, u32[]{:S(2)}, u32[]{:S(2)}) collective-permute-start(bf16[4,272,128]{2,1,0:T(8,128)(2,1)S(1)} %bitcast.14), channel_id=1, source_target_pairs={{480,0},{0,32},{32,64},{64,96},{96,128},{128,160},{160,192},{192,2... | collective-permute-start | bytes 835592 | tf_op jit(solution)/shard_map/gather_weight/ppermute | solution.py:256
  46.0 9.7 %collective-permute-start = (bf16[4,272,128]{2,1,0:T(8,128)(2,1)S(1)}, bf16[4,272,128]{2,1,0:T(8,128)(2,1)}, u32[]{:S(2)}, u32[]{:S(2)}) collective-permute-start(bf16[4,272,128]{2,1,0:T(8,128)(2,1)S(1)} %bitcast.15), channel_id=1, source_target_pairs={{32,0},{64,32},{96,64},{128,96},{160,128},{192,160},{224,192},{256... | collective-permute-start | bytes 835592 | tf_op jit(solution)/shard_map/gather_weight/ppermute | solution.py:256
  57.7 6.9 %collective-permute-start.3 = (bf16[1536,512]{1,0:T(8,128)(2,1)S(1)}, bf16[1536,512]{1,0:T(8,128)(2,1)S(1)}, u32[]{:S(2)}, u32[]{:S(2)}) collective-permute-start(bf16[1536,512]{1,0:T(8,128)(2,1)S(1)} %get-tuple-element.23), channel_id=1, source_target_pairs={{1,0},{0,1},{3,2},{2,3},{5,4},{4,5},{7,6},{6,7},{9,8},{8,9},{11,10... | collective-permute-start | bytes 4718600 | tf_op jit(solution)/shard_map/other_half/ppermute | solution.py:277

commit v5 on v4

--- a/solution.py
+++ b/solution.py
@@ -67,8 +67,8 @@
     first = (lax.axis_index("y") * 2 + lax.axis_index("core")) * 512
     rows = [query_here[:, pl.ds(pl.multiple_of(first + j * 128, 128), 128)] for j in range(4)]
     high, low, _ = split3(jnp.concatenate(rows, axis=0))
-    rows = [high.astype(jnp.float32), low.astype(jnp.float32), jnp.zeros((8, 128), jnp.float32)]
-    piece_here[256:272, :] = jnp.concatenate(rows, axis=0).astype(jnp.bfloat16)
+    rows = [high.astype(jnp.float32), low.astype(jnp.float32)]
+    piece_here[256:264, :] = jnp.concatenate(rows, axis=0).astype(jnp.bfloat16)
     stores[4].start()
     loads[3].wait()
     loads[4].wait()
@@ -89,34 +89,32 @@
         copy.wait()
 
 
-def product(tokens, first, second, pair):
-    strips = []
-    for zh in (2 * pair, 2 * pair + 1):
-        for ref in (first, second):
-            blocks = [ref[zh, 64 * at : 64 * at + 64, :] for at in range(4)]
-            strips.append(jnp.concatenate(blocks, axis=1))
-    rows = jnp.concatenate(strips, axis=0)
-    return lax.dot_general(tokens[...], rows, NT, preferred_element_type=jnp.float32)
-
-
-def half_kernel(mine, tokens, w0, w1, w3, w2, out, *queries):
-    weights = (w0, w1, w2, w3)
+def half_kernel(mine, tokens, w0, w1, w3, w2, out, *rest):
+    *queries, weights, sems = rest
     half = lax.axis_index("core") if mine else 1 - lax.axis_index("core")
-    slot = lax.rem(2 * half - lax.axis_index("zl") + 4, 4)
-    for at in range(4):
-
-        @pl.when(slot == at)
-        def _():
-            for pair in range(2):
-                total = product(tokens, weights[at], weights[(at + 1) % 4], pair)
-                out[:, 256 * pair : 256 * pair + 256] = total.astype(jnp.bfloat16)
-
+    copies = []
+    for at, ref in enumerate((w0, w1, w2, w3)):
+        to = weights.at[lax.rem(lax.axis_index("zl") + at, 4)]
+        copies.append(pltpu.make_async_copy(ref, to, sems.at[at]))
+    for copy in copies:
+        copy.start()
+    for copy in copies:
+        copy.wait()
+    for pair in range(2):
+        strips = []
+        for zh in (2 * pair, 2 * pair + 1):
+            for k in range(2):
+                blocks = [weights[2 * half + k, zh, 64 * at : 64 * at + 64, :] for at in range(4)]
+                strips.append(jnp.concatenate(blocks, axis=1))
+        rows = jnp.concatenate(strips, axis=0)
+        total = lax.dot_general(tokens[...], rows, NT, preferred_element_type=jnp.float32)
+        out[:, 256 * pair : 256 * pair + 256] = total.astype(jnp.bfloat16)
     for ref in queries:
-        slots = []
-        for weight in weights:
-            rows = [weight[zh, 256:272, :].astype(jnp.float32)[0:8] for zh in range(4)]
-            slots.append(jnp.concatenate(rows, axis=0))
-        ref[...] = jnp.concatenate(slots, axis=1).astype(jnp.bfloat16)
+        columns = []
+        for zl in range(4):
+            rows = [weights[zl, zh, 256:264, :].astype(jnp.float32) for zh in range(4)]
+            columns.append(jnp.concatenate(rows, axis=0))
+        ref[...] = jnp.concatenate(columns, axis=1).astype(jnp.bfloat16)
 
 
 def add_kernel(first, second, queries, out):
@@ -171,7 +169,7 @@
     gram = lax.dot_general(in_proj, out_proj, TN, precision=HIGHEST, preferred_element_type=jnp.float32)
     gram = gram / math.sqrt(length)
     packed[...] = jnp.concatenate([gram[0:32], gram[32:64]], axis=1)
-    zl, core = lax.axis_index("zl"), lax.axis_index("core")
+    core = lax.axis_index("core")
     factors = []
     for y in range(4):
         halves = [packed[8 * y + 4 * at : 8 * y + 4 * at + 4, :] for at in range(2)]
@@ -190,20 +188,25 @@
     flat = lax.dot_general(ones, every, NT, precision=HIGHEST, preferred_element_type=jnp.float32)
     row = lax.broadcasted_iota(jnp.int32, (512, 128), 0) // 8
     column = lax.broadcasted_iota(jnp.int32, (512, 128), 1)
-    chosen = ((row % 4) * 16 + (row // 4 + zl) % 4 * 4 + row // 16 == column).astype(jnp.float32)
+    chosen = ((row % 4) * 16 + (row // 4) % 4 * 4 + row // 16 == column).astype(jnp.float32)
     result = jnp.dot(flat, chosen, precision=HIGHEST, preferred_element_type=jnp.float32)
+    half = packed[pl.ds(pl.multiple_of(16 * core, 16), 16), :]
     for at in range(8):
-        out[at, 0:32, :] = packed[...]
-        out[at, 32:40, :] = result
+        out[at, 0:16, :] = half
+        out[at, 16:24, :] = result
 
 
 def final_kernel(sums, grads, scores):
-    total = sums[0, 0:32, :] + sums[2, 0:32, :] + sums[4, 0:32, :] + sums[6, 0:32, :]
+    halves = []
+    for core in range(2):
+        four = [sums[2 * y + core, 0:16, :] for y in range(4)]
+        halves.append(four[0] + four[1] + four[2] + four[3])
+    total = jnp.concatenate(halves, axis=0)
     grads[pl.ds(0, 32, stride=2), :] = total[:, 0:64]
     grads[pl.ds(1, 32, stride=2), :] = total[:, 64:128]
-    result = sums[0, 32:40, :]
+    result = sums[0, 16:24, :]
     for at in range(1, 8):
-        result = result + sums[at, 32:40, :]
+        result = result + sums[at, 16:24, :]
     scores[...] = result[0:1, 0:64] / 64.0
 
 
@@ -226,7 +229,7 @@
             prepare_kernel,
             out_shape=(
                 jax.ShapeDtypeStruct((4, length, features), bf16),
-                jax.ShapeDtypeStruct((272, 128), bf16),
+                jax.ShapeDtypeStruct((264, 128), bf16),
                 jax.ShapeDtypeStruct((4, 288, 512), bf16),
             ),
             in_specs=[ANY] * 8,
@@ -237,7 +240,7 @@
                 pltpu.VMEM((64, 512), bf16),
                 pltpu.VMEM((1, 4096), f32),
                 pltpu.VMEM((64, 512), bf16),
-                pltpu.VMEM((272, 128), bf16),
+                pltpu.VMEM((264, 128), bf16),
                 pltpu.VMEM((4, 288, 512), bf16),
                 pltpu.SemaphoreType.DMA((26,)),
             ],
@@ -266,8 +269,9 @@
         return pl.pallas_call(
             functools.partial(half_kernel, own),
             out_shape=sums if own else (sums, query),
-            in_specs=[VMEM] * 5,
+            in_specs=[VMEM] + [ANY] * 4,
             out_specs=VMEM if own else (VMEM, VMEM),
+            scratch_shapes=[pltpu.VMEM((4, 4, 264, 128), bf16), pltpu.SemaphoreType.DMA((4,))],
             compiler_params=PARAMS,
             cost_estimate=cost(0, 1 << 10),
         )(every, mine, after, before, across)
@@ -299,7 +303,7 @@
     with jax.named_scope("gram"):
         sums = pl.pallas_call(
             functools.partial(gram_kernel, length, width),
-            out_shape=jax.ShapeDtypeStruct((8, 40, 128), f32),
+            out_shape=jax.ShapeDtypeStruct((8, 24, 128), f32),
             in_specs=[VMEM] * 2,
             out_specs=VMEM,
             scratch_shapes=[pltpu.VMEM((32, 128), f32)],

time: 114 us -> 113 us (level)
  blocking collectives: 70.2 us -> 68.8 us
where the time goes in v5:
time: 113 us; the launch traced here: 112 us
  blocking collectives  68.8 us (61%)
  starting transfers between devices  26.7 us (24%)
  Pallas kernels  10.4 us (9%)
  waiting for transfers between devices  5.59 us (5%)
    all_to_all x1, blocking collectives, shards(): parts = lax.all_to_all(partial, PLANE, 0, 0, tiled=True)  33 us
    all_gather x1, blocking collectives, shards(): mine = lax.all_gather(piece, 'zh', axis=0)  24.4 us
    ppermute x3, starting transfers between devices, shards(): after, before, across = [lax.ppermute(mine, Z, way) for way in ways]  13.5 us
    all_to_all x1, blocking collectives, shards(): sums = lax.all_to_all(sums, TENSOR, 0, 0, tiled=True)  7.72 us
    all_to_all x1, starting transfers between devices, shards(): lax.all_to_all(copies, 'x', 0, 0, tiled=True).reshape(4 * length, features)  4.99 us
    ppermute x3, waiting for transfers between devices, shards(): after, before, across = [lax.ppermute(mine, Z, way) for way in ways]  4.73 us
    pallas_call x2, Pallas kernels, partial_sums(): pl.pallas_call(functools.partial(half_kernel, own), out_shape=sums if own...  4.26 us
    all_to_all x1, starting transfers between devices, shards(): shared = lax.all_to_all(shared, 'y', 0, 0, tiled=True)  4.19 us
  transfers between devices with their start and end apart: 6, of which 2 were waited for; matrix products, arithmetic and copies ran while one was open for 0% of the time, Pallas kernels for 2%

profile of v5, /device:TPU:1, one launch (start us, length us, event | category | flops | bytes accessed | tf_op | source)
XLA Modules:
  0.0 112.2 jit_solution(7830818408957646124)
XLA Ops:
  0.6 2.8 %prepare.1 = (bf16[4,384,512]{2,1,0:T(8,128)(2,1)}, bf16[264,128]{1,0:T(8,128)(2,1)}, bf16[4,288,512]{2,1,0:T(8,128)(2,1)}) custom-call(bf16[384,512]{1,0:T(8,128)(2,1)} %bitcast.19, bf16[384,512]{1,0:T(8,128)(2,1)} %bitcast.20, bf16[384,512]{1,0:T(8,128)(2,1)} %bitcast.21, f32[1,512]{1,0:T(1,128)} %bitcast.25, bf16[64,512]{1,0:T(8,128)(2,1)} %bitcast.22, ...), custom_call_target="tpu_custom_call" | custom-call | flops 25165824 | bytes 5242880 | tf_op jit(solution)/shard_map/prepare/pallas_call | solution.py:228
  3.5 0.0 copy-start
  3.5 5.0 %all-to-all-start = ((bf16[4,384,512]{2,1,0:T(8,128)(2,1)}), bf16[4,384,512]{2,1,0:T(8,128)(2,1)S(1)}, u32[]{:S(2)}, u32[]{:S(2)}) async-start(bf16[4,384,512]{2,1,0:T(8,128)(2,1)} %get-tuple-element.17), calls=%async_computation | async-start | bytes 3145728 | tf_op jit(solution)/shard_map/gather_tokens/all_to_all | solution.py:254
  8.5 0.0 copy-done
  8.5 24.4 %all-gather = bf16[1056,128]{1,0:T(8,128)(2,1)S(1)} all-gather(bf16[264,128]{1,0:T(8,128)(2,1)S(1)} %copy-done), channel_id=2, replica_groups=mesh['zh'=4,'zl'=4,'x'=4,'y'=4,'core'=2] {'zh'}, dimensions={0}, use_global_device_ids=true | all-gather | bytes 337920 | tf_op jit(solution)/shard_map/gather_weight/all_gather | solution.py:256
  32.8 0.0 all-to-all-done
  32.8 4.2 %all-to-all-start.1 = ((bf16[4,288,512]{2,1,0:T(8,128)(2,1)}), bf16[4,288,512]{2,1,0:T(8,128)(2,1)S(1)}, u32[]{:S(2)}, u32[]{:S(2)}) async-start(bf16[4,288,512]{2,1,0:T(8,128)(2,1)} %get-tuple-element.19), calls=%async_computation.1 | async-start | bytes 2359296 | tf_op jit(solution)/shard_map/share_tokens/all_to_all | solution.py:262
  37.0 7.0 %collective-permute-start.2 = (bf16[4,264,128]{2,1,0:T(8,128)(2,1)S(1)}, bf16[4,264,128]{2,1,0:T(8,128)(2,1)S(1)}, u32[]{:S(2)}, u32[]{:S(2)}) collective-permute-start(bf16[4,264,128]{2,1,0:T(8,128)(2,1)S(1)} %bitcast.13), channel_id=1, source_target_pairs={{64,0},{480,32},{128,64},{32,96},{192,128},{96,160},{256,192},{160... | collective-permute-start | bytes 811016 | tf_op jit(solution)/shard_map/gather_weight/ppermute | solution.py:259
  44.0 1.9 %collective-permute-start.1 = (bf16[4,264,128]{2,1,0:T(8,128)(2,1)S(1)}, bf16[4,264,128]{2,1,0:T(8,128)(2,1)}, u32[]{:S(2)}, u32[]{:S(2)}) collective-permute-start(bf16[4,264,128]{2,1,0:T(8,128)(2,1)S(1)} %bitcast.14), channel_id=1, source_target_pairs={{480,0},{0,32},{32,64},{64,96},{96,128},{128,160},{160,192},{192,2... | collective-permute-start | bytes 811016 | tf_op jit(solution)/shard_map/gather_weight/ppermute | solution.py:259
  46.0 4.6 %collective-permute-start = (bf16[4,264,128]{2,1,0:T(8,128)(2,1)S(1)}, bf16[4,264,128]{2,1,0:T(8,128)(2,1)}, u32[]{:S(2)}, u32[]{:S(2)}) collective-permute-start(bf16[4,264,128]{2,1,0:T(8,128)(2,1)S(1)} %bitcast.15), channel_id=1, source_target_pairs={{32,0},{64,32},{96,64},{128,96},{160,128},{192,160},{224,192},{256... | collective-permute-start | bytes 811016 | tf_op jit(solution)/shard_map/gather_weight/ppermute | solution.py:259
  50.5 0.0 all-to-all-done.1.shared
  50.5 0.0 collective-permute-done.2.w2
  50.6 4.7 %collective-permute-done.1.w3 = bf16[4,264,128]{2,1,0:T(8,128)(2,1)} collective-permute-done((bf16[4,264,128]{2,1,0:T(8,128)(2,1)S(1)}, bf16[4,264,128]{2,1,0:T(8,128)(2,1)}, u32[]{:S(2)}, u32[]{:S(2)}) %collective-permute-start.1) | collective-permute-done | bytes 270368 | tf_op jit(solution)/shard_map/gather_weight/ppermute | solution.py:259
  55.3 0.0 collective-permute-done.w1
  55.3 2.1 %other_half.1 = (bf16[1536,512]{1,0:T(8,128)(2,1)S(1)}, bf16[32,512]{1,0:T(8,128)(2,1)S(1)}) custom-call(bf16[1536,512]{1,0:T(8,128)(2,1)S(1)} %bitcast.11, bf16[4,264,128]{2,1,0:T(8,128)(2,1)S(1)} %bitcast.16, bf16[4,264,128]{2,1,0:T(8,128)(2,1)} %collective-permute-done.w1, bf16[4,264,128]{2,1,0:T(8,128)(2,1)} %collective-permute-done.1.w3, ...), custom_call_target="tpu_custom_call" | custom-call | bytes 1024 | tf_op jit(solution)/shard_map/other_half/pallas_call | solution.py:269
  57.4 4.1 %collective-permute-start.3 = (bf16[1536,512]{1,0:T(8,128)(2,1)S(1)}, bf16[1536,512]{1,0:T(8,128)(2,1)S(1)}, u32[]{:S(2)}, u32[]{:S(2)}) collective-permute-start(bf16[1536,512]{1,0:T(8,128)(2,1)S(1)} %get-tuple-element.23), channel_id=1, source_target_pairs={{1,0},{0,1},{3,2},{2,3},{5,4},{4,5},{7,6},{6,7},{9,8},{8,9},{11,10... | collective-permute-start | bytes 4718600 | tf_op jit(solution)/shard_map/other_half/ppermute | solution.py:281
  61.5 2.1 %own_half.2.first = bf16[1536,512]{1,0:T(8,128)(2,1)S(1)} custom-call(bf16[1536,512]{1,0:T(8,128)(2,1)S(1)} %bitcast.12, bf16[4,264,128]{2,1,0:T(8,128)(2,1)S(1)} %bitcast.17, bf16[4,264,128]{2,1,0:T(8,128)(2,1)} %collective-permute-done.w1, bf16[4,264,128]{2,1,0:T(8,128)(2,1)} %collective-permute-done.1.w3, bf16[4,264,128]{2,1,0:T(8,128)(2,1)S(1)} %collective-permute-done.2.w2), custom_call_target="tpu_custom_call" | custom-call | bytes 1024 | tf_op jit(solution)/shard_map/own_half/pallas_call | solution.py:269
  63.7 0.9 collective-permute-done.3.second
  64.5 0.4 own_half.3
  64.9 33.0 %all_to_all.20.parts = bf16[16,128,512]{2,1,0:T(8,128)(2,1)S(1)} all-to-all(bf16[16,128,512]{2,1,0:T(8,128)(2,1)S(1)} %own_half.3), channel_id=1, replica_groups=mesh['zh'=4,'zl'=4,'x'=4,'y'=4,'core'=2] {'x','y'}, dimensions={0} | all-to-all | bytes 4194304 | tf_op jit(solution)/shard_map/exchange_parts/all_to_all | solution.py:292
  97.9 1.1 token_sums.1
  99.0 3.7 %all-gather.1 = f32[96,512]{1,0:T(8,128)S(1)} all-gather(f32[48,512]{1,0:T(8,128)S(1)} %token_sums.1), channel_id=3, replica_groups=mesh['zh'=4,'zl'=4,'x'=4,'y'=4,'core'=2] {'core'}, dimensions={0}, use_global_device_ids=true | all-gather | bytes 294912 | tf_op jit(solution)/shard_map/token_sums/all_gather | solution.py:302
  102.7 1.1 %gram.1 = f32[8,24,128]{2,1,0:T(8,128)S(1)} custom-call(f32[2,48,512]{2,1,0:T(8,128)S(1)} %bitcast.18, bf16[16,128,512]{2,1,0:T(8,128)(2,1)S(1)} %all_to_all.20.parts), custom_call_target="tpu_custom_call" | custom-call | flops 4194304 | bytes 1048576 | tf_op jit(solution)/shard_map/gram/pallas_call | solution.py:304
  103.8 7.7 %all_to_all.21.sums = f32[8,24,128]{2,1,0:T(8,128)S(1)} all-to-all(f32[8,24,128]{2,1,0:T(8,128)S(1)} %gram.1), channel_id=1, replica_groups=mesh['zh'=4,'zl'=4,'x'=4,'y'=4,'core'=2] {'y','core'}, dimensions={0} | all-to-all | bytes 196608 | tf_op jit(solution)/shard_map/gram/all_to_all | solution.py:313
  111.5 0.7 scores.1
Async XLA Ops:
  3.5 5.0 %copy-start = (bf16[264,128]{1,0:T(8,128)(2,1)S(1)}, bf16[264,128]{1,0:T(8,128)(2,1)}, u32[]{:S(2)}) copy-start(bf16[264,128]{1,0:T(8,128)(2,1)} %get-tuple-element.16) | copy-start | bytes 202756
  3.5 29.4 %all-to-all-start = ((bf16[4,384,512]{2,1,0:T(8,128)(2,1)}), bf16[4,384,512]{2,1,0:T(8,128)(2,1)S(1)}, u32[]{:S(2)}, u32[]{:S(2)}) async-start(bf16[4,384,512]{2,1,0:T(8,128)(2,1)} %get-tuple-element.17), calls=%async_computation | async-start | bytes 3145728 | tf_op jit(solution)/shard_map/gather_tokens/all_to_all | solution.py:254
  32.8 17.7 %all-to-all-start.1 = ((bf16[4,288,512]{2,1,0:T(8,128)(2,1)}), bf16[4,288,512]{2,1,0:T(8,128)(2,1)S(1)}, u32[]{:S(2)}, u32[]{:S(2)}) async-start(bf16[4,288,512]{2,1,0:T(8,128)(2,1)} %get-tuple-element.19), calls=%async_computation.1 | async-start | bytes 2359296 | tf_op jit(solution)/shard_map/share_tokens/all_to_all | solution.py:262
  37.0 13.5 %collective-permute-start.2 = (bf16[4,264,128]{2,1,0:T(8,128)(2,1)S(1)}, bf16[4,264,128]{2,1,0:T(8,128)(2,1)S(1)}, u32[]{:S(2)}, u32[]{:S(2)}) collective-permute-start(bf16[4,264,128]{2,1,0:T(8,128)(2,1)S(1)} %bitcast.13), channel_id=1, source_target_pairs={{64,0},{480,32},{128,64},{32,96},{192,128},{96,160},{256,192},{160... | collective-permute-start | bytes 811016 | tf_op jit(solution)/shard_map/gather_weight/ppermute | solution.py:259
  44.0 11.3 %collective-permute-start.1 = (bf16[4,264,128]{2,1,0:T(8,128)(2,1)S(1)}, bf16[4,264,128]{2,1,0:T(8,128)(2,1)}, u32[]{:S(2)}, u32[]{:S(2)}) collective-permute-start(bf16[4,264,128]{2,1,0:T(8,128)(2,1)S(1)} %bitcast.14), channel_id=1, source_target_pairs={{480,0},{0,32},{32,64},{64,96},{96,128},{128,160},{160,192},{192,2... | collective-permute-start | bytes 811016 | tf_op jit(solution)/shard_map/gather_weight/ppermute | solution.py:259
  46.0 9.3 %collective-permute-start = (bf16[4,264,128]{2,1,0:T(8,128)(2,1)S(1)}, bf16[4,264,128]{2,1,0:T(8,128)(2,1)}, u32[]{:S(2)}, u32[]{:S(2)}) collective-permute-start(bf16[4,264,128]{2,1,0:T(8,128)(2,1)S(1)} %bitcast.15), channel_id=1, source_target_pairs={{32,0},{64,32},{96,64},{128,96},{160,128},{192,160},{224,192},{256... | collective-permute-start | bytes 811016 | tf_op jit(solution)/shard_map/gather_weight/ppermute | solution.py:259
  57.4 7.1 %collective-permute-start.3 = (bf16[1536,512]{1,0:T(8,128)(2,1)S(1)}, bf16[1536,512]{1,0:T(8,128)(2,1)S(1)}, u32[]{:S(2)}, u32[]{:S(2)}) collective-permute-start(bf16[1536,512]{1,0:T(8,128)(2,1)S(1)} %get-tuple-element.23), channel_id=1, source_target_pairs={{1,0},{0,1},{3,2},{2,3},{5,4},{4,5},{7,6},{6,7},{9,8},{8,9},{11,10... | collective-permute-start | bytes 4718600 | tf_op jit(solution)/shard_map/other_half/ppermute | solution.py:281

commit v6 on v5

--- a/solution.py
+++ b/solution.py
@@ -89,40 +89,43 @@
         copy.wait()
 
 
-def half_kernel(mine, tokens, w0, w1, w3, w2, out, *rest):
-    *queries, weights, sems = rest
+def half_kernel(mine, tokens, w0, w1, w3, w2, out, query, weights, sems):
     half = lax.axis_index("core") if mine else 1 - lax.axis_index("core")
     copies = []
     for at, ref in enumerate((w0, w1, w2, w3)):
-        to = weights.at[lax.rem(lax.axis_index("zl") + at, 4)]
-        copies.append(pltpu.make_async_copy(ref, to, sems.at[at]))
-    for copy in copies:
-        copy.start()
-    for copy in copies:
-        copy.wait()
+        zl = lax.rem(lax.axis_index("zl") + at, 4)
+        copy = pltpu.make_async_copy(ref, weights.at[lax.rem(zl, 2)], sems.at[at])
+        copies.append((lax.div(zl, 2) == half, copy))
+    for needed, copy in copies:
+        pl.when(needed)(copy.start)
+    for needed, copy in copies:
+        pl.when(needed)(copy.wait)
     for pair in range(2):
         strips = []
         for zh in (2 * pair, 2 * pair + 1):
             for k in range(2):
-                blocks = [weights[2 * half + k, zh, 64 * at : 64 * at + 64, :] for at in range(4)]
+                blocks = [weights[k, zh, 64 * at : 64 * at + 64, :] for at in range(4)]
                 strips.append(jnp.concatenate(blocks, axis=1))
         rows = jnp.concatenate(strips, axis=0)
         total = lax.dot_general(tokens[...], rows, NT, preferred_element_type=jnp.float32)
         out[:, 256 * pair : 256 * pair + 256] = total.astype(jnp.bfloat16)
-    for ref in queries:
-        columns = []
-        for zl in range(4):
-            rows = [weights[zl, zh, 256:264, :].astype(jnp.float32) for zh in range(4)]
-            columns.append(jnp.concatenate(rows, axis=0))
-        ref[...] = jnp.concatenate(columns, axis=1).astype(jnp.bfloat16)
-
-
-def add_kernel(first, second, queries, out):
+    columns = []
+    for k in range(2):
+        rows = [weights[k, zh, 256:264, :].astype(jnp.float32) for zh in range(4)]
+        columns.append(jnp.concatenate(rows, axis=0))
+    query[...] = jnp.concatenate(columns, axis=1).astype(jnp.bfloat16)
+
+
+def add_kernel(first, second, mine, theirs, out):
+    core = lax.axis_index("core")
+    low = jnp.where(core == 0, mine[...], theirs[...])
+    high = jnp.where(core == 0, theirs[...], mine[...])
+    queries = jnp.concatenate([low, high], axis=1)
     for at in range(16):
         rows = slice(96 * at, 96 * at + 96)
         total = first[rows, :].astype(jnp.float32) + second[rows, :].astype(jnp.float32)
         out[at, 0:96, :] = total.astype(jnp.bfloat16)
-        out[at, 96:128, :] = queries[...]
+        out[at, 96:128, :] = queries
 
 
 def sums_kernel(parts, shared, out):
@@ -265,29 +268,30 @@
 
     def partial_sums(own):
         sums = jax.ShapeDtypeStruct((4 * length, 512), bf16)
-        query = jax.ShapeDtypeStruct((32, 512), bf16)
+        query = jax.ShapeDtypeStruct((32, 256), bf16)
         return pl.pallas_call(
             functools.partial(half_kernel, own),
-            out_shape=sums if own else (sums, query),
+            out_shape=(sums, query),
             in_specs=[VMEM] + [ANY] * 4,
-            out_specs=VMEM if own else (VMEM, VMEM),
-            scratch_shapes=[pltpu.VMEM((4, 4, 264, 128), bf16), pltpu.SemaphoreType.DMA((4,))],
+            out_specs=(VMEM, VMEM),
+            scratch_shapes=[pltpu.VMEM((2, 4, 264, 128), bf16), pltpu.SemaphoreType.DMA((4,))],
             compiler_params=PARAMS,
             cost_estimate=cost(0, 1 << 10),
         )(every, mine, after, before, across)
 
     with jax.named_scope("other_half"):
-        other, query = partial_sums(False)
+        other, theirs = partial_sums(False)
         other = lax.ppermute(other, "core", shift(2, 1))
     with jax.named_scope("own_half"):
+        own, query = partial_sums(True)
         partial = pl.pallas_call(
             add_kernel,
             out_shape=jax.ShapeDtypeStruct((16, length // 4 + 32, 512), bf16),
-            in_specs=[VMEM] * 3,
+            in_specs=[VMEM] * 4,
             out_specs=VMEM,
             compiler_params=PARAMS,
             cost_estimate=cost(0, 1 << 10),
-        )(partial_sums(True), other, query)
+        )(own, other, query, theirs)
     with jax.named_scope("exchange_parts"):
         parts = lax.all_to_all(partial, PLANE, 0, 0, tiled=True)
     with jax.named_scope("token_sums"):

time: 113 us -> 113 us (level)
  no operation moved by 1% of the time
where the time goes in v6:
time: 113 us; the launch traced here: 112 us
  blocking collectives  68.8 us (61%)
  starting transfers between devices  26.7 us (24%)
  Pallas kernels  10.3 us (9%)
  waiting for transfers between devices  5.66 us (5%)
    all_to_all x1, blocking collectives, shards(): parts = lax.all_to_all(partial, PLANE, 0, 0, tiled=True)  33 us
    all_gather x1, blocking collectives, shards(): mine = lax.all_gather(piece, 'zh', axis=0)  24.4 us
    ppermute x3, starting transfers between devices, shards(): after, before, across = [lax.ppermute(mine, Z, way) for way in ways]  13.5 us
    all_to_all x1, blocking collectives, shards(): sums = lax.all_to_all(sums, TENSOR, 0, 0, tiled=True)  7.72 us
    all_to_all x1, starting transfers between devices, shards(): lax.all_to_all(copies, 'x', 0, 0, tiled=True).reshape(4 * length, features)  4.99 us
    ppermute x3, waiting for transfers between devices, shards(): after, before, across = [lax.ppermute(mine, Z, way) for way in ways]  4.73 us
    all_to_all x1, starting transfers between devices, shards(): shared = lax.all_to_all(shared, 'y', 0, 0, tiled=True)  4.19 us
    pallas_call x2, Pallas kernels, partial_sums(): pl.pallas_call(functools.partial(half_kernel, own), out_shape=(sums, quer...  4.11 us
  transfers between devices with their start and end apart: 6, of which 2 were waited for; matrix products, arithmetic and copies ran while one was open for 0% of the time, Pallas kernels for 2%

profile of v6, /device:TPU:1, one launch (start us, length us, event | category | flops | bytes accessed | tf_op | source)
XLA Modules:
  0.0 112.2 jit_solution(5052234698562124822)
XLA Ops:
  0.6 2.8 %prepare.1 = (bf16[4,384,512]{2,1,0:T(8,128)(2,1)}, bf16[264,128]{1,0:T(8,128)(2,1)}, bf16[4,288,512]{2,1,0:T(8,128)(2,1)}) custom-call(bf16[384,512]{1,0:T(8,128)(2,1)} %bitcast.19, bf16[384,512]{1,0:T(8,128)(2,1)} %bitcast.20, bf16[384,512]{1,0:T(8,128)(2,1)} %bitcast.21, f32[1,512]{1,0:T(1,128)} %bitcast.25, bf16[64,512]{1,0:T(8,128)(2,1)} %bitcast.22, ...), custom_call_target="tpu_custom_call" | custom-call | flops 25165824 | bytes 5242880 | tf_op jit(solution)/shard_map/prepare/pallas_call | solution.py:231
  3.5 0.0 copy-start
  3.5 5.0 %all-to-all-start = ((bf16[4,384,512]{2,1,0:T(8,128)(2,1)}), bf16[4,384,512]{2,1,0:T(8,128)(2,1)S(1)}, u32[]{:S(2)}, u32[]{:S(2)}) async-start(bf16[4,384,512]{2,1,0:T(8,128)(2,1)} %get-tuple-element.19), calls=%async_computation | async-start | bytes 3145728 | tf_op jit(solution)/shard_map/gather_tokens/all_to_all | solution.py:257
  8.5 0.0 copy-done
  8.5 24.4 %all-gather = bf16[1056,128]{1,0:T(8,128)(2,1)S(1)} all-gather(bf16[264,128]{1,0:T(8,128)(2,1)S(1)} %copy-done), channel_id=2, replica_groups=mesh['zh'=4,'zl'=4,'x'=4,'y'=4,'core'=2] {'zh'}, dimensions={0}, use_global_device_ids=true | all-gather | bytes 337920 | tf_op jit(solution)/shard_map/gather_weight/all_gather | solution.py:259
  32.9 0.0 all-to-all-done
  32.9 4.2 %all-to-all-start.1 = ((bf16[4,288,512]{2,1,0:T(8,128)(2,1)}), bf16[4,288,512]{2,1,0:T(8,128)(2,1)S(1)}, u32[]{:S(2)}, u32[]{:S(2)}) async-start(bf16[4,288,512]{2,1,0:T(8,128)(2,1)} %get-tuple-element.21), calls=%async_computation.1 | async-start | bytes 2359296 | tf_op jit(solution)/shard_map/share_tokens/all_to_all | solution.py:265
  37.0 7.0 %collective-permute-start.2 = (bf16[4,264,128]{2,1,0:T(8,128)(2,1)S(1)}, bf16[4,264,128]{2,1,0:T(8,128)(2,1)S(1)}, u32[]{:S(2)}, u32[]{:S(2)}) collective-permute-start(bf16[4,264,128]{2,1,0:T(8,128)(2,1)S(1)} %bitcast.13), channel_id=1, source_target_pairs={{64,0},{480,32},{128,64},{32,96},{192,128},{96,160},{256,192},{160... | collective-permute-start | bytes 811016 | tf_op jit(solution)/shard_map/gather_weight/ppermute | solution.py:262
  44.0 1.9 %collective-permute-start.1 = (bf16[4,264,128]{2,1,0:T(8,128)(2,1)S(1)}, bf16[4,264,128]{2,1,0:T(8,128)(2,1)}, u32[]{:S(2)}, u32[]{:S(2)}) collective-permute-start(bf16[4,264,128]{2,1,0:T(8,128)(2,1)S(1)} %bitcast.14), channel_id=1, source_target_pairs={{480,0},{0,32},{32,64},{64,96},{96,128},{128,160},{160,192},{192,2... | collective-permute-start | bytes 811016 | tf_op jit(solution)/shard_map/gather_weight/ppermute | solution.py:262
  46.0 4.6 %collective-permute-start = (bf16[4,264,128]{2,1,0:T(8,128)(2,1)S(1)}, bf16[4,264,128]{2,1,0:T(8,128)(2,1)}, u32[]{:S(2)}, u32[]{:S(2)}) collective-permute-start(bf16[4,264,128]{2,1,0:T(8,128)(2,1)S(1)} %bitcast.15), channel_id=1, source_target_pairs={{32,0},{64,32},{96,64},{128,96},{160,128},{192,160},{224,192},{256... | collective-permute-start | bytes 811016 | tf_op jit(solution)/shard_map/gather_weight/ppermute | solution.py:262
  50.5 0.0 all-to-all-done.1.shared
  50.6 0.0 collective-permute-done.2.w2
  50.6 4.7 %collective-permute-done.1.w3 = bf16[4,264,128]{2,1,0:T(8,128)(2,1)} collective-permute-done((bf16[4,264,128]{2,1,0:T(8,128)(2,1)S(1)}, bf16[4,264,128]{2,1,0:T(8,128)(2,1)}, u32[]{:S(2)}, u32[]{:S(2)}) %collective-permute-start.1) | collective-permute-done | bytes 270368 | tf_op jit(solution)/shard_map/gather_weight/ppermute | solution.py:262
  55.3 0.0 collective-permute-done.w1
  55.3 2.0 %other_half.1 = (bf16[1536,512]{1,0:T(8,128)(2,1)S(1)}, bf16[32,256]{1,0:T(8,128)(2,1)S(1)}) custom-call(bf16[1536,512]{1,0:T(8,128)(2,1)S(1)} %bitcast.11, bf16[4,264,128]{2,1,0:T(8,128)(2,1)S(1)} %bitcast.16, bf16[4,264,128]{2,1,0:T(8,128)(2,1)} %collective-permute-done.w1, bf16[4,264,128]{2,1,0:T(8,128)(2,1)} %collective-permute-done.1.w3, ...), custom_call_target="tpu_custom_call" | custom-call | bytes 1024 | tf_op jit(solution)/shard_map/other_half/pallas_call | solution.py:272
  57.3 4.1 %collective-permute-start.3 = (bf16[1536,512]{1,0:T(8,128)(2,1)S(1)}, bf16[1536,512]{1,0:T(8,128)(2,1)S(1)}, u32[]{:S(2)}, u32[]{:S(2)}) collective-permute-start(bf16[1536,512]{1,0:T(8,128)(2,1)S(1)} %get-tuple-element.26), channel_id=1, source_target_pairs={{1,0},{0,1},{3,2},{2,3},{5,4},{4,5},{7,6},{6,7},{9,8},{8,9},{11,10... | collective-permute-start | bytes 4718600 | tf_op jit(solution)/shard_map/other_half/ppermute | solution.py:284
  61.4 2.1 %own_half.2 = (bf16[1536,512]{1,0:T(8,128)(2,1)S(1)}, bf16[32,256]{1,0:T(8,128)(2,1)S(1)}) custom-call(bf16[1536,512]{1,0:T(8,128)(2,1)S(1)} %bitcast.12, bf16[4,264,128]{2,1,0:T(8,128)(2,1)S(1)} %bitcast.17, bf16[4,264,128]{2,1,0:T(8,128)(2,1)} %collective-permute-done.w1, bf16[4,264,128]{2,1,0:T(8,128)(2,1)} %collective-permute-done.1.w3, ...), custom_call_target="tpu_custom_call" | custom-call | bytes 1024 | tf_op jit(solution)/shard_map/own_half/pallas_call | solution.py:272
  63.5 0.9 collective-permute-done.3.second
  64.4 0.4 own_half.3
  64.9 33.0 %all_to_all.20.parts = bf16[16,128,512]{2,1,0:T(8,128)(2,1)S(1)} all-to-all(bf16[16,128,512]{2,1,0:T(8,128)(2,1)S(1)} %own_half.3), channel_id=1, replica_groups=mesh['zh'=4,'zl'=4,'x'=4,'y'=4,'core'=2] {'x','y'}, dimensions={0} | all-to-all | bytes 4194304 | tf_op jit(solution)/shard_map/exchange_parts/all_to_all | solution.py:296
  97.9 1.1 token_sums.1
  98.9 3.7 %all-gather.1 = f32[96,512]{1,0:T(8,128)S(1)} all-gather(f32[48,512]{1,0:T(8,128)S(1)} %token_sums.1), channel_id=3, replica_groups=mesh['zh'=4,'zl'=4,'x'=4,'y'=4,'core'=2] {'core'}, dimensions={0}, use_global_device_ids=true | all-gather | bytes 294912 | tf_op jit(solution)/shard_map/token_sums/all_gather | solution.py:306
  102.6 1.1 %gram.1 = f32[8,24,128]{2,1,0:T(8,128)S(1)} custom-call(f32[2,48,512]{2,1,0:T(8,128)S(1)} %bitcast.18, bf16[16,128,512]{2,1,0:T(8,128)(2,1)S(1)} %all_to_all.20.parts), custom_call_target="tpu_custom_call" | custom-call | flops 4194304 | bytes 1048576 | tf_op jit(solution)/shard_map/gram/pallas_call | solution.py:308
  103.8 7.7 %all_to_all.21.sums = f32[8,24,128]{2,1,0:T(8,128)S(1)} all-to-all(f32[8,24,128]{2,1,0:T(8,128)S(1)} %gram.1), channel_id=1, replica_groups=mesh['zh'=4,'zl'=4,'x'=4,'y'=4,'core'=2] {'y','core'}, dimensions={0} | all-to-all | bytes 196608 | tf_op jit(solution)/shard_map/gram/all_to_all | solution.py:317
  111.5 0.7 scores.1
Async XLA Ops:
  3.5 5.0 %copy-start = (bf16[264,128]{1,0:T(8,128)(2,1)S(1)}, bf16[264,128]{1,0:T(8,128)(2,1)}, u32[]{:S(2)}) copy-start(bf16[264,128]{1,0:T(8,128)(2,1)} %get-tuple-element.18) | copy-start | bytes 202756
  3.5 29.4 %all-to-all-start = ((bf16[4,384,512]{2,1,0:T(8,128)(2,1)}), bf16[4,384,512]{2,1,0:T(8,128)(2,1)S(1)}, u32[]{:S(2)}, u32[]{:S(2)}) async-start(bf16[4,384,512]{2,1,0:T(8,128)(2,1)} %get-tuple-element.19), calls=%async_computation | async-start | bytes 3145728 | tf_op jit(solution)/shard_map/gather_tokens/all_to_all | solution.py:257
  32.9 17.7 %all-to-all-start.1 = ((bf16[4,288,512]{2,1,0:T(8,128)(2,1)}), bf16[4,288,512]{2,1,0:T(8,128)(2,1)S(1)}, u32[]{:S(2)}, u32[]{:S(2)}) async-start(bf16[4,288,512]{2,1,0:T(8,128)(2,1)} %get-tuple-element.21), calls=%async_computation.1 | async-start | bytes 2359296 | tf_op jit(solution)/shard_map/share_tokens/all_to_all | solution.py:265
  37.0 13.5 %collective-permute-start.2 = (bf16[4,264,128]{2,1,0:T(8,128)(2,1)S(1)}, bf16[4,264,128]{2,1,0:T(8,128)(2,1)S(1)}, u32[]{:S(2)}, u32[]{:S(2)}) collective-permute-start(bf16[4,264,128]{2,1,0:T(8,128)(2,1)S(1)} %bitcast.13), channel_id=1, source_target_pairs={{64,0},{480,32},{128,64},{32,96},{192,128},{96,160},{256,192},{160... | collective-permute-start | bytes 811016 | tf_op jit(solution)/shard_map/gather_weight/ppermute | solution.py:262
  44.0 11.3 %collective-permute-start.1 = (bf16[4,264,128]{2,1,0:T(8,128)(2,1)S(1)}, bf16[4,264,128]{2,1,0:T(8,128)(2,1)}, u32[]{:S(2)}, u32[]{:S(2)}) collective-permute-start(bf16[4,264,128]{2,1,0:T(8,128)(2,1)S(1)} %bitcast.14), channel_id=1, source_target_pairs={{480,0},{0,32},{32,64},{64,96},{96,128},{128,160},{160,192},{192,2... | collective-permute-start | bytes 811016 | tf_op jit(solution)/shard_map/gather_weight/ppermute | solution.py:262
  46.0 9.3 %collective-permute-start = (bf16[4,264,128]{2,1,0:T(8,128)(2,1)S(1)}, bf16[4,264,128]{2,1,0:T(8,128)(2,1)}, u32[]{:S(2)}, u32[]{:S(2)}) collective-permute-start(bf16[4,264,128]{2,1,0:T(8,128)(2,1)S(1)} %bitcast.15), channel_id=1, source_target_pairs={{32,0},{64,32},{96,64},{128,96},{160,128},{192,160},{224,192},{256... | collective-permute-start | bytes 811016 | tf_op jit(solution)/shard_map/gather_weight/ppermute | solution.py:262
  57.3 7.1 %collective-permute-start.3 = (bf16[1536,512]{1,0:T(8,128)(2,1)S(1)}, bf16[1536,512]{1,0:T(8,128)(2,1)S(1)}, u32[]{:S(2)}, u32[]{:S(2)}) collective-permute-start(bf16[1536,512]{1,0:T(8,128)(2,1)S(1)} %get-tuple-element.26), channel_id=1, source_target_pairs={{1,0},{0,1},{3,2},{2,3},{5,4},{4,5},{7,6},{6,7},{9,8},{8,9},{11,10... | collective-permute-start | bytes 4718600 | tf_op jit(solution)/shard_map/other_half/ppermute | solution.py:284

commit v7 on v6

--- a/solution.py
+++ b/solution.py
@@ -91,29 +91,33 @@
 
 def half_kernel(mine, tokens, w0, w1, w3, w2, out, query, weights, sems):
     half = lax.axis_index("core") if mine else 1 - lax.axis_index("core")
+    zl = lax.axis_index("zl")
     copies = []
-    for at, ref in enumerate((w0, w1, w2, w3)):
-        zl = lax.rem(lax.axis_index("zl") + at, 4)
-        copy = pltpu.make_async_copy(ref, weights.at[lax.rem(zl, 2)], sems.at[at])
-        copies.append((lax.div(zl, 2) == half, copy))
+    for at, ref in enumerate((w1, w3)):
+        needed = lax.div(lax.rem(zl + 2 * at + 1, 4), 2) == half
+        copies.append((needed, pltpu.make_async_copy(ref, weights, sems.at[at])))
     for needed, copy in copies:
         pl.when(needed)(copy.start)
+
+    def multiply(ref, part):
+        strips, rows = [], []
+        for zh in range(4):
+            blocks = [ref[zh, 64 * at : 64 * at + 64, :] for at in range(4)]
+            strips.append(jnp.concatenate(blocks, axis=1))
+            rows.append(ref[zh, 256:264, :].astype(jnp.float32))
+        strips = jnp.concatenate(strips, axis=0)
+        total = lax.dot_general(tokens[...], strips, NT, preferred_element_type=jnp.float32)
+        k = lax.rem(zl + part, 2)
+        out[:, pl.ds(pl.multiple_of(256 * k, 256), 256)] = total.astype(jnp.bfloat16)
+        rows = jnp.concatenate(rows, axis=0).astype(jnp.bfloat16)
+        query[:, pl.ds(pl.multiple_of(128 * k, 128), 128)] = rows
+
+    own = lax.div(zl, 2) == half
+    pl.when(own)(lambda: multiply(w0, 0))
+    pl.when(jnp.logical_not(own))(lambda: multiply(w2, 0))
     for needed, copy in copies:
         pl.when(needed)(copy.wait)
-    for pair in range(2):
-        strips = []
-        for zh in (2 * pair, 2 * pair + 1):
-            for k in range(2):
-                blocks = [weights[k, zh, 64 * at : 64 * at + 64, :] for at in range(4)]
-                strips.append(jnp.concatenate(blocks, axis=1))
-        rows = jnp.concatenate(strips, axis=0)
-        total = lax.dot_general(tokens[...], rows, NT, preferred_element_type=jnp.float32)
-        out[:, 256 * pair : 256 * pair + 256] = total.astype(jnp.bfloat16)
-    columns = []
-    for k in range(2):
-        rows = [weights[k, zh, 256:264, :].astype(jnp.float32) for zh in range(4)]
-        columns.append(jnp.concatenate(rows, axis=0))
-    query[...] = jnp.concatenate(columns, axis=1).astype(jnp.bfloat16)
+    multiply(weights, 1)
 
 
 def add_kernel(first, second, mine, theirs, out):
@@ -138,7 +142,7 @@
     weighted_out = stream_out = in_proj = jnp.zeros((96, 64), jnp.float32)
     squares = dots = jnp.zeros((96, 1), jnp.float32)
     for y in range(4):
-        strips = [block[:, 128 * y + 64 * k : 128 * y + 64 * k + 64] for k in range(2) for block in blocks]
+        strips = [block[:, 256 * k + 64 * y : 256 * k + 64 * y + 64] for k in range(2) for block in blocks]
         stream = shared[y, 0:96, :].astype(jnp.float32) + jnp.concatenate(strips, axis=1)
         tail = shared[y, 256:288, :].astype(jnp.float32)
         gain = tail[24:25] + tail[25:26] + tail[26:27]
@@ -272,9 +276,9 @@
         return pl.pallas_call(
             functools.partial(half_kernel, own),
             out_shape=(sums, query),
-            in_specs=[VMEM] + [ANY] * 4,
+            in_specs=[VMEM, VMEM, ANY, ANY, VMEM],
             out_specs=(VMEM, VMEM),
-            scratch_shapes=[pltpu.VMEM((2, 4, 264, 128), bf16), pltpu.SemaphoreType.DMA((4,))],
+            scratch_shapes=[pltpu.VMEM((4, 264, 128), bf16), pltpu.SemaphoreType.DMA((2,))],
             compiler_params=PARAMS,
             cost_estimate=cost(0, 1 << 10),
         )(every, mine, after, before, across)

time: 113 us -> 112 us (level)
  transfers between devices with their start and end apart: 6 -> 6, of which waited for: 2 -> 2; matrix products, arithmetic and copies ran while one was open for 0% -> 0% of each run, Pallas kernels for 2% -> 1%
where the time goes in v7:
time: 112 us
  blocking collectives  68.8 us (61%)
  starting transfers between devices  26.8 us (24%)
  Pallas kernels  9.29 us (8%)
  waiting for transfers between devices  6.14 us (5%)
    all_to_all x1, blocking collectives, shards(): parts = lax.all_to_all(partial, PLANE, 0, 0, tiled=True)  33 us
    all_gather x1, blocking collectives, shards(): mine = lax.all_gather(piece, 'zh', axis=0)  24.4 us
    ppermute x3, starting transfers between devices, shards(): after, before, across = [lax.ppermute(mine, Z, way) for way in ways]  13.5 us
    all_to_all x1, blocking collectives, shards(): sums = lax.all_to_all(sums, TENSOR, 0, 0, tiled=True)  7.72 us
    all_to_all x1, starting transfers between devices, shards(): lax.all_to_all(copies, 'x', 0, 0, tiled=True).reshape(4 * length, features)  4.99 us
    ppermute x3, waiting for transfers between devices, shards(): after, before, across = [lax.ppermute(mine, Z, way) for way in ways]  4.73 us
    all_to_all x1, starting transfers between devices, shards(): shared = lax.all_to_all(shared, 'y', 0, 0, tiled=True)  4.19 us
    ppermute x1, starting transfers between devices, shards(): other = lax.ppermute(other, 'core', shift(2, 1))  4.11 us
  transfers between devices with their start and end apart: 6, of which 2 were waited for; matrix products, arithmetic and copies ran while one was open for 0% of the time, Pallas kernels for 1%

profile of v7, /device:TPU:1, one launch (start us, length us, event | category | flops | bytes accessed | tf_op | source)
XLA Modules:
  0.0 111.7 jit_solution(9037071557355111928)
XLA Ops:
  0.6 2.8 %prepare.1 = (bf16[4,384,512]{2,1,0:T(8,128)(2,1)}, bf16[264,128]{1,0:T(8,128)(2,1)}, bf16[4,288,512]{2,1,0:T(8,128)(2,1)}) custom-call(bf16[384,512]{1,0:T(8,128)(2,1)} %bitcast.19, bf16[384,512]{1,0:T(8,128)(2,1)} %bitcast.20, bf16[384,512]{1,0:T(8,128)(2,1)} %bitcast.21, f32[1,512]{1,0:T(1,128)} %bitcast.25, bf16[64,512]{1,0:T(8,128)(2,1)} %bitcast.22, ...), custom_call_target="tpu_custom_call" | custom-call | flops 25165824 | bytes 5242880 | tf_op jit(solution)/shard_map/prepare/pallas_call | solution.py:235
  3.5 0.0 copy-start
  3.5 5.0 %all-to-all-start = ((bf16[4,384,512]{2,1,0:T(8,128)(2,1)}), bf16[4,384,512]{2,1,0:T(8,128)(2,1)S(1)}, u32[]{:S(2)}, u32[]{:S(2)}) async-start(bf16[4,384,512]{2,1,0:T(8,128)(2,1)} %get-tuple-element.19), calls=%async_computation | async-start | bytes 3145728 | tf_op jit(solution)/shard_map/gather_tokens/all_to_all | solution.py:261
  8.5 0.0 copy-done
  8.5 24.4 %all-gather = bf16[1056,128]{1,0:T(8,128)(2,1)S(1)} all-gather(bf16[264,128]{1,0:T(8,128)(2,1)S(1)} %copy-done), channel_id=2, replica_groups=mesh['zh'=4,'zl'=4,'x'=4,'y'=4,'core'=2] {'zh'}, dimensions={0}, use_global_device_ids=true | all-gather | bytes 337920 | tf_op jit(solution)/shard_map/gather_weight/all_gather | solution.py:263
  32.9 0.0 all-to-all-done
  32.9 4.2 %all-to-all-start.1 = ((bf16[4,288,512]{2,1,0:T(8,128)(2,1)}), bf16[4,288,512]{2,1,0:T(8,128)(2,1)S(1)}, u32[]{:S(2)}, u32[]{:S(2)}) async-start(bf16[4,288,512]{2,1,0:T(8,128)(2,1)} %get-tuple-element.21), calls=%async_computation.1 | async-start | bytes 2359296 | tf_op jit(solution)/shard_map/share_tokens/all_to_all | solution.py:269
  37.0 7.0 %collective-permute-start.2 = (bf16[4,264,128]{2,1,0:T(8,128)(2,1)S(1)}, bf16[4,264,128]{2,1,0:T(8,128)(2,1)S(1)}, u32[]{:S(2)}, u32[]{:S(2)}) collective-permute-start(bf16[4,264,128]{2,1,0:T(8,128)(2,1)S(1)} %bitcast.13), channel_id=1, source_target_pairs={{64,0},{480,32},{128,64},{32,96},{192,128},{96,160},{256,192},{160... | collective-permute-start | bytes 811016 | tf_op jit(solution)/shard_map/gather_weight/ppermute | solution.py:266
  44.0 1.9 %collective-permute-start.1 = (bf16[4,264,128]{2,1,0:T(8,128)(2,1)S(1)}, bf16[4,264,128]{2,1,0:T(8,128)(2,1)}, u32[]{:S(2)}, u32[]{:S(2)}) collective-permute-start(bf16[4,264,128]{2,1,0:T(8,128)(2,1)S(1)} %bitcast.14), channel_id=1, source_target_pairs={{480,0},{0,32},{32,64},{64,96},{96,128},{128,160},{160,192},{192,2... | collective-permute-start | bytes 811016 | tf_op jit(solution)/shard_map/gather_weight/ppermute | solution.py:266
  46.0 4.6 %collective-permute-start = (bf16[4,264,128]{2,1,0:T(8,128)(2,1)S(1)}, bf16[4,264,128]{2,1,0:T(8,128)(2,1)}, u32[]{:S(2)}, u32[]{:S(2)}) collective-permute-start(bf16[4,264,128]{2,1,0:T(8,128)(2,1)S(1)} %bitcast.15), channel_id=1, source_target_pairs={{32,0},{64,32},{96,64},{128,96},{160,128},{192,160},{224,192},{256... | collective-permute-start | bytes 811016 | tf_op jit(solution)/shard_map/gather_weight/ppermute | solution.py:266
  50.5 0.0 all-to-all-done.1.shared
  50.6 0.0 collective-permute-done.2.w2
  50.6 4.7 %collective-permute-done.1.w3 = bf16[4,264,128]{2,1,0:T(8,128)(2,1)} collective-permute-done((bf16[4,264,128]{2,1,0:T(8,128)(2,1)S(1)}, bf16[4,264,128]{2,1,0:T(8,128)(2,1)}, u32[]{:S(2)}, u32[]{:S(2)}) %collective-permute-start.1) | collective-permute-done | bytes 270368 | tf_op jit(solution)/shard_map/gather_weight/ppermute | solution.py:266
  55.3 0.0 collective-permute-done.w1
  55.3 1.6 %other_half.1 = (bf16[1536,512]{1,0:T(8,128)(2,1)S(1)}, bf16[32,256]{1,0:T(8,128)(2,1)S(1)}) custom-call(bf16[1536,512]{1,0:T(8,128)(2,1)S(1)} %bitcast.11, bf16[4,264,128]{2,1,0:T(8,128)(2,1)S(1)} %bitcast.16, bf16[4,264,128]{2,1,0:T(8,128)(2,1)} %collective-permute-done.w1, bf16[4,264,128]{2,1,0:T(8,128)(2,1)} %collective-permute-done.1.w3, ...), custom_call_target="tpu_custom_call" | custom-call | bytes 1024 | tf_op jit(solution)/shard_map/other_half/pallas_call | solution.py:276
  56.9 4.1 %collective-permute-start.3 = (bf16[1536,512]{1,0:T(8,128)(2,1)S(1)}, bf16[1536,512]{1,0:T(8,128)(2,1)S(1)}, u32[]{:S(2)}, u32[]{:S(2)}) collective-permute-start(bf16[1536,512]{1,0:T(8,128)(2,1)S(1)} %get-tuple-element.26), channel_id=1, source_target_pairs={{1,0},{0,1},{3,2},{2,3},{5,4},{4,5},{7,6},{6,7},{9,8},{8,9},{11,10... | collective-permute-start | bytes 4718600 | tf_op jit(solution)/shard_map/other_half/ppermute | solution.py:288
  61.0 1.6 %own_half.2 = (bf16[1536,512]{1,0:T(8,128)(2,1)S(1)}, bf16[32,256]{1,0:T(8,128)(2,1)S(1)}) custom-call(bf16[1536,512]{1,0:T(8,128)(2,1)S(1)} %bitcast.12, bf16[4,264,128]{2,1,0:T(8,128)(2,1)S(1)} %bitcast.17, bf16[4,264,128]{2,1,0:T(8,128)(2,1)} %collective-permute-done.w1, bf16[4,264,128]{2,1,0:T(8,128)(2,1)} %collective-permute-done.1.w3, ...), custom_call_target="tpu_custom_call" | custom-call | bytes 1024 | tf_op jit(solution)/shard_map/own_half/pallas_call | solution.py:276
  62.6 1.4 %collective-permute-done.3.second = bf16[1536,512]{1,0:T(8,128)(2,1)S(1)} collective-permute-done((bf16[1536,512]{1,0:T(8,128)(2,1)S(1)}, bf16[1536,512]{1,0:T(8,128)(2,1)S(1)}, u32[]{:S(2)}, u32[]{:S(2)}) %collective-permute-start.3) | collective-permute-done | bytes 1572896 | tf_op jit(solution)/shard_map/other_half/ppermute | solution.py:288
  64.0 0.4 own_half.3
  64.4 33.0 %all_to_all.20.parts = bf16[16,128,512]{2,1,0:T(8,128)(2,1)S(1)} all-to-all(bf16[16,128,512]{2,1,0:T(8,128)(2,1)S(1)} %own_half.3), channel_id=1, replica_groups=mesh['zh'=4,'zl'=4,'x'=4,'y'=4,'core'=2] {'x','y'}, dimensions={0} | all-to-all | bytes 4194304 | tf_op jit(solution)/shard_map/exchange_parts/all_to_all | solution.py:300
  97.4 1.0 token_sums.1
  98.4 3.7 %all-gather.1 = f32[96,512]{1,0:T(8,128)S(1)} all-gather(f32[48,512]{1,0:T(8,128)S(1)} %token_sums.1), channel_id=3, replica_groups=mesh['zh'=4,'zl'=4,'x'=4,'y'=4,'core'=2] {'core'}, dimensions={0}, use_global_device_ids=true | all-gather | bytes 294912 | tf_op jit(solution)/shard_map/token_sums/all_gather | solution.py:310
  102.1 1.1 %gram.1 = f32[8,24,128]{2,1,0:T(8,128)S(1)} custom-call(f32[2,48,512]{2,1,0:T(8,128)S(1)} %bitcast.18, bf16[16,128,512]{2,1,0:T(8,128)(2,1)S(1)} %all_to_all.20.parts), custom_call_target="tpu_custom_call" | custom-call | flops 4194304 | bytes 1048576 | tf_op jit(solution)/shard_map/gram/pallas_call | solution.py:312
  103.3 7.7 %all_to_all.21.sums = f32[8,24,128]{2,1,0:T(8,128)S(1)} all-to-all(f32[8,24,128]{2,1,0:T(8,128)S(1)} %gram.1), channel_id=1, replica_groups=mesh['zh'=4,'zl'=4,'x'=4,'y'=4,'core'=2] {'y','core'}, dimensions={0} | all-to-all | bytes 196608 | tf_op jit(solution)/shard_map/gram/all_to_all | solution.py:321
  111.0 0.7 scores.1
Async XLA Ops:
  3.5 5.0 %copy-start = (bf16[264,128]{1,0:T(8,128)(2,1)S(1)}, bf16[264,128]{1,0:T(8,128)(2,1)}, u32[]{:S(2)}) copy-start(bf16[264,128]{1,0:T(8,128)(2,1)} %get-tuple-element.18) | copy-start | bytes 202756
  3.5 29.4 %all-to-all-start = ((bf16[4,384,512]{2,1,0:T(8,128)(2,1)}), bf16[4,384,512]{2,1,0:T(8,128)(2,1)S(1)}, u32[]{:S(2)}, u32[]{:S(2)}) async-start(bf16[4,384,512]{2,1,0:T(8,128)(2,1)} %get-tuple-element.19), calls=%async_computation | async-start | bytes 3145728 | tf_op jit(solution)/shard_map/gather_tokens/all_to_all | solution.py:261
  32.9 17.7 %all-to-all-start.1 = ((bf16[4,288,512]{2,1,0:T(8,128)(2,1)}), bf16[4,288,512]{2,1,0:T(8,128)(2,1)S(1)}, u32[]{:S(2)}, u32[]{:S(2)}) async-start(bf16[4,288,512]{2,1,0:T(8,128)(2,1)} %get-tuple-element.21), calls=%async_computation.1 | async-start | bytes 2359296 | tf_op jit(solution)/shard_map/share_tokens/all_to_all | solution.py:269
  37.0 13.5 %collective-permute-start.2 = (bf16[4,264,128]{2,1,0:T(8,128)(2,1)S(1)}, bf16[4,264,128]{2,1,0:T(8,128)(2,1)S(1)}, u32[]{:S(2)}, u32[]{:S(2)}) collective-permute-start(bf16[4,264,128]{2,1,0:T(8,128)(2,1)S(1)} %bitcast.13), channel_id=1, source_target_pairs={{64,0},{480,32},{128,64},{32,96},{192,128},{96,160},{256,192},{160... | collective-permute-start | bytes 811016 | tf_op jit(solution)/shard_map/gather_weight/ppermute | solution.py:266
  44.0 11.3 %collective-permute-start.1 = (bf16[4,264,128]{2,1,0:T(8,128)(2,1)S(1)}, bf16[4,264,128]{2,1,0:T(8,128)(2,1)}, u32[]{:S(2)}, u32[]{:S(2)}) collective-permute-start(bf16[4,264,128]{2,1,0:T(8,128)(2,1)S(1)} %bitcast.14), channel_id=1, source_target_pairs={{480,0},{0,32},{32,64},{64,96},{96,128},{128,160},{160,192},{192,2... | collective-permute-start | bytes 811016 | tf_op jit(solution)/shard_map/gather_weight/ppermute | solution.py:266
  46.0 9.3 %collective-permute-start = (bf16[4,264,128]{2,1,0:T(8,128)(2,1)S(1)}, bf16[4,264,128]{2,1,0:T(8,128)(2,1)}, u32[]{:S(2)}, u32[]{:S(2)}) collective-permute-start(bf16[4,264,128]{2,1,0:T(8,128)(2,1)S(1)} %bitcast.15), channel_id=1, source_target_pairs={{32,0},{64,32},{96,64},{128,96},{160,128},{192,160},{224,192},{256... | collective-permute-start | bytes 811016 | tf_op jit(solution)/shard_map/gather_weight/ppermute | solution.py:266
  56.9 7.1 %collective-permute-start.3 = (bf16[1536,512]{1,0:T(8,128)(2,1)S(1)}, bf16[1536,512]{1,0:T(8,128)(2,1)S(1)}, u32[]{:S(2)}, u32[]{:S(2)}) collective-permute-start(bf16[1536,512]{1,0:T(8,128)(2,1)S(1)} %get-tuple-element.26), channel_id=1, source_target_pairs={{1,0},{0,1},{3,2},{2,3},{5,4},{4,5},{7,6},{6,7},{9,8},{8,9},{11,10... | collective-permute-start | bytes 4718600 | tf_op jit(solution)/shard_map/other_half/ppermute | solution.py:288

commit v8 on v7

--- a/solution.py
+++ b/solution.py
@@ -162,6 +162,13 @@
     out[...] = jnp.concatenate([total[0:48], total[48:96]], axis=1)
 
 
+def pick(value, chosen):
+    n = value.shape[0]
+    terms = jnp.concatenate(split3(value), axis=0)
+    terms = jnp.dot(terms, chosen.astype(jnp.bfloat16), preferred_element_type=jnp.float32)
+    return terms[0:n] + terms[n : 2 * n] + terms[2 * n : 3 * n]
+
+
 def gram_kernel(length, width, both, parts, out, packed):
     total = both[0] + both[1]
     total = jnp.concatenate([total[:, 0:256], total[:, 256:512]], axis=0)
@@ -172,7 +179,7 @@
     column = lax.broadcasted_iota(jnp.int32, (64, 64), 1)
     source = jnp.where(column < 32, 2 * column, 2 * column - 63)
     order = (row == source).astype(jnp.float32)
-    in_proj = jnp.dot(total[:, 128:192], order, precision=HIGHEST)
+    in_proj = pick(total[:, 128:192], order)
     gram = lax.dot_general(in_proj, out_proj, TN, precision=HIGHEST, preferred_element_type=jnp.float32)
     gram = gram / math.sqrt(length)
     packed[...] = jnp.concatenate([gram[0:32], gram[32:64]], axis=1)
@@ -196,7 +203,7 @@
     row = lax.broadcasted_iota(jnp.int32, (512, 128), 0) // 8
     column = lax.broadcasted_iota(jnp.int32, (512, 128), 1)
     chosen = ((row % 4) * 16 + (row // 4) % 4 * 4 + row // 16 == column).astype(jnp.float32)
-    result = jnp.dot(flat, chosen, precision=HIGHEST, preferred_element_type=jnp.float32)
+    result = pick(flat, chosen)
     half = packed[pl.ds(pl.multiple_of(16 * core, 16), 16), :]
     for at in range(8):
         out[at, 0:16, :] = half

time: 112 us -> 112 us (level)
  no operation moved by 1% of the time
where the time goes in v8:
time: 112 us
  blocking collectives  68.8 us (61%)
  starting transfers between devices  26.8 us (24%)
  Pallas kernels  9.22 us (8%)
  waiting for transfers between devices  6.14 us (5%)
    all_to_all x1, blocking collectives, shards(): parts = lax.all_to_all(partial, PLANE, 0, 0, tiled=True)  33 us
    all_gather x1, blocking collectives, shards(): mine = lax.all_gather(piece, 'zh', axis=0)  24.4 us
    ppermute x3, starting transfers between devices, shards(): after, before, across = [lax.ppermute(mine, Z, way) for way in ways]  13.5 us
    all_to_all x1, blocking collectives, shards(): sums = lax.all_to_all(sums, TENSOR, 0, 0, tiled=True)  7.71 us
    all_to_all x1, starting transfers between devices, shards(): lax.all_to_all(copies, 'x', 0, 0, tiled=True).reshape(4 * length, features)  4.99 us
    ppermute x3, waiting for transfers between devices, shards(): after, before, across = [lax.ppermute(mine, Z, way) for way in ways]  4.73 us
    all_to_all x1, starting transfers between devices, shards(): shared = lax.all_to_all(shared, 'y', 0, 0, tiled=True)  4.19 us
    ppermute x1, starting transfers between devices, shards(): other = lax.ppermute(other, 'core', shift(2, 1))  4.11 us
  transfers between devices with their start and end apart: 6, of which 2 were waited for; matrix products, arithmetic and copies ran while one was open for 0% of the time, Pallas kernels for 1%

profile of v8, /device:TPU:1, one launch (start us, length us, event | category | flops | bytes accessed | tf_op | source)
XLA Modules:
  0.0 111.6 jit_solution(3969877494343719613)
XLA Ops:
  0.6 2.8 %prepare.1 = (bf16[4,384,512]{2,1,0:T(8,128)(2,1)}, bf16[264,128]{1,0:T(8,128)(2,1)}, bf16[4,288,512]{2,1,0:T(8,128)(2,1)}) custom-call(bf16[384,512]{1,0:T(8,128)(2,1)} %bitcast.19, bf16[384,512]{1,0:T(8,128)(2,1)} %bitcast.20, bf16[384,512]{1,0:T(8,128)(2,1)} %bitcast.21, f32[1,512]{1,0:T(1,128)} %bitcast.25, bf16[64,512]{1,0:T(8,128)(2,1)} %bitcast.22, ...), custom_call_target="tpu_custom_call" | custom-call | flops 25165824 | bytes 5242880 | tf_op jit(solution)/shard_map/prepare/pallas_call | solution.py:242
  3.5 0.0 copy-start
  3.5 5.0 %all-to-all-start = ((bf16[4,384,512]{2,1,0:T(8,128)(2,1)}), bf16[4,384,512]{2,1,0:T(8,128)(2,1)S(1)}, u32[]{:S(2)}, u32[]{:S(2)}) async-start(bf16[4,384,512]{2,1,0:T(8,128)(2,1)} %get-tuple-element.19), calls=%async_computation | async-start | bytes 3145728 | tf_op jit(solution)/shard_map/gather_tokens/all_to_all | solution.py:268
  8.5 0.0 copy-done
  8.5 24.4 %all-gather = bf16[1056,128]{1,0:T(8,128)(2,1)S(1)} all-gather(bf16[264,128]{1,0:T(8,128)(2,1)S(1)} %copy-done), channel_id=2, replica_groups=mesh['zh'=4,'zl'=4,'x'=4,'y'=4,'core'=2] {'zh'}, dimensions={0}, use_global_device_ids=true | all-gather | bytes 337920 | tf_op jit(solution)/shard_map/gather_weight/all_gather | solution.py:270
  32.9 0.0 all-to-all-done
  32.9 4.2 %all-to-all-start.1 = ((bf16[4,288,512]{2,1,0:T(8,128)(2,1)}), bf16[4,288,512]{2,1,0:T(8,128)(2,1)S(1)}, u32[]{:S(2)}, u32[]{:S(2)}) async-start(bf16[4,288,512]{2,1,0:T(8,128)(2,1)} %get-tuple-element.21), calls=%async_computation.1 | async-start | bytes 2359296 | tf_op jit(solution)/shard_map/share_tokens/all_to_all | solution.py:276
  37.0 7.0 %collective-permute-start.2 = (bf16[4,264,128]{2,1,0:T(8,128)(2,1)S(1)}, bf16[4,264,128]{2,1,0:T(8,128)(2,1)S(1)}, u32[]{:S(2)}, u32[]{:S(2)}) collective-permute-start(bf16[4,264,128]{2,1,0:T(8,128)(2,1)S(1)} %bitcast.13), channel_id=1, source_target_pairs={{64,0},{480,32},{128,64},{32,96},{192,128},{96,160},{256,192},{160... | collective-permute-start | bytes 811016 | tf_op jit(solution)/shard_map/gather_weight/ppermute | solution.py:273
  44.0 1.9 %collective-permute-start.1 = (bf16[4,264,128]{2,1,0:T(8,128)(2,1)S(1)}, bf16[4,264,128]{2,1,0:T(8,128)(2,1)}, u32[]{:S(2)}, u32[]{:S(2)}) collective-permute-start(bf16[4,264,128]{2,1,0:T(8,128)(2,1)S(1)} %bitcast.14), channel_id=1, source_target_pairs={{480,0},{0,32},{32,64},{64,96},{96,128},{128,160},{160,192},{192,2... | collective-permute-start | bytes 811016 | tf_op jit(solution)/shard_map/gather_weight/ppermute | solution.py:273
  46.0 4.6 %collective-permute-start = (bf16[4,264,128]{2,1,0:T(8,128)(2,1)S(1)}, bf16[4,264,128]{2,1,0:T(8,128)(2,1)}, u32[]{:S(2)}, u32[]{:S(2)}) collective-permute-start(bf16[4,264,128]{2,1,0:T(8,128)(2,1)S(1)} %bitcast.15), channel_id=1, source_target_pairs={{32,0},{64,32},{96,64},{128,96},{160,128},{192,160},{224,192},{256... | collective-permute-start | bytes 811016 | tf_op jit(solution)/shard_map/gather_weight/ppermute | solution.py:273
  50.5 0.0 all-to-all-done.1.shared
  50.6 0.0 collective-permute-done.2.w2
  50.6 4.7 %collective-permute-done.1.w3 = bf16[4,264,128]{2,1,0:T(8,128)(2,1)} collective-permute-done((bf16[4,264,128]{2,1,0:T(8,128)(2,1)S(1)}, bf16[4,264,128]{2,1,0:T(8,128)(2,1)}, u32[]{:S(2)}, u32[]{:S(2)}) %collective-permute-start.1) | collective-permute-done | bytes 270368 | tf_op jit(solution)/shard_map/gather_weight/ppermute | solution.py:273
  55.3 0.0 collective-permute-done.w1
  55.3 1.6 %other_half.1 = (bf16[1536,512]{1,0:T(8,128)(2,1)S(1)}, bf16[32,256]{1,0:T(8,128)(2,1)S(1)}) custom-call(bf16[1536,512]{1,0:T(8,128)(2,1)S(1)} %bitcast.11, bf16[4,264,128]{2,1,0:T(8,128)(2,1)S(1)} %bitcast.16, bf16[4,264,128]{2,1,0:T(8,128)(2,1)} %collective-permute-done.w1, bf16[4,264,128]{2,1,0:T(8,128)(2,1)} %collective-permute-done.1.w3, ...), custom_call_target="tpu_custom_call" | custom-call | bytes 1024 | tf_op jit(solution)/shard_map/other_half/pallas_call | solution.py:283
  56.9 4.1 %collective-permute-start.3 = (bf16[1536,512]{1,0:T(8,128)(2,1)S(1)}, bf16[1536,512]{1,0:T(8,128)(2,1)S(1)}, u32[]{:S(2)}, u32[]{:S(2)}) collective-permute-start(bf16[1536,512]{1,0:T(8,128)(2,1)S(1)} %get-tuple-element.26), channel_id=1, source_target_pairs={{1,0},{0,1},{3,2},{2,3},{5,4},{4,5},{7,6},{6,7},{9,8},{8,9},{11,10... | collective-permute-start | bytes 4718600 | tf_op jit(solution)/shard_map/other_half/ppermute | solution.py:295
  61.0 1.6 %own_half.2 = (bf16[1536,512]{1,0:T(8,128)(2,1)S(1)}, bf16[32,256]{1,0:T(8,128)(2,1)S(1)}) custom-call(bf16[1536,512]{1,0:T(8,128)(2,1)S(1)} %bitcast.12, bf16[4,264,128]{2,1,0:T(8,128)(2,1)S(1)} %bitcast.17, bf16[4,264,128]{2,1,0:T(8,128)(2,1)} %collective-permute-done.w1, bf16[4,264,128]{2,1,0:T(8,128)(2,1)} %collective-permute-done.1.w3, ...), custom_call_target="tpu_custom_call" | custom-call | bytes 1024 | tf_op jit(solution)/shard_map/own_half/pallas_call | solution.py:283
  62.6 1.4 %collective-permute-done.3.second = bf16[1536,512]{1,0:T(8,128)(2,1)S(1)} collective-permute-done((bf16[1536,512]{1,0:T(8,128)(2,1)S(1)}, bf16[1536,512]{1,0:T(8,128)(2,1)S(1)}, u32[]{:S(2)}, u32[]{:S(2)}) %collective-permute-start.3) | collective-permute-done | bytes 1572896 | tf_op jit(solution)/shard_map/other_half/ppermute | solution.py:295
  64.0 0.4 own_half.3
  64.4 33.0 %all_to_all.20.parts = bf16[16,128,512]{2,1,0:T(8,128)(2,1)S(1)} all-to-all(bf16[16,128,512]{2,1,0:T(8,128)(2,1)S(1)} %own_half.3), channel_id=1, replica_groups=mesh['zh'=4,'zl'=4,'x'=4,'y'=4,'core'=2] {'x','y'}, dimensions={0} | all-to-all | bytes 4194304 | tf_op jit(solution)/shard_map/exchange_parts/all_to_all | solution.py:307
  97.4 1.0 token_sums.1
  98.4 3.7 %all-gather.1 = f32[96,512]{1,0:T(8,128)S(1)} all-gather(f32[48,512]{1,0:T(8,128)S(1)} %token_sums.1), channel_id=3, replica_groups=mesh['zh'=4,'zl'=4,'x'=4,'y'=4,'core'=2] {'core'}, dimensions={0}, use_global_device_ids=true | all-gather | bytes 294912 | tf_op jit(solution)/shard_map/token_sums/all_gather | solution.py:317
  102.1 1.1 gram.1
  103.2 7.7 %all_to_all.21.sums = f32[8,24,128]{2,1,0:T(8,128)S(1)} all-to-all(f32[8,24,128]{2,1,0:T(8,128)S(1)} %gram.1), channel_id=1, replica_groups=mesh['zh'=4,'zl'=4,'x'=4,'y'=4,'core'=2] {'y','core'}, dimensions={0} | all-to-all | bytes 196608 | tf_op jit(solution)/shard_map/gram/all_to_all | solution.py:328
  110.9 0.7 scores.1
Async XLA Ops:
  3.5 5.0 %copy-start = (bf16[264,128]{1,0:T(8,128)(2,1)S(1)}, bf16[264,128]{1,0:T(8,128)(2,1)}, u32[]{:S(2)}) copy-start(bf16[264,128]{1,0:T(8,128)(2,1)} %get-tuple-element.18) | copy-start | bytes 202756
  3.5 29.4 %all-to-all-start = ((bf16[4,384,512]{2,1,0:T(8,128)(2,1)}), bf16[4,384,512]{2,1,0:T(8,128)(2,1)S(1)}, u32[]{:S(2)}, u32[]{:S(2)}) async-start(bf16[4,384,512]{2,1,0:T(8,128)(2,1)} %get-tuple-element.19), calls=%async_computation | async-start | bytes 3145728 | tf_op jit(solution)/shard_map/gather_tokens/all_to_all | solution.py:268
  32.9 17.7 %all-to-all-start.1 = ((bf16[4,288,512]{2,1,0:T(8,128)(2,1)}), bf16[4,288,512]{2,1,0:T(8,128)(2,1)S(1)}, u32[]{:S(2)}, u32[]{:S(2)}) async-start(bf16[4,288,512]{2,1,0:T(8,128)(2,1)} %get-tuple-element.21), calls=%async_computation.1 | async-start | bytes 2359296 | tf_op jit(solution)/shard_map/share_tokens/all_to_all | solution.py:276
  37.0 13.5 %collective-permute-start.2 = (bf16[4,264,128]{2,1,0:T(8,128)(2,1)S(1)}, bf16[4,264,128]{2,1,0:T(8,128)(2,1)S(1)}, u32[]{:S(2)}, u32[]{:S(2)}) collective-permute-start(bf16[4,264,128]{2,1,0:T(8,128)(2,1)S(1)} %bitcast.13), channel_id=1, source_target_pairs={{64,0},{480,32},{128,64},{32,96},{192,128},{96,160},{256,192},{160... | collective-permute-start | bytes 811016 | tf_op jit(solution)/shard_map/gather_weight/ppermute | solution.py:273
  44.0 11.3 %collective-permute-start.1 = (bf16[4,264,128]{2,1,0:T(8,128)(2,1)S(1)}, bf16[4,264,128]{2,1,0:T(8,128)(2,1)}, u32[]{:S(2)}, u32[]{:S(2)}) collective-permute-start(bf16[4,264,128]{2,1,0:T(8,128)(2,1)S(1)} %bitcast.14), channel_id=1, source_target_pairs={{480,0},{0,32},{32,64},{64,96},{96,128},{128,160},{160,192},{192,2... | collective-permute-start | bytes 811016 | tf_op jit(solution)/shard_map/gather_weight/ppermute | solution.py:273
  46.0 9.3 %collective-permute-start = (bf16[4,264,128]{2,1,0:T(8,128)(2,1)S(1)}, bf16[4,264,128]{2,1,0:T(8,128)(2,1)}, u32[]{:S(2)}, u32[]{:S(2)}) collective-permute-start(bf16[4,264,128]{2,1,0:T(8,128)(2,1)S(1)} %bitcast.15), channel_id=1, source_target_pairs={{32,0},{64,32},{96,64},{128,96},{160,128},{192,160},{224,192},{256... | collective-permute-start | bytes 811016 | tf_op jit(solution)/shard_map/gather_weight/ppermute | solution.py:273
  56.9 7.1 %collective-permute-start.3 = (bf16[1536,512]{1,0:T(8,128)(2,1)S(1)}, bf16[1536,512]{1,0:T(8,128)(2,1)S(1)}, u32[]{:S(2)}, u32[]{:S(2)}) collective-permute-start(bf16[1536,512]{1,0:T(8,128)(2,1)S(1)} %get-tuple-element.26), channel_id=1, source_target_pairs={{1,0},{0,1},{3,2},{2,3},{5,4},{4,5},{7,6},{6,7},{9,8},{8,9},{11,10... | collective-permute-start | bytes 4718600 | tf_op jit(solution)/shard_map/other_half/ppermute | solution.py:295

commit v9 on v8

--- a/solution.py
+++ b/solution.py
@@ -198,8 +198,10 @@
             every = term if every is None else every + term
         sources = sources + [every[:, 128 * at : 128 * at + 128] for at in range(4)]
     every = jnp.concatenate(sources, axis=0)
-    ones = jnp.ones((8, 128), jnp.float32)
-    flat = lax.dot_general(ones, every, NT, precision=HIGHEST, preferred_element_type=jnp.float32)
+    ones = jnp.ones((8, 128), jnp.bfloat16)
+    every = jnp.concatenate(split3(every), axis=0)
+    flat = lax.dot_general(ones, every, NT, preferred_element_type=jnp.float32)
+    flat = flat[:, 0:512] + flat[:, 512:1024] + flat[:, 1024:1536]
     row = lax.broadcasted_iota(jnp.int32, (512, 128), 0) // 8
     column = lax.broadcasted_iota(jnp.int32, (512, 128), 1)
     chosen = ((row % 4) * 16 + (row // 4) % 4 * 4 + row // 16 == column).astype(jnp.float32)

time: 112 us -> 112 us (level)
  no operation moved by 1% of the time
where the time goes in v9:
time: 112 us
  blocking collectives  68.8 us (61%)
  starting transfers between devices  26.8 us (24%)
  Pallas kernels  9.15 us (8%)
  waiting for transfers between devices  6.14 us (5%)
    all_to_all x1, blocking collectives, shards(): parts = lax.all_to_all(partial, PLANE, 0, 0, tiled=True)  33 us
    all_gather x1, blocking collectives, shards(): mine = lax.all_gather(piece, 'zh', axis=0)  24.4 us
    ppermute x3, starting transfers between devices, shards(): after, before, across = [lax.ppermute(mine, Z, way) for way in ways]  13.5 us
    all_to_all x1, blocking collectives, shards(): sums = lax.all_to_all(sums, TENSOR, 0, 0, tiled=True)  7.71 us
    all_to_all x1, starting transfers between devices, shards(): lax.all_to_all(copies, 'x', 0, 0, tiled=True).reshape(4 * length, features)  4.99 us
    ppermute x3, waiting for transfers between devices, shards(): after, before, across = [lax.ppermute(mine, Z, way) for way in ways]  4.73 us
    all_to_all x1, starting transfers between devices, shards(): shared = lax.all_to_all(shared, 'y', 0, 0, tiled=True)  4.19 us
    ppermute x1, starting transfers between devices, shards(): other = lax.ppermute(other, 'core', shift(2, 1))  4.11 us
  transfers between devices with their start and end apart: 6, of which 2 were waited for; matrix products, arithmetic and copies ran while one was open for 0% of the time, Pallas kernels for 1%

profile of v9, /device:TPU:1, one launch (start us, length us, event | category | flops | bytes accessed | tf_op | source)
XLA Modules:
  0.0 111.5 jit_solution(13151113443821580438)
XLA Ops:
  0.6 2.8 %prepare.1 = (bf16[4,384,512]{2,1,0:T(8,128)(2,1)}, bf16[264,128]{1,0:T(8,128)(2,1)}, bf16[4,288,512]{2,1,0:T(8,128)(2,1)}) custom-call(bf16[384,512]{1,0:T(8,128)(2,1)} %bitcast.19, bf16[384,512]{1,0:T(8,128)(2,1)} %bitcast.20, bf16[384,512]{1,0:T(8,128)(2,1)} %bitcast.21, f32[1,512]{1,0:T(1,128)} %bitcast.25, bf16[64,512]{1,0:T(8,128)(2,1)} %bitcast.22, ...), custom_call_target="tpu_custom_call" | custom-call | flops 25165824 | bytes 5242880 | tf_op jit(solution)/shard_map/prepare/pallas_call | solution.py:244
  3.5 0.0 copy-start
  3.5 5.0 %all-to-all-start = ((bf16[4,384,512]{2,1,0:T(8,128)(2,1)}), bf16[4,384,512]{2,1,0:T(8,128)(2,1)S(1)}, u32[]{:S(2)}, u32[]{:S(2)}) async-start(bf16[4,384,512]{2,1,0:T(8,128)(2,1)} %get-tuple-element.19), calls=%async_computation | async-start | bytes 3145728 | tf_op jit(solution)/shard_map/gather_tokens/all_to_all | solution.py:270
  8.5 0.0 copy-done
  8.5 24.4 %all-gather = bf16[1056,128]{1,0:T(8,128)(2,1)S(1)} all-gather(bf16[264,128]{1,0:T(8,128)(2,1)S(1)} %copy-done), channel_id=2, replica_groups=mesh['zh'=4,'zl'=4,'x'=4,'y'=4,'core'=2] {'zh'}, dimensions={0}, use_global_device_ids=true | all-gather | bytes 337920 | tf_op jit(solution)/shard_map/gather_weight/all_gather | solution.py:272
  32.9 0.0 all-to-all-done
  32.9 4.2 %all-to-all-start.1 = ((bf16[4,288,512]{2,1,0:T(8,128)(2,1)}), bf16[4,288,512]{2,1,0:T(8,128)(2,1)S(1)}, u32[]{:S(2)}, u32[]{:S(2)}) async-start(bf16[4,288,512]{2,1,0:T(8,128)(2,1)} %get-tuple-element.21), calls=%async_computation.1 | async-start | bytes 2359296 | tf_op jit(solution)/shard_map/share_tokens/all_to_all | solution.py:278
  37.0 7.0 %collective-permute-start.2 = (bf16[4,264,128]{2,1,0:T(8,128)(2,1)S(1)}, bf16[4,264,128]{2,1,0:T(8,128)(2,1)S(1)}, u32[]{:S(2)}, u32[]{:S(2)}) collective-permute-start(bf16[4,264,128]{2,1,0:T(8,128)(2,1)S(1)} %bitcast.13), channel_id=1, source_target_pairs={{64,0},{480,32},{128,64},{32,96},{192,128},{96,160},{256,192},{160... | collective-permute-start | bytes 811016 | tf_op jit(solution)/shard_map/gather_weight/ppermute | solution.py:275
  44.0 1.9 %collective-permute-start.1 = (bf16[4,264,128]{2,1,0:T(8,128)(2,1)S(1)}, bf16[4,264,128]{2,1,0:T(8,128)(2,1)}, u32[]{:S(2)}, u32[]{:S(2)}) collective-permute-start(bf16[4,264,128]{2,1,0:T(8,128)(2,1)S(1)} %bitcast.14), channel_id=1, source_target_pairs={{480,0},{0,32},{32,64},{64,96},{96,128},{128,160},{160,192},{192,2... | collective-permute-start | bytes 811016 | tf_op jit(solution)/shard_map/gather_weight/ppermute | solution.py:275
  46.0 4.6 %collective-permute-start = (bf16[4,264,128]{2,1,0:T(8,128)(2,1)S(1)}, bf16[4,264,128]{2,1,0:T(8,128)(2,1)}, u32[]{:S(2)}, u32[]{:S(2)}) collective-permute-start(bf16[4,264,128]{2,1,0:T(8,128)(2,1)S(1)} %bitcast.15), channel_id=1, source_target_pairs={{32,0},{64,32},{96,64},{128,96},{160,128},{192,160},{224,192},{256... | collective-permute-start | bytes 811016 | tf_op jit(solution)/shard_map/gather_weight/ppermute | solution.py:275
  50.5 0.0 all-to-all-done.1.shared
  50.6 0.0 collective-permute-done.2.w2
  50.6 4.7 %collective-permute-done.1.w3 = bf16[4,264,128]{2,1,0:T(8,128)(2,1)} collective-permute-done((bf16[4,264,128]{2,1,0:T(8,128)(2,1)S(1)}, bf16[4,264,128]{2,1,0:T(8,128)(2,1)}, u32[]{:S(2)}, u32[]{:S(2)}) %collective-permute-start.1) | collective-permute-done | bytes 270368 | tf_op jit(solution)/shard_map/gather_weight/ppermute | solution.py:275
  55.3 0.0 collective-permute-done.w1
  55.3 1.6 %other_half.1 = (bf16[1536,512]{1,0:T(8,128)(2,1)S(1)}, bf16[32,256]{1,0:T(8,128)(2,1)S(1)}) custom-call(bf16[1536,512]{1,0:T(8,128)(2,1)S(1)} %bitcast.11, bf16[4,264,128]{2,1,0:T(8,128)(2,1)S(1)} %bitcast.16, bf16[4,264,128]{2,1,0:T(8,128)(2,1)} %collective-permute-done.w1, bf16[4,264,128]{2,1,0:T(8,128)(2,1)} %collective-permute-done.1.w3, ...), custom_call_target="tpu_custom_call" | custom-call | bytes 1024 | tf_op jit(solution)/shard_map/other_half/pallas_call | solution.py:285
  56.9 4.1 %collective-permute-start.3 = (bf16[1536,512]{1,0:T(8,128)(2,1)S(1)}, bf16[1536,512]{1,0:T(8,128)(2,1)S(1)}, u32[]{:S(2)}, u32[]{:S(2)}) collective-permute-start(bf16[1536,512]{1,0:T(8,128)(2,1)S(1)} %get-tuple-element.26), channel_id=1, source_target_pairs={{1,0},{0,1},{3,2},{2,3},{5,4},{4,5},{7,6},{6,7},{9,8},{8,9},{11,10... | collective-permute-start | bytes 4718600 | tf_op jit(solution)/shard_map/other_half/ppermute | solution.py:297
  61.0 1.6 %own_half.2 = (bf16[1536,512]{1,0:T(8,128)(2,1)S(1)}, bf16[32,256]{1,0:T(8,128)(2,1)S(1)}) custom-call(bf16[1536,512]{1,0:T(8,128)(2,1)S(1)} %bitcast.12, bf16[4,264,128]{2,1,0:T(8,128)(2,1)S(1)} %bitcast.17, bf16[4,264,128]{2,1,0:T(8,128)(2,1)} %collective-permute-done.w1, bf16[4,264,128]{2,1,0:T(8,128)(2,1)} %collective-permute-done.1.w3, ...), custom_call_target="tpu_custom_call" | custom-call | bytes 1024 | tf_op jit(solution)/shard_map/own_half/pallas_call | solution.py:285
  62.6 1.4 %collective-permute-done.3.second = bf16[1536,512]{1,0:T(8,128)(2,1)S(1)} collective-permute-done((bf16[1536,512]{1,0:T(8,128)(2,1)S(1)}, bf16[1536,512]{1,0:T(8,128)(2,1)S(1)}, u32[]{:S(2)}, u32[]{:S(2)}) %collective-permute-start.3) | collective-permute-done | bytes 1572896 | tf_op jit(solution)/shard_map/other_half/ppermute | solution.py:297
  64.0 0.4 own_half.3
  64.4 33.0 %all_to_all.20.parts = bf16[16,128,512]{2,1,0:T(8,128)(2,1)S(1)} all-to-all(bf16[16,128,512]{2,1,0:T(8,128)(2,1)S(1)} %own_half.3), channel_id=1, replica_groups=mesh['zh'=4,'zl'=4,'x'=4,'y'=4,'core'=2] {'x','y'}, dimensions={0} | all-to-all | bytes 4194304 | tf_op jit(solution)/shard_map/exchange_parts/all_to_all | solution.py:309
  97.4 1.0 token_sums.1
  98.4 3.7 %all-gather.1 = f32[96,512]{1,0:T(8,128)S(1)} all-gather(f32[48,512]{1,0:T(8,128)S(1)} %token_sums.1), channel_id=3, replica_groups=mesh['zh'=4,'zl'=4,'x'=4,'y'=4,'core'=2] {'core'}, dimensions={0}, use_global_device_ids=true | all-gather | bytes 294912 | tf_op jit(solution)/shard_map/token_sums/all_gather | solution.py:319
  102.1 1.0 gram.1
  103.1 7.7 %all_to_all.21.sums = f32[8,24,128]{2,1,0:T(8,128)S(1)} all-to-all(f32[8,24,128]{2,1,0:T(8,128)S(1)} %gram.1), channel_id=1, replica_groups=mesh['zh'=4,'zl'=4,'x'=4,'y'=4,'core'=2] {'y','core'}, dimensions={0} | all-to-all | bytes 196608 | tf_op jit(solution)/shard_map/gram/all_to_all | solution.py:330
  110.8 0.7 scores.1
Async XLA Ops:
  3.5 5.0 %copy-start = (bf16[264,128]{1,0:T(8,128)(2,1)S(1)}, bf16[264,128]{1,0:T(8,128)(2,1)}, u32[]{:S(2)}) copy-start(bf16[264,128]{1,0:T(8,128)(2,1)} %get-tuple-element.18) | copy-start | bytes 202756
  3.5 29.4 %all-to-all-start = ((bf16[4,384,512]{2,1,0:T(8,128)(2,1)}), bf16[4,384,512]{2,1,0:T(8,128)(2,1)S(1)}, u32[]{:S(2)}, u32[]{:S(2)}) async-start(bf16[4,384,512]{2,1,0:T(8,128)(2,1)} %get-tuple-element.19), calls=%async_computation | async-start | bytes 3145728 | tf_op jit(solution)/shard_map/gather_tokens/all_to_all | solution.py:270
  32.9 17.7 %all-to-all-start.1 = ((bf16[4,288,512]{2,1,0:T(8,128)(2,1)}), bf16[4,288,512]{2,1,0:T(8,128)(2,1)S(1)}, u32[]{:S(2)}, u32[]{:S(2)}) async-start(bf16[4,288,512]{2,1,0:T(8,128)(2,1)} %get-tuple-element.21), calls=%async_computation.1 | async-start | bytes 2359296 | tf_op jit(solution)/shard_map/share_tokens/all_to_all | solution.py:278
  37.0 13.5 %collective-permute-start.2 = (bf16[4,264,128]{2,1,0:T(8,128)(2,1)S(1)}, bf16[4,264,128]{2,1,0:T(8,128)(2,1)S(1)}, u32[]{:S(2)}, u32[]{:S(2)}) collective-permute-start(bf16[4,264,128]{2,1,0:T(8,128)(2,1)S(1)} %bitcast.13), channel_id=1, source_target_pairs={{64,0},{480,32},{128,64},{32,96},{192,128},{96,160},{256,192},{160... | collective-permute-start | bytes 811016 | tf_op jit(solution)/shard_map/gather_weight/ppermute | solution.py:275
  44.0 11.3 %collective-permute-start.1 = (bf16[4,264,128]{2,1,0:T(8,128)(2,1)S(1)}, bf16[4,264,128]{2,1,0:T(8,128)(2,1)}, u32[]{:S(2)}, u32[]{:S(2)}) collective-permute-start(bf16[4,264,128]{2,1,0:T(8,128)(2,1)S(1)} %bitcast.14), channel_id=1, source_target_pairs={{480,0},{0,32},{32,64},{64,96},{96,128},{128,160},{160,192},{192,2... | collective-permute-start | bytes 811016 | tf_op jit(solution)/shard_map/gather_weight/ppermute | solution.py:275
  46.0 9.3 %collective-permute-start = (bf16[4,264,128]{2,1,0:T(8,128)(2,1)S(1)}, bf16[4,264,128]{2,1,0:T(8,128)(2,1)}, u32[]{:S(2)}, u32[]{:S(2)}) collective-permute-start(bf16[4,264,128]{2,1,0:T(8,128)(2,1)S(1)} %bitcast.15), channel_id=1, source_target_pairs={{32,0},{64,32},{96,64},{128,96},{160,128},{192,160},{224,192},{256... | collective-permute-start | bytes 811016 | tf_op jit(solution)/shard_map/gather_weight/ppermute | solution.py:275
  56.9 7.1 %collective-permute-start.3 = (bf16[1536,512]{1,0:T(8,128)(2,1)S(1)}, bf16[1536,512]{1,0:T(8,128)(2,1)S(1)}, u32[]{:S(2)}, u32[]{:S(2)}) collective-permute-start(bf16[1536,512]{1,0:T(8,128)(2,1)S(1)} %get-tuple-element.26), channel_id=1, source_target_pairs={{1,0},{0,1},{3,2},{2,3},{5,4},{4,5},{7,6},{6,7},{9,8},{8,9},{11,10... | collective-permute-start | bytes 4718600 | tf_op jit(solution)/shard_map/other_half/ppermute | solution.py:297
